TPU v7x, 256 devices: a whole 4x4x8 slice. The times are simulated.
256 devices in a mesh: section: 2 (over y_hi), ctx: 128 (over x, y_lo, z, core).
Axes of the slice: x: 4, y: 4 (y_hi: 2, y_lo: 2; y = y_hi * 2 + y_lo), z: 8, core: 2. Of those that a mesh axis runs over, the one named last changes fastest.
Arguments:
- queries: bfloat16 [32768, 2048], P(('section', 'ctx')), parts along dimension 0, may hold values from -300 to 300
- key_rows_slotted: bfloat16 [32768, 512], P(('section', 'ctx')), parts along dimension 0, may hold values from -12 to 12
- value_rows_slotted: bfloat16 [32768, 512], P(('section', 'ctx')), parts along dimension 0, may hold values from -5 to 5
- output_gradient: bfloat16 [32768, 2048], P(('section', 'ctx')), parts along dimension 0, may hold values from -5 to 5
- slot_to_block: int32 [512], P('section'), parts along dimension 0, may hold values from 0 to 255, as said below
- doc_starts: int32 [684], P('section'), parts along dimension 0, may hold values from 0 to 16384, as said below
- block_live: int32 [512, 4], P('section'), parts along dimension 0, may hold values from 0 to 1, as said below
Outputs:
- query_grad: bfloat16 [32768, 2048], P(('section', 'ctx')), parts along dimension 0
- key_gradient: bfloat16 [32768, 512], P(('section', 'ctx')), parts along dimension 0
- value_gradient: bfloat16 [32768, 512], P(('section', 'ctx')), parts along dimension 0
There are 2 independent parts, one for each index of `section`. A program takes and returns all parts, laid end to end along the dimension named above; each array names one. Nothing has to cross between parts.
Inputs may be any that keep to these rules, and one draw needn't show every extreme that they name: `slot_to_block`: index i of ctx holds slots 2i and 2i + 1; slot 2i holds block m and slot 2i + 1 holds block 255 - m, where m = (i - r) mod (128) for one r of each draw. `doc_starts`: Ascending, the first entry 0; every document holds at most 192 tokens; entries equal to 16384 start no document. `block_live`: entry [b, d] is 1 where block b and block b - d of the sequence hold tokens of one document, always 1 at d = 0, else 0.
All inputs are finite; a program needn't handle non-finite values.
Results may differ from a plain program's by a relative error of at most 0.005.
Values may be sent and summed in bfloat16 or wider, within the bound.
No kernel may reach another device: no remote copies, remote signals or barrier semaphores. Data moves between devices by JAX's collectives and lax.ppermute only.
A program may use at most 128 MiB of HBM per device.

v0:
```python
import functools
import math

import jax
import jax.numpy as jnp
from jax import lax
from jax.experimental import pallas as pl
from jax.experimental.pallas import tpu as pltpu
from jax.sharding import PartitionSpec as P

QUERY_HEADS = 16
KEY_VALUE_HEADS = 4
GROUP = QUERY_HEADS // KEY_VALUE_HEADS
HEAD_WIDTH = 128
ROWS = 64
KV = KEY_VALUE_HEADS * HEAD_WIDTH
WIDE = QUERY_HEADS * HEAD_WIDTH
REACH = 3
SPAN = (REACH + 1) * ROWS
SCALE = 1.0 / math.sqrt(HEAD_WIDTH)
EXP2_SCALE = SCALE * math.log2(math.e)
MASKED = -1e30
FAR = 1 << 30
ENTRIES = 9
VMEM_LIMIT = 48 * 1024 * 1024

TABLE_A, TABLE_B, TABLE_C = 4, 6, 8


def send(array, even_by, odd_by):
    count = lax.axis_size("ctx")
    pairs = [(i, (i + (odd_by if i % 2 else even_by)) % count) for i in range(count)]
    return lax.ppermute(array, "ctx", pairs)


def fold_flags(chip_base, slots, live):
    half = slots.shape[0] // 2
    middle_even = slots[chip_base] == half - 1
    middle_odd = slots[chip_base + 2] == half - 1
    far_middle = jnp.logical_and(middle_odd, live[half * (REACH + 1) + REACH] == 1)
    return middle_even, far_middle


def attention_kernel(
    place,
    slots,
    live,
    row_start,
    q_own,
    q_sib,
    g_own,
    g_sib,
    kv_own,
    kv_sib,
    kv_a,
    kv_b,
    kv_c,
    dq_first,
    dq_rest,
    out_own,
    out_sib,
    out_a,
    out_b,
    out_c,
    table,
    total,
    q_work,
    g_work,
    dq,
    bias,
):
    me = place[0]
    count = slots.shape[0] // 2
    parity = lax.rem(me, 2)
    is_odd = parity == 1
    chip_base = 2 * (me - parity)
    middle_even, far_middle = fold_flags(chip_base, slots, live)

    own_at = pl.multiple_of(parity * 128, 128)
    sib_at = pl.multiple_of((1 - parity) * 128, 128)
    table[pl.ds(own_at, 128), :] = kv_own[...]
    table[pl.ds(sib_at, 128), :] = kv_sib[...]
    table[TABLE_A * ROWS : TABLE_B * ROWS, :] = kv_a[...]
    table[TABLE_B * ROWS : TABLE_C * ROWS, :] = kv_b[...]
    table[TABLE_C * ROWS :, :] = kv_c[...]
    total[...] = jnp.zeros_like(total)

    toward = jnp.where(is_odd, 1, -1)
    near_a = lax.rem(me + 2 * toward + count, count)
    near_b = lax.rem(me + toward + count, count)
    far = lax.rem(me + 3 * toward + count, count)
    entry_ids = [slots[chip_base + e] for e in range(4)]
    entry_ids += [slots[2 * near_a], slots[2 * near_a + 1]]
    entry_ids += [slots[2 * near_b], slots[2 * near_b + 1]]
    entry_ids += [slots[2 * far + parity]]

    own_row = pl.multiple_of(parity * ROWS, ROWS)
    other_row = pl.multiple_of((1 - parity) * ROWS, ROWS)
    q_work[0] = q_own[pl.ds(own_row, ROWS), :]
    g_work[0] = g_own[pl.ds(own_row, ROWS), :]

    @pl.when(middle_even)
    def _():
        q_work[1] = q_own[pl.ds(other_row, ROWS), :]
        g_work[1] = g_own[pl.ds(other_row, ROWS), :]

    @pl.when(jnp.logical_not(middle_even))
    def _():
        q_work[1] = q_sib[pl.ds(own_row, ROWS), :]
        g_work[1] = g_sib[pl.ds(own_row, ROWS), :]

    @pl.when(far_middle)
    def _():
        q_work[2] = q_sib[ROWS:, :]
        g_work[2] = g_sib[ROWS:, :]

    first = jnp.where(jnp.logical_and(far_middle, is_odd), 1, 0)
    last = jnp.where(jnp.logical_and(far_middle, jnp.logical_not(is_odd)), 3, 2)

    own_entry = 3 * parity
    other_entry = jnp.where(middle_even, 1 + parity, jnp.where(is_odd, 1, 2))

    def work_item(item, carry):
        entry = jnp.where(item == 0, own_entry, jnp.where(item == 1, other_entry, 3))
        query_id = slots[chip_base + entry]
        indices = []
        key_base = []
        for distance in range(REACH + 1):
            key_id = query_id - distance
            is_live = jnp.logical_and(
                key_id >= 0, live[query_id * (REACH + 1) + distance] == 1
            )
            index = jnp.int32(0)
            found = jnp.bool_(False)
            for e in range(ENTRIES):
                match = entry_ids[e] == key_id
                index = jnp.where(match, e, index)
                found = jnp.logical_or(found, match)
            ok = jnp.logical_and(is_live, found)
            indices.append(pl.multiple_of(jnp.where(ok, index, 0) * ROWS, ROWS))
            key_base.append(jnp.where(ok, key_id * ROWS, FAR))
        lane = lax.broadcasted_iota(jnp.int32, (1, GROUP * ROWS), 1)
        query_pos = query_id * ROWS + lax.rem(lane, ROWS)
        query_start = row_start[pl.ds(entry, 1), :]
        sub = lax.broadcasted_iota(jnp.int32, (ROWS, GROUP * ROWS), 0)
        for distance in range(REACH + 1):
            key_pos = sub + key_base[distance]
            allowed = jnp.logical_and(key_pos <= query_pos, key_pos >= query_start)
            bias[distance * ROWS : (distance + 1) * ROWS, :] = jnp.where(
                allowed, 0.0, MASKED
            )
        for g in range(KEY_VALUE_HEADS):
            kcols = slice(g * HEAD_WIDTH, (g + 1) * HEAD_WIDTH)
            vcols = slice(KV + g * HEAD_WIDTH, KV + (g + 1) * HEAD_WIDTH)
            heads = [
                slice((GROUP * g + j) * HEAD_WIDTH, (GROUP * g + j + 1) * HEAD_WIDTH)
                for j in range(GROUP)
            ]
            keys = jnp.concatenate([table[pl.ds(i, ROWS), kcols] for i in indices], 0)
            values = jnp.concatenate([table[pl.ds(i, ROWS), vcols] for i in indices], 0)
            q = jnp.concatenate([q_work[item, :, h] for h in heads], 0)
            grad = jnp.concatenate([g_work[item, :, h] for h in heads], 0)
            nt = (((1,), (1,)), ((), ()))
            raw = lax.dot_general(keys, q, nt, preferred_element_type=jnp.float32)
            raw = raw + bias[...]
            top = jnp.max(raw, axis=0, keepdims=True)
            weights = jnp.exp2((raw - top) * EXP2_SCALE)
            probs = weights * (1.0 / jnp.sum(weights, axis=0, keepdims=True))
            grad_scores = lax.dot_general(
                values, grad, nt, preferred_element_type=jnp.float32
            )
            offset = jnp.sum(probs * grad_scores, axis=0, keepdims=True)
            score_low = (probs * (grad_scores - offset)).astype(jnp.bfloat16)
            value_add = jnp.dot(
                probs.astype(jnp.bfloat16), grad, preferred_element_type=jnp.float32
            )
            key_add = jnp.dot(score_low, q, preferred_element_type=jnp.float32)
            query_add = lax.dot_general(
                score_low,
                keys,
                (((0,), (0,)), ((), ())),
                preferred_element_type=jnp.float32,
            )
            query_add = (query_add * SCALE).astype(jnp.bfloat16)
            for j, h in enumerate(heads):
                dq[item, :, h] = query_add[j * ROWS : (j + 1) * ROWS]
            for distance in range(REACH + 1):
                part = slice(distance * ROWS, (distance + 1) * ROWS)
                at = pl.ds(indices[distance], ROWS)
                total[at, kcols] += key_add[part] * SCALE
                total[at, vcols] += value_add[part]
        return carry

    lax.fori_loop(first, last, work_item, 0)

    dq_first[...] = dq[0]
    dq_rest[...] = dq[1:]
    out_own[...] = total[pl.ds(own_at, 128), :]
    out_sib[...] = total[pl.ds(sib_at, 128), :].astype(jnp.bfloat16)
    out_a[...] = total[TABLE_A * ROWS : TABLE_B * ROWS, :].astype(jnp.bfloat16)
    out_b[...] = total[TABLE_B * ROWS : TABLE_C * ROWS, :].astype(jnp.bfloat16)
    out_c[...] = total[TABLE_C * ROWS :, :].astype(jnp.bfloat16)


def query_grad_kernel(place, slots, live, first, rest, theirs, out):
    me = place[0]
    parity = lax.rem(me, 2)
    is_odd = parity == 1
    middle_even, far_middle = fold_flags(2 * (me - parity), slots, live)
    own_row = pl.multiple_of(parity * ROWS, ROWS)
    other_row = pl.multiple_of((1 - parity) * ROWS, ROWS)
    moved = jnp.logical_and(far_middle, is_odd)

    @pl.when(moved)
    def _():
        out[pl.ds(own_row, ROWS), :] = theirs[1]

    @pl.when(jnp.logical_not(moved))
    def _():
        out[pl.ds(own_row, ROWS), :] = first[...]

    @pl.when(middle_even)
    def _():
        out[pl.ds(other_row, ROWS), :] = rest[0]

    @pl.when(jnp.logical_not(middle_even))
    def _():
        out[pl.ds(other_row, ROWS), :] = theirs[0]


def sum_kernel(place, own, sib, back_a, back_b, back_c, key_out, value_out, acc):
    parity = lax.rem(place[0], 2)
    acc[...] = (
        own[...]
        + sib[...].astype(jnp.float32)
        + back_a[...].astype(jnp.float32)
        + back_b[...].astype(jnp.float32)
    )
    at = pl.ds(pl.multiple_of((1 - parity) * ROWS, ROWS), ROWS)
    acc[at, :] += back_c[...].astype(jnp.float32)
    key_out[...] = acc[:, :KV].astype(jnp.bfloat16)
    value_out[...] = acc[:, KV:].astype(jnp.bfloat16)


def vmem(count):
    return [pl.BlockSpec(memory_space=pltpu.VMEM)] * count


def smem(count):
    return [pl.BlockSpec(memory_space=pltpu.SMEM)] * count


def shards(
    queries,
    key_rows_slotted,
    value_rows_slotted,
    output_gradient,
    slot_to_block,
    doc_starts,
    block_live,
):
    me = lax.axis_index("ctx")
    parity = me % 2
    place = me.astype(jnp.int32).reshape(1)
    live = block_live.reshape(-1)
    params = pltpu.CompilerParams(vmem_limit_bytes=VMEM_LIMIT)

    kv = jnp.concatenate([key_rows_slotted, value_rows_slotted], axis=1)
    kv_far = lax.dynamic_slice_in_dim(kv, (1 - parity) * ROWS, ROWS, 0)
    kv_c = send(kv_far, -3, 3)
    kv_a = send(kv, 2, -2)
    kv_b = send(kv, -1, 1)
    kv_sib = send(kv, 1, -1)
    q_sib = send(queries, 1, -1)
    g_sib = send(output_gradient, 1, -1)

    ids = lax.dynamic_slice_in_dim(slot_to_block, 2 * (me - parity), 4, 0)
    positions = ids[:, None] * ROWS + lax.iota(jnp.int32, ROWS)[None, :]
    starts = jnp.max(
        jnp.where(
            doc_starts[None, None, :] <= positions[:, :, None],
            doc_starts[None, None, :],
            0,
        ),
        axis=2,
    )
    row_start = jnp.tile(starts, (1, GROUP))

    bf16 = functools.partial(jax.ShapeDtypeStruct, dtype=jnp.bfloat16)
    dq_first, dq_rest, own, sib, out_a, out_b, out_c = pl.pallas_call(
        attention_kernel,
        out_shape=(
            bf16((ROWS, WIDE)),
            bf16((2, ROWS, WIDE)),
            jax.ShapeDtypeStruct((2 * ROWS, 2 * KV), jnp.float32),
            bf16((2 * ROWS, 2 * KV)),
            bf16((2 * ROWS, 2 * KV)),
            bf16((2 * ROWS, 2 * KV)),
            bf16((ROWS, 2 * KV)),
        ),
        in_specs=smem(3) + vmem(10),
        out_specs=tuple(vmem(7)),
        scratch_shapes=[
            pltpu.VMEM((ENTRIES * ROWS, 2 * KV), jnp.bfloat16),
            pltpu.VMEM((ENTRIES * ROWS, 2 * KV), jnp.float32),
            pltpu.VMEM((3, ROWS, WIDE), jnp.bfloat16),
            pltpu.VMEM((3, ROWS, WIDE), jnp.bfloat16),
            pltpu.VMEM((3, ROWS, WIDE), jnp.bfloat16),
            pltpu.VMEM((SPAN, GROUP * ROWS), jnp.float32),
        ],
        compiler_params=params,
        name="attention_items",
    )(
        place,
        slot_to_block,
        live,
        row_start,
        queries,
        q_sib,
        output_gradient,
        g_sib,
        kv,
        kv_sib,
        kv_a,
        kv_b,
        kv_c,
    )

    back_c = send(out_c, -3, 3)
    back_a = send(out_a, -2, 2)
    back_b = send(out_b, -1, 1)
    back_sib = send(sib, 1, -1)
    dq_sib = send(dq_rest, 1, -1)

    query_grad = pl.pallas_call(
        query_grad_kernel,
        out_shape=bf16((2 * ROWS, WIDE)),
        in_specs=smem(3) + vmem(3),
        out_specs=vmem(1)[0],
        compiler_params=params,
        name="query_gradient_rows",
    )(place, slot_to_block, live, dq_first, dq_rest, dq_sib)

    key_gradient, value_gradient = pl.pallas_call(
        sum_kernel,
        out_shape=(bf16((2 * ROWS, KV)), bf16((2 * ROWS, KV))),
        in_specs=smem(1) + vmem(5),
        out_specs=tuple(vmem(2)),
        scratch_shapes=[pltpu.VMEM((2 * ROWS, 2 * KV), jnp.float32)],
        compiler_params=params,
        name="key_value_gradient_sum",
    )(place, own, back_sib, back_a, back_b, back_c)
    return query_grad, key_gradient, value_gradient


def solution(mesh):
    rows = P(("section", "ctx"), None)
    return jax.shard_map(
        shards,
        mesh=mesh,
        in_specs=(rows, rows, rows, rows, P("section"), P("section"), P("section", None)),
        out_specs=(rows, rows, rows),
        check_vma=False,
    )
```

profile of v0, /device:TPU:16, one launch (start us, length us, event | category | flops | bytes accessed | tf_op | source)
XLA Modules:
  0.0 48.0 jit_solution(13749361968106370683)
XLA Ops:
  0.6 0.1 collective-permute-start
  0.7 0.5 %collective-permute-start.1 = (bf16[128,2048]{1,0:T(8,128)(2,1)}, bf16[128,2048]{1,0:T(8,128)(2,1)S(1)}, u32[]{:S(2)}, u32[]{:S(2)}) collective-permute-start(bf16[128,2048]{1,0:T(8,128)(2,1)} %g_own.1), channel_id=1, source_target_pairs={{0,1},{1,0},{2,3},{3,2},{4,5},{5,4},{6,7},{7,6},{8,9},{9,8},{10,11... | collective-permute-start | bytes 1572872 | tf_op jit(solution)/shard_map/ppermute | solution.py:33
  1.2 0.0 copy-start.2
  1.2 0.0 copy-start.4
  1.2 0.0 copy-start.3
  1.2 0.0 copy-start
  1.2 0.0 copy-start.1
  1.3 1.0 %constant_dynamic-update-slice_fusion.1 = bf16[128,1024]{1,0:T(8,128)(2,1)S(1)} fusion(bf16[128,512]{1,0:T(8,128)(2,1)} %param.8), kind=kLoop, calls=%fused_computation.2 | loop fusion | bytes 262144
  2.3 0.9 %constant_dynamic-update-slice_fusion.kv_own = bf16[128,1024]{1,0:T(8,128)(2,1)S(1)} fusion(bf16[128,1024]{1,0:T(8,128)(2,1)S(1)} %constant_dynamic-update-slice_fusion.1, bf16[128,512]{1,0:T(8,128)(2,1)} %param.9), kind=kLoop, calls=%fused_computation.1 | loop fusion | bytes 262144 | tf_op jit(solution)/shard_map/concatenate | solution.py:268
  3.2 9.0 %collective-permute-start.5 = (bf16[64,1024]{1,0:T(8,128)(2,1)S(1)}, bf16[64,1024]{1,0:T(8,128)(2,1)S(1)}, u32[]{:S(2)}, u32[]{:S(2)}) collective-permute-start(bf16[64,1024]{1,0:T(8,128)(2,1)S(1)} %constant_dynamic-slice_fusion), channel_id=1, source_target_pairs={{0,125},{1,4},{2,127},{3,6},{4,1},{5,8},{6,3},{7,10},{8,5},{9,12},... | collective-permute-start | bytes 393224 | tf_op jit(solution)/shard_map/ppermute | solution.py:33
  12.2 0.0 collective-permute-start.4
  12.2 1.0 %collective-permute-start.3 = (bf16[128,1024]{1,0:T(8,128)(2,1)S(1)}, bf16[128,1024]{1,0:T(8,128)(2,1)S(1)}, u32[]{:S(2)}, u32[]{:S(2)}) collective-permute-start(bf16[128,1024]{1,0:T(8,128)(2,1)S(1)} %constant_dynamic-update-slice_fusion.kv_own), channel_id=1, source_target_pairs={{0,2},{1,127},{2,4},{3,1},{4,6},{5,3},{6,8},{7,5},{8,10},{9,7},{10... | collective-permute-start | bytes 786440 | tf_op jit(solution)/shard_map/ppermute | solution.py:33
  13.3 0.0 copy-done.2
  13.3 0.1 dynamic-slice_multiply_fusion
  13.3 2.8 %collective-permute-done.5.kv_c = bf16[64,1024]{1,0:T(8,128)(2,1)S(1)} collective-permute-done((bf16[64,1024]{1,0:T(8,128)(2,1)S(1)}, bf16[64,1024]{1,0:T(8,128)(2,1)S(1)}, u32[]{:S(2)}, u32[]{:S(2)}) %collective-permute-start.5) | collective-permute-done | bytes 131104 | tf_op jit(solution)/shard_map/ppermute | solution.py:33
  16.1 2.3 %collective-permute-start.2 = (bf16[128,1024]{1,0:T(8,128)(2,1)S(1)}, bf16[128,1024]{1,0:T(8,128)(2,1)S(1)}, u32[]{:S(2)}, u32[]{:S(2)}) collective-permute-start(bf16[128,1024]{1,0:T(8,128)(2,1)S(1)} %constant_dynamic-update-slice_fusion.kv_own), channel_id=1, source_target_pairs={{0,1},{1,0},{2,3},{3,2},{4,5},{5,4},{6,7},{7,6},{8,9},{9,8},{10,11... | collective-permute-start | bytes 786440 | tf_op jit(solution)/shard_map/ppermute | solution.py:33
  18.4 0.1 iota_add_fusion
  18.5 0.0 copy-done.4
  18.5 0.2 select_reduce_fusion
  18.7 0.1 tile.10.row_start
  18.8 0.0 copy-done.3
  18.8 0.1 copy.11
  19.0 0.1 reshape.40.live
  19.1 5.4 %collective-permute-done.4.kv_b = bf16[128,1024]{1,0:T(8,128)(2,1)S(1)} collective-permute-done((bf16[128,1024]{1,0:T(8,128)(2,1)S(1)}, bf16[128,1024]{1,0:T(8,128)(2,1)S(1)}, u32[]{:S(2)}, u32[]{:S(2)}) %collective-permute-start.4) | collective-permute-done | bytes 262176 | tf_op jit(solution)/shard_map/ppermute | solution.py:33
  24.5 0.6 %collective-permute-done.3.kv_a = bf16[128,1024]{1,0:T(8,128)(2,1)S(1)} collective-permute-done((bf16[128,1024]{1,0:T(8,128)(2,1)S(1)}, bf16[128,1024]{1,0:T(8,128)(2,1)S(1)}, u32[]{:S(2)}, u32[]{:S(2)}) %collective-permute-start.3) | collective-permute-done | bytes 262176 | tf_op jit(solution)/shard_map/ppermute | solution.py:33
  25.0 0.0 collective-permute-done.2.kv_sib
  25.0 0.0 collective-permute-done.q_sib
  25.0 0.0 collective-permute-done.1.g_sib
  25.1 0.0 copy-done
  25.1 0.0 copy-done.1
  25.1 4.7 %attention_items.1 = (bf16[64,2048]{1,0:T(8,128)(2,1)S(1)}, bf16[2,64,2048]{2,1,0:T(8,128)(2,1)S(1)}, f32[128,1024]{1,0:T(8,128)S(1)}, bf16[128,1024]{1,0:T(8,12...) custom-call(s32[1]{0:T(128)} %bitcast.place, ...), custom_call_target="tpu_custom_call" | custom-call | tf_op jit(solution)/shard_map/attention_items/pallas_call | solution.py:290
  29.7 0.1 collective-permute-start.6
  29.8 0.5 %collective-permute-start.7 = (bf16[128,1024]{1,0:T(8,128)(2,1)S(1)}, bf16[128,1024]{1,0:T(8,128)(2,1)S(1)}, u32[]{:S(2)}, u32[]{:S(2)}) collective-permute-start(bf16[128,1024]{1,0:T(8,128)(2,1)S(1)} %get-tuple-element.15), channel_id=1, source_target_pairs={{0,1},{1,0},{2,3},{3,2},{4,5},{5,4},{6,7},{7,6},{8,9},{9,8},{10,11... | collective-permute-start | bytes 786440 | tf_op jit(solution)/shard_map/ppermute | solution.py:33
  30.3 2.8 %collective-permute-start.8 = (bf16[128,1024]{1,0:T(8,128)(2,1)S(1)}, bf16[128,1024]{1,0:T(8,128)(2,1)S(1)}, u32[]{:S(2)}, u32[]{:S(2)}) collective-permute-start(bf16[128,1024]{1,0:T(8,128)(2,1)S(1)} %get-tuple-element.16), channel_id=1, source_target_pairs={{0,126},{1,3},{2,0},{3,5},{4,2},{5,7},{6,4},{7,9},{8,6},{9,11},{10... | collective-permute-start | bytes 786440 | tf_op jit(solution)/shard_map/ppermute | solution.py:33
  33.1 2.9 %collective-permute-start.9 = (bf16[128,1024]{1,0:T(8,128)(2,1)S(1)}, bf16[128,1024]{1,0:T(8,128)(2,1)S(1)}, u32[]{:S(2)}, u32[]{:S(2)}) collective-permute-start(bf16[128,1024]{1,0:T(8,128)(2,1)S(1)} %get-tuple-element.17), channel_id=1, source_target_pairs={{0,127},{1,2},{2,1},{3,4},{4,3},{5,6},{6,5},{7,8},{8,7},{9,10},{10... | collective-permute-start | bytes 786440 | tf_op jit(solution)/shard_map/ppermute | solution.py:33
  36.0 0.0 collective-permute-start.10
  36.0 9.6 %collective-permute-done.10.back_c = bf16[64,1024]{1,0:T(8,128)(2,1)S(1)} collective-permute-done((bf16[64,1024]{1,0:T(8,128)(2,1)S(1)}, bf16[64,1024]{1,0:T(8,128)(2,1)S(1)}, u32[]{:S(2)}, u32[]{:S(2)}) %collective-permute-start.10) | collective-permute-done | bytes 131104 | tf_op jit(solution)/shard_map/ppermute | solution.py:33
  45.6 0.0 collective-permute-done.7.sib
  45.6 0.0 collective-permute-done.8.back_a
  45.6 0.0 collective-permute-done.9.back_b
  45.6 0.9 %key_value_gradient_sum.1 = (bf16[128,512]{1,0:T(8,128)(2,1)}, bf16[128,512]{1,0:T(8,128)(2,1)}) custom-call(s32[1]{0:T(128)} %bitcast.place, f32[128,1024]{1,0:T(8,128)S(1)} %get-tuple-element.14.own, bf16[128,1024]{1,0:T(8,128)(2,1)S(1)} %collective-permute-done.7.sib, bf16[128,1024]{1,0:T(8,128)(2,1)S(1)} %collective-permute-done.8.back_a, ...), custom_call_target="tpu_custom_call" | custom-call | tf_op jit(solution)/shard_map/key_value_gradient_sum/pallas_call | solution.py:344
  46.6 0.0 collective-permute-done.6.theirs
  46.6 1.5 %query_gradient_rows.1 = bf16[128,2048]{1,0:T(8,128)(2,1)} custom-call(s32[1]{0:T(128)} %bitcast.place, s32[256]{0:T(256)S(1)} %copy-done.2, s32[1024]{0:T(1024)S(1)} %reshape.40.live, bf16[64,2048]{1,0:T(8,128)(2,1)S(1)} %get-tuple-element.12.first, bf16[2,64,2048]{2,1,0:T(8,128)(2,1)S(1)} %get-tuple-element.13.rest, ...), custom_call_target="tpu_custom_call" | custom-call | tf_op jit(solution)/shard_map/query_gradient_rows/pallas_call | solution.py:335
  (2 shorter events, 0.0 us)
Async XLA Ops:
  0.6 24.4 %collective-permute-start = (bf16[128,2048]{1,0:T(8,128)(2,1)}, bf16[128,2048]{1,0:T(8,128)(2,1)S(1)}, u32[]{:S(2)}, u32[]{:S(2)}) collective-permute-start(bf16[128,2048]{1,0:T(8,128)(2,1)} %q_own.1), channel_id=1, source_target_pairs={{0,1},{1,0},{2,3},{3,2},{4,5},{5,4},{6,7},{7,6},{8,9},{9,8},{10,11... | collective-permute-start | bytes 1572872 | tf_op jit(solution)/shard_map/ppermute | solution.py:33
  0.7 24.3 %collective-permute-start.1 = (bf16[128,2048]{1,0:T(8,128)(2,1)}, bf16[128,2048]{1,0:T(8,128)(2,1)S(1)}, u32[]{:S(2)}, u32[]{:S(2)}) collective-permute-start(bf16[128,2048]{1,0:T(8,128)(2,1)} %g_own.1), channel_id=1, source_target_pairs={{0,1},{1,0},{2,3},{3,2},{4,5},{5,4},{6,7},{7,6},{8,9},{9,8},{10,11... | collective-permute-start | bytes 1572872 | tf_op jit(solution)/shard_map/ppermute | solution.py:33
  1.2 12.0 %copy-start.2 = (s32[256]{0:T(256)S(1)}, s32[256]{0:T(256)}, u32[]{:S(2)}) copy-start(s32[256]{0:T(256)} %slots.3) | copy-start | bytes 3076
  1.2 17.2 %copy-start.4 = (s32[342]{0:T(512)S(1)}, s32[342]{0:T(512)}, u32[]{:S(2)}) copy-start(s32[342]{0:T(512)} %param.12) | copy-start | bytes 4108
  1.2 17.6 %copy-start.3 = (s32[256,4]{0,1:T(4,128)S(1)}, s32[256,4]{0,1:T(4,128)}, u32[]{:S(2)}) copy-start(s32[256,4]{0,1:T(4,128)} %param.13) | copy-start | bytes 12292
  1.2 23.8 %copy-start = (bf16[128,2048]{1,0:T(8,128)(2,1)S(1)}, bf16[128,2048]{1,0:T(8,128)(2,1)}, u32[]{:S(2)}) copy-start(bf16[128,2048]{1,0:T(8,128)(2,1)} %q_own.1) | copy-start | bytes 1572868
  1.2 23.8 %copy-start.1 = (bf16[128,2048]{1,0:T(8,128)(2,1)S(1)}, bf16[128,2048]{1,0:T(8,128)(2,1)}, u32[]{:S(2)}) copy-start(bf16[128,2048]{1,0:T(8,128)(2,1)} %g_own.1) | copy-start | bytes 1572868
  3.2 12.9 %collective-permute-start.5 = (bf16[64,1024]{1,0:T(8,128)(2,1)S(1)}, bf16[64,1024]{1,0:T(8,128)(2,1)S(1)}, u32[]{:S(2)}, u32[]{:S(2)}) collective-permute-start(bf16[64,1024]{1,0:T(8,128)(2,1)S(1)} %constant_dynamic-slice_fusion), channel_id=1, source_target_pairs={{0,125},{1,4},{2,127},{3,6},{4,1},{5,8},{6,3},{7,10},{8,5},{9,12},... | collective-permute-start | bytes 393224 | tf_op jit(solution)/shard_map/ppermute | solution.py:33
  12.2 12.3 %collective-permute-start.4 = (bf16[128,1024]{1,0:T(8,128)(2,1)S(1)}, bf16[128,1024]{1,0:T(8,128)(2,1)S(1)}, u32[]{:S(2)}, u32[]{:S(2)}) collective-permute-start(bf16[128,1024]{1,0:T(8,128)(2,1)S(1)} %constant_dynamic-update-slice_fusion.kv_own), channel_id=1, source_target_pairs={{0,127},{1,2},{2,1},{3,4},{4,3},{5,6},{6,5},{7,8},{8,7},{9,10},{10... | collective-permute-start | bytes 786440 | tf_op jit(solution)/shard_map/ppermute | solution.py:33
  12.2 12.8 %collective-permute-start.3 = (bf16[128,1024]{1,0:T(8,128)(2,1)S(1)}, bf16[128,1024]{1,0:T(8,128)(2,1)S(1)}, u32[]{:S(2)}, u32[]{:S(2)}) collective-permute-start(bf16[128,1024]{1,0:T(8,128)(2,1)S(1)} %constant_dynamic-update-slice_fusion.kv_own), channel_id=1, source_target_pairs={{0,2},{1,127},{2,4},{3,1},{4,6},{5,3},{6,8},{7,5},{8,10},{9,7},{10... | collective-permute-start | bytes 786440 | tf_op jit(solution)/shard_map/ppermute | solution.py:33
  16.1 8.9 %collective-permute-start.2 = (bf16[128,1024]{1,0:T(8,128)(2,1)S(1)}, bf16[128,1024]{1,0:T(8,128)(2,1)S(1)}, u32[]{:S(2)}, u32[]{:S(2)}) collective-permute-start(bf16[128,1024]{1,0:T(8,128)(2,1)S(1)} %constant_dynamic-update-slice_fusion.kv_own), channel_id=1, source_target_pairs={{0,1},{1,0},{2,3},{3,2},{4,5},{5,4},{6,7},{7,6},{8,9},{9,8},{10,11... | collective-permute-start | bytes 786440 | tf_op jit(solution)/shard_map/ppermute | solution.py:33
  29.7 16.8 %collective-permute-start.6 = (bf16[2,64,2048]{2,1,0:T(8,128)(2,1)S(1)}, bf16[2,64,2048]{2,1,0:T(8,128)(2,1)S(1)}, u32[]{:S(2)}, u32[]{:S(2)}) collective-permute-start(bf16[2,64,2048]{2,1,0:T(8,128)(2,1)S(1)} %get-tuple-element.13.rest), channel_id=1, source_target_pairs={{0,1},{1,0},{2,3},{3,2},{4,5},{5,4},{6,7},{7,6},{8,9},{9,8},{10,11... | collective-permute-start | bytes 1572872 | tf_op jit(solution)/shard_map/ppermute | solution.py:33
  29.8 15.8 %collective-permute-start.7 = (bf16[128,1024]{1,0:T(8,128)(2,1)S(1)}, bf16[128,1024]{1,0:T(8,128)(2,1)S(1)}, u32[]{:S(2)}, u32[]{:S(2)}) collective-permute-start(bf16[128,1024]{1,0:T(8,128)(2,1)S(1)} %get-tuple-element.15), channel_id=1, source_target_pairs={{0,1},{1,0},{2,3},{3,2},{4,5},{5,4},{6,7},{7,6},{8,9},{9,8},{10,11... | collective-permute-start | bytes 786440 | tf_op jit(solution)/shard_map/ppermute | solution.py:33
  30.3 15.3 %collective-permute-start.8 = (bf16[128,1024]{1,0:T(8,128)(2,1)S(1)}, bf16[128,1024]{1,0:T(8,128)(2,1)S(1)}, u32[]{:S(2)}, u32[]{:S(2)}) collective-permute-start(bf16[128,1024]{1,0:T(8,128)(2,1)S(1)} %get-tuple-element.16), channel_id=1, source_target_pairs={{0,126},{1,3},{2,0},{3,5},{4,2},{5,7},{6,4},{7,9},{8,6},{9,11},{10... | collective-permute-start | bytes 786440 | tf_op jit(solution)/shard_map/ppermute | solution.py:33
  33.1 12.5 %collective-permute-start.9 = (bf16[128,1024]{1,0:T(8,128)(2,1)S(1)}, bf16[128,1024]{1,0:T(8,128)(2,1)S(1)}, u32[]{:S(2)}, u32[]{:S(2)}) collective-permute-start(bf16[128,1024]{1,0:T(8,128)(2,1)S(1)} %get-tuple-element.17), channel_id=1, source_target_pairs={{0,127},{1,2},{2,1},{3,4},{4,3},{5,6},{6,5},{7,8},{8,7},{9,10},{10... | collective-permute-start | bytes 786440 | tf_op jit(solution)/shard_map/ppermute | solution.py:33
  36.0 9.6 %collective-permute-start.10 = (bf16[64,1024]{1,0:T(8,128)(2,1)S(1)}, bf16[64,1024]{1,0:T(8,128)(2,1)S(1)}, u32[]{:S(2)}, u32[]{:S(2)}) collective-permute-start(bf16[64,1024]{1,0:T(8,128)(2,1)S(1)} %get-tuple-element.18), channel_id=1, source_target_pairs={{0,125},{1,4},{2,127},{3,6},{4,1},{5,8},{6,3},{7,10},{8,5},{9,12},... | collective-permute-start | bytes 393224 | tf_op jit(solution)/shard_map/ppermute | solution.py:33
where the time goes:
time: 48.3 us; the launch traced here: 48 us
  starting transfers between devices  19.2 us (40%)
  waiting for transfers between devices  18.4 us (38%)
  Pallas kernels  7.04 us (15%)
  local copies, waits for them, and re-layouts  2.3 us (5%)
  between operations  0.75 us (2%)
    ppermute x11, starting transfers between devices, send(): return lax.ppermute(array, 'ctx', pairs)  19.2 us
    ppermute x11, waiting for transfers between devices, send(): return lax.ppermute(array, 'ctx', pairs)  18.4 us
    pallas_call x1, Pallas kernels, shards(): pl.pallas_call(attention_kernel, out_shape=(bf16((ROWS, WIDE)), bf16((2,...  4.65 us
    pallas_call x1, Pallas kernels, shards(): pl.pallas_call(query_grad_kernel, out_shape=bf16((2 * ROWS, WIDE)), in_sp...  1.46 us
    unnamed x12, local copies, waits for them, and re-layouts  1.16 us
  transfers between devices with their start and end apart: 11, of which 4 were waited for; matrix products, arithmetic and copies ran while one was open for 6% of the time, Pallas kernels for 2%

commit v1 on v0

--- a/solution.py
+++ b/solution.py
@@ -22,7 +22,7 @@
 MASKED = -1e30
 FAR = 1 << 30
 ENTRIES = 9
-VMEM_LIMIT = 48 * 1024 * 1024
+VMEM_LIMIT = 24 * 1024 * 1024
 
 TABLE_A, TABLE_B, TABLE_C = 4, 6, 8
 
@@ -202,7 +202,37 @@
     out_c[...] = total[TABLE_C * ROWS :, :].astype(jnp.bfloat16)
 
 
-def query_grad_kernel(place, slots, live, first, rest, theirs, out):
+def pack_kernel(place, keys, values, both, far, sems):
+    at = pl.ds(pl.multiple_of((1 - lax.rem(place[0], 2)) * ROWS, ROWS), ROWS)
+    copies = [
+        pltpu.make_async_copy(source, target, sems.at[n])
+        for n, (source, target) in enumerate(
+            [
+                (keys.at[at, :], far.at[:, pl.ds(0, KV)]),
+                (values.at[at, :], far.at[:, pl.ds(KV, KV)]),
+                (keys, both.at[:, pl.ds(0, KV)]),
+                (values, both.at[:, pl.ds(KV, KV)]),
+            ]
+        )
+    ]
+    for copy in copies:
+        copy.start()
+    for copy in copies:
+        copy.wait()
+
+
+def prefetch_kernel(queries, grads, q_own, g_own, sems):
+    copies = [
+        pltpu.make_async_copy(queries, q_own, sems.at[0]),
+        pltpu.make_async_copy(grads, g_own, sems.at[1]),
+    ]
+    for copy in copies:
+        copy.start()
+    for copy in copies:
+        copy.wait()
+
+
+def early_kernel(place, slots, live, first, rest, theirs, own, back_c, out, acc):
     me = place[0]
     parity = lax.rem(me, 2)
     is_odd = parity == 1
@@ -227,23 +257,35 @@
     def _():
         out[pl.ds(other_row, ROWS), :] = theirs[0]
 
-
-def sum_kernel(place, own, sib, back_a, back_b, back_c, key_out, value_out, acc):
-    parity = lax.rem(place[0], 2)
-    acc[...] = (
-        own[...]
-        + sib[...].astype(jnp.float32)
-        + back_a[...].astype(jnp.float32)
-        + back_b[...].astype(jnp.float32)
-    )
-    at = pl.ds(pl.multiple_of((1 - parity) * ROWS, ROWS), ROWS)
-    acc[at, :] += back_c[...].astype(jnp.float32)
-    key_out[...] = acc[:, :KV].astype(jnp.bfloat16)
-    value_out[...] = acc[:, KV:].astype(jnp.bfloat16)
+    acc[pl.ds(own_row, ROWS), :] = own[pl.ds(own_row, ROWS), :]
+    acc[pl.ds(other_row, ROWS), :] = own[pl.ds(other_row, ROWS), :] + back_c[
+        ...
+    ].astype(jnp.float32)
+
+
+def sum_kernel(own, sib, back_a, back_b, key_out, value_out):
+    def total(columns):
+        return (
+            own[:, columns]
+            + sib[:, columns].astype(jnp.float32)
+            + back_a[:, columns].astype(jnp.float32)
+            + back_b[:, columns].astype(jnp.float32)
+        ).astype(jnp.bfloat16)
+
+    key_out[...] = total(slice(0, KV))
+    value_out[...] = total(slice(KV, 2 * KV))
 
 
 def vmem(count):
     return [pl.BlockSpec(memory_space=pltpu.VMEM)] * count
+
+
+def in_hbm(array):
+    return pltpu.with_memory_space_constraint(array, pltpu.HBM)
+
+
+def hbm(count):
+    return [pl.BlockSpec(memory_space=pltpu.HBM)] * count
 
 
 def smem(count):
@@ -260,13 +302,20 @@
     block_live,
 ):
     me = lax.axis_index("ctx")
-    parity = me % 2
     place = me.astype(jnp.int32).reshape(1)
     live = block_live.reshape(-1)
     params = pltpu.CompilerParams(vmem_limit_bytes=VMEM_LIMIT)
 
-    kv = jnp.concatenate([key_rows_slotted, value_rows_slotted], axis=1)
-    kv_far = lax.dynamic_slice_in_dim(kv, (1 - parity) * ROWS, ROWS, 0)
+    bf16 = functools.partial(jax.ShapeDtypeStruct, dtype=jnp.bfloat16)
+    kv, kv_far = pl.pallas_call(
+        pack_kernel,
+        out_shape=(bf16((2 * ROWS, 2 * KV)), bf16((ROWS, 2 * KV))),
+        in_specs=smem(1) + hbm(2),
+        out_specs=tuple(vmem(2)),
+        scratch_shapes=[pltpu.SemaphoreType.DMA((4,))],
+        compiler_params=params,
+        name="key_value_pack",
+    )(place, in_hbm(key_rows_slotted), in_hbm(value_rows_slotted))
     kv_c = send(kv_far, -3, 3)
     kv_a = send(kv, 2, -2)
     kv_b = send(kv, -1, 1)
@@ -274,7 +323,20 @@
     q_sib = send(queries, 1, -1)
     g_sib = send(output_gradient, 1, -1)
 
-    ids = lax.dynamic_slice_in_dim(slot_to_block, 2 * (me - parity), 4, 0)
+    q_own, g_own = pl.pallas_call(
+        prefetch_kernel,
+        out_shape=(bf16((2 * ROWS, WIDE)), bf16((2 * ROWS, WIDE))),
+        in_specs=hbm(2),
+        out_specs=tuple(vmem(2)),
+        scratch_shapes=[pltpu.SemaphoreType.DMA((2,))],
+        compiler_params=params,
+        cost_estimate=pl.CostEstimate(
+            flops=0, bytes_accessed=1 << 21, transcendentals=0
+        ),
+        name="own_rows",
+    )(in_hbm(queries), in_hbm(output_gradient))
+
+    ids = lax.dynamic_slice_in_dim(slot_to_block, 2 * (me - me % 2), 4, 0)
     positions = ids[:, None] * ROWS + lax.iota(jnp.int32, ROWS)[None, :]
     starts = jnp.max(
         jnp.where(
@@ -286,7 +348,6 @@
     )
     row_start = jnp.tile(starts, (1, GROUP))
 
-    bf16 = functools.partial(jax.ShapeDtypeStruct, dtype=jnp.bfloat16)
     dq_first, dq_rest, own, sib, out_a, out_b, out_c = pl.pallas_call(
         attention_kernel,
         out_shape=(
@@ -315,9 +376,9 @@
         slot_to_block,
         live,
         row_start,
-        queries,
+        q_own,
         q_sib,
-        output_gradient,
+        g_own,
         g_sib,
         kv,
         kv_sib,
@@ -332,24 +393,29 @@
     back_sib = send(sib, 1, -1)
     dq_sib = send(dq_rest, 1, -1)
 
-    query_grad = pl.pallas_call(
-        query_grad_kernel,
-        out_shape=bf16((2 * ROWS, WIDE)),
-        in_specs=smem(3) + vmem(3),
-        out_specs=vmem(1)[0],
+    query_grad, own = pl.pallas_call(
+        early_kernel,
+        out_shape=(
+            bf16((2 * ROWS, WIDE)),
+            jax.ShapeDtypeStruct((2 * ROWS, 2 * KV), jnp.float32),
+        ),
+        in_specs=smem(3) + vmem(5),
+        out_specs=tuple(vmem(2)),
         compiler_params=params,
+        cost_estimate=pl.CostEstimate(
+            flops=1 << 36, bytes_accessed=1 << 22, transcendentals=0
+        ),
         name="query_gradient_rows",
-    )(place, slot_to_block, live, dq_first, dq_rest, dq_sib)
+    )(place, slot_to_block, live, dq_first, dq_rest, dq_sib, own, back_c)
 
     key_gradient, value_gradient = pl.pallas_call(
         sum_kernel,
         out_shape=(bf16((2 * ROWS, KV)), bf16((2 * ROWS, KV))),
-        in_specs=smem(1) + vmem(5),
+        in_specs=vmem(4),
         out_specs=tuple(vmem(2)),
-        scratch_shapes=[pltpu.VMEM((2 * ROWS, 2 * KV), jnp.float32)],
         compiler_params=params,
         name="key_value_gradient_sum",
-    )(place, own, back_sib, back_a, back_b, back_c)
+    )(own, back_sib, back_a, back_b)
     return query_grad, key_gradient, value_gradient
 
 

time: 48.3 us -> 44.4 us (0.919)
  waiting for transfers between devices: 18.4 us -> 11.1 us
  Pallas kernels: 7.04 us -> 9.21 us
  starting transfers between devices: 19.2 us -> 21.2 us
  local copies, waits for them, and re-layouts: 2.3 us -> 1.61 us
    ppermute x11, waiting for transfers between devices: 18.4 us -> 11.1 us  [send(): return lax.ppermute(array, 'ctx', pairs)]
    pallas_call x1 -> x3, Pallas kernels: 1.46 us -> 3.79 us  [the longest x1 1.5 us: shards(): pl.pallas_call(early_kernel, out_shape=(bf16((2 * ROWS, WIDE)), jax.Shape...]
    ppermute x11, starting transfers between devices: 19.2 us -> 21.2 us  [send(): return lax.ppermute(array, 'ctx', pairs)]
    concatenate x1 -> x0, local copies, waits for them, and re-layouts: 0.92 us -> none  [shards(): kv = jnp.concatenate([key_rows_slotted, value_rows_slotted], axis=1)]
    unnamed x12 -> x7, local copies, waits for them, and re-layouts: 1.16 us -> 1.4 us
  transfers between devices with their start and end apart: 11 -> 11, of which waited for: 4 -> 5; matrix products, arithmetic and copies ran while one was open for 6% -> 2% of each run, Pallas kernels for 2% -> 9%
where the time goes in v1:
time: 44.4 us; the launch traced here: 44.2 us
  starting transfers between devices  21.2 us (48%)
  waiting for transfers between devices  11.1 us (25%)
  Pallas kernels  9.21 us (21%)
  local copies, waits for them, and re-layouts  1.61 us (4%)
  between operations  0.75 us (2%)
    ppermute x11, starting transfers between devices, send(): return lax.ppermute(array, 'ctx', pairs)  21.2 us
    ppermute x11, waiting for transfers between devices, send(): return lax.ppermute(array, 'ctx', pairs)  11.1 us
    pallas_call x1, Pallas kernels, shards(): pl.pallas_call(attention_kernel, out_shape=(bf16((ROWS, WIDE)), bf16((2,...  4.65 us
    pallas_call x1, Pallas kernels, shards(): pl.pallas_call(early_kernel, out_shape=(bf16((2 * ROWS, WIDE)), jax.Shape...  1.5 us
    unnamed x7, local copies, waits for them, and re-layouts  1.4 us
    pallas_call x1, Pallas kernels, shards(): pl.pallas_call(prefetch_kernel, out_shape=(bf16((2 * ROWS, WIDE)), bf16((...  1.22 us
    pallas_call x1, Pallas kernels, shards(): pl.pallas_call(pack_kernel, out_shape=(bf16((2 * ROWS, 2 * KV)), bf16((RO...  1.07 us
  transfers between devices with their start and end apart: 11, of which 5 were waited for; matrix products, arithmetic and copies ran while one was open for 2% of the time, Pallas kernels for 9%

profile of v1, /device:TPU:16, one launch (start us, length us, event | category | flops | bytes accessed | tf_op | source)
XLA Modules:
  0.0 44.2 jit_solution(594930673030052089)
XLA Ops:
  0.6 0.1 collective-permute-start
  0.7 0.5 %collective-permute-start.1 = (bf16[128,2048]{1,0:T(8,128)(2,1)}, bf16[128,2048]{1,0:T(8,128)(2,1)S(1)}, u32[]{:S(2)}, u32[]{:S(2)}) collective-permute-start(bf16[128,2048]{1,0:T(8,128)(2,1)} %grads.1), channel_id=1, source_target_pairs={{0,1},{1,0},{2,3},{3,2},{4,5},{5,4},{6,7},{7,6},{8,9},{9,8},{10,11... | collective-permute-start | bytes 1572872 | tf_op jit(solution)/shard_map/ppermute | solution.py:33
  1.2 1.1 %key_value_pack.1 = (bf16[128,1024]{1,0:T(8,128)(2,1)S(1)}, bf16[64,1024]{1,0:T(8,128)(2,1)S(1)}) custom-call(s32[1]{0:T(128)} %bitcast.place, bf16[128,512]{1,0:T(8,128)(2,1)} %keys.1, bf16[128,512]{1,0:T(8,128)(2,1)} %values.1), custom_call_target="tpu_custom_call" | custom-call | tf_op jit(solution)/shard_map/key_value_pack/pallas_call | solution.py:310
  2.3 9.0 %collective-permute-start.5 = (bf16[64,1024]{1,0:T(8,128)(2,1)S(1)}, bf16[64,1024]{1,0:T(8,128)(2,1)S(1)}, u32[]{:S(2)}, u32[]{:S(2)}) collective-permute-start(bf16[64,1024]{1,0:T(8,128)(2,1)S(1)} %get-tuple-element.21), channel_id=1, source_target_pairs={{0,125},{1,4},{2,127},{3,6},{4,1},{5,8},{6,3},{7,10},{8,5},{9,12},... | collective-permute-start | bytes 393224 | tf_op jit(solution)/shard_map/ppermute | solution.py:33
  11.3 0.0 collective-permute-start.4
  11.3 1.0 %collective-permute-start.3 = (bf16[128,1024]{1,0:T(8,128)(2,1)S(1)}, bf16[128,1024]{1,0:T(8,128)(2,1)S(1)}, u32[]{:S(2)}, u32[]{:S(2)}) collective-permute-start(bf16[128,1024]{1,0:T(8,128)(2,1)S(1)} %get-tuple-element.20.kv_own), channel_id=1, source_target_pairs={{0,2},{1,127},{2,4},{3,1},{4,6},{5,3},{6,8},{7,5},{8,10},{9,7},{10... | collective-permute-start | bytes 786440 | tf_op jit(solution)/shard_map/ppermute | solution.py:33
  12.4 1.2 %own_rows.1 = (bf16[128,2048]{1,0:T(8,128)(2,1)S(1)}, bf16[128,2048]{1,0:T(8,128)(2,1)S(1)}) custom-call(bf16[128,2048]{1,0:T(8,128)(2,1)} %queries.1, bf16[128,2048]{1,0:T(8,128)(2,1)} %grads.1), custom_call_target="tpu_custom_call" | custom-call | bytes 2097152 | tf_op jit(solution)/shard_map/own_rows/pallas_call | solution.py:326
  13.6 0.0 copy-start
  13.6 0.7 %copy-done = s32[256]{0:T(256)S(1)} copy-done((s32[256]{0:T(256)S(1)}, s32[256]{0:T(256)}, u32[]{:S(2)}) %copy-start) | copy-done | bytes 1048
  14.3 0.0 copy-start.2
  14.3 0.1 dynamic-slice_multiply_fusion
  14.4 0.9 %collective-permute-done.5.kv_c = bf16[64,1024]{1,0:T(8,128)(2,1)S(1)} collective-permute-done((bf16[64,1024]{1,0:T(8,128)(2,1)S(1)}, bf16[64,1024]{1,0:T(8,128)(2,1)S(1)}, u32[]{:S(2)}, u32[]{:S(2)}) %collective-permute-start.5) | collective-permute-done | bytes 131104 | tf_op jit(solution)/shard_map/ppermute | solution.py:33
  15.2 4.2 %collective-permute-start.2 = (bf16[128,1024]{1,0:T(8,128)(2,1)S(1)}, bf16[128,1024]{1,0:T(8,128)(2,1)S(1)}, u32[]{:S(2)}, u32[]{:S(2)}) collective-permute-start(bf16[128,1024]{1,0:T(8,128)(2,1)S(1)} %get-tuple-element.20.kv_own), channel_id=1, source_target_pairs={{0,1},{1,0},{2,3},{3,2},{4,5},{5,4},{6,7},{7,6},{8,9},{9,8},{10,11... | collective-permute-start | bytes 786440 | tf_op jit(solution)/shard_map/ppermute | solution.py:33
  19.4 0.1 iota_add_fusion
  19.5 0.0 copy-done.2
  19.5 0.2 select_reduce_fusion
  19.7 0.0 copy-start.1
  19.8 0.1 tile.10.row_start
  19.8 0.6 %copy-done.1 = s32[256,4]{0,1:T(4,128)S(1)} copy-done((s32[256,4]{0,1:T(4,128)S(1)}, s32[256,4]{0,1:T(4,128)}, u32[]{:S(2)}) %copy-start.1) | copy-done | bytes 4120
  20.4 0.1 copy.11
  20.6 0.1 reshape.40.live
  20.7 2.9 %collective-permute-done.4.kv_b = bf16[128,1024]{1,0:T(8,128)(2,1)S(1)} collective-permute-done((bf16[128,1024]{1,0:T(8,128)(2,1)S(1)}, bf16[128,1024]{1,0:T(8,128)(2,1)S(1)}, u32[]{:S(2)}, u32[]{:S(2)}) %collective-permute-start.4) | collective-permute-done | bytes 262176 | tf_op jit(solution)/shard_map/ppermute | solution.py:33
  23.6 0.6 %collective-permute-done.3.kv_a = bf16[128,1024]{1,0:T(8,128)(2,1)S(1)} collective-permute-done((bf16[128,1024]{1,0:T(8,128)(2,1)S(1)}, bf16[128,1024]{1,0:T(8,128)(2,1)S(1)}, u32[]{:S(2)}, u32[]{:S(2)}) %collective-permute-start.3) | collective-permute-done | bytes 262176 | tf_op jit(solution)/shard_map/ppermute | solution.py:33
  24.1 0.0 collective-permute-done.2.kv_sib
  24.1 0.0 collective-permute-done.q_sib
  24.1 0.0 collective-permute-done.1.g_sib
  24.2 4.7 %attention_items.1 = (bf16[64,2048]{1,0:T(8,128)(2,1)S(1)}, bf16[2,64,2048]{2,1,0:T(8,128)(2,1)S(1)}, f32[128,1024]{1,0:T(8,128)S(1)}, bf16[128,1024]{1,0:T(8,12...) custom-call(s32[1]{0:T(128)} %bitcast.place, ...), custom_call_target="tpu_custom_call" | custom-call | tf_op jit(solution)/shard_map/attention_items/pallas_call | solution.py:351
  28.8 0.1 collective-permute-start.6
  28.9 0.1 collective-permute-start.7
  29.0 0.4 collective-permute-start.8
  29.4 2.9 %collective-permute-start.9 = (bf16[128,1024]{1,0:T(8,128)(2,1)S(1)}, bf16[128,1024]{1,0:T(8,128)(2,1)S(1)}, u32[]{:S(2)}, u32[]{:S(2)}) collective-permute-start(bf16[128,1024]{1,0:T(8,128)(2,1)S(1)} %get-tuple-element.29), channel_id=1, source_target_pairs={{0,126},{1,3},{2,0},{3,5},{4,2},{5,7},{6,4},{7,9},{8,6},{9,11},{10... | collective-permute-start | bytes 786440 | tf_op jit(solution)/shard_map/ppermute | solution.py:33
  32.3 2.9 %collective-permute-start.10 = (bf16[128,1024]{1,0:T(8,128)(2,1)S(1)}, bf16[128,1024]{1,0:T(8,128)(2,1)S(1)}, u32[]{:S(2)}, u32[]{:S(2)}) collective-permute-start(bf16[128,1024]{1,0:T(8,128)(2,1)S(1)} %get-tuple-element.30), channel_id=1, source_target_pairs={{0,127},{1,2},{2,1},{3,4},{4,3},{5,6},{6,5},{7,8},{8,7},{9,10},{10... | collective-permute-start | bytes 786440 | tf_op jit(solution)/shard_map/ppermute | solution.py:33
  35.2 3.4 %collective-permute-done.7.back_c = bf16[64,1024]{1,0:T(8,128)(2,1)S(1)} collective-permute-done((bf16[64,1024]{1,0:T(8,128)(2,1)S(1)}, bf16[64,1024]{1,0:T(8,128)(2,1)S(1)}, u32[]{:S(2)}, u32[]{:S(2)}) %collective-permute-start.7) | collective-permute-done | bytes 131104 | tf_op jit(solution)/shard_map/ppermute | solution.py:33
  38.6 0.0 collective-permute-done.6.theirs
  38.6 1.5 %query_gradient_rows.1 = (bf16[128,2048]{1,0:T(8,128)(2,1)}, f32[128,1024]{1,0:T(8,128)S(1)}) custom-call(s32[1]{0:T(128)} %bitcast.place, s32[256]{0:T(256)S(1)} %copy-done, s32[1024]{0:T(1024)S(1)} %reshape.40.live, bf16[64,2048]{1,0:T(8,128)(2,1)S(1)} %get-tuple-element.22.first, bf16[2,64,2048]{2,1,0:T(8,128)(2,1)S(1)} %get-tuple-element.23.rest, ...), custom_call_target="tpu_custom_call" | custom-call | flops 68719476736 | bytes 4194304 | tf_op jit(solution)/shard_map/query_gradient_rows/pallas_call | solution.py:396
  40.1 0.0 collective-permute-done.8.sib
  40.1 0.0 collective-permute-done.9.back_a
  40.1 3.3 %collective-permute-done.10.back_b = bf16[128,1024]{1,0:T(8,128)(2,1)S(1)} collective-permute-done((bf16[128,1024]{1,0:T(8,128)(2,1)S(1)}, bf16[128,1024]{1,0:T(8,128)(2,1)S(1)}, u32[]{:S(2)}, u32[]{:S(2)}) %collective-permute-start.10) | collective-permute-done | bytes 262176 | tf_op jit(solution)/shard_map/ppermute | solution.py:33
  43.5 0.8 %key_value_gradient_sum.1 = (bf16[128,512]{1,0:T(8,128)(2,1)}, bf16[128,512]{1,0:T(8,128)(2,1)}) custom-call(f32[128,1024]{1,0:T(8,128)S(1)} %get-tuple-element.27.own, bf16[128,1024]{1,0:T(8,128)(2,1)S(1)} %collective-permute-done.8.sib, bf16[128,1024]{1,0:T(8,128)(2,1)S(1)} %collective-permute-done.9.back_a, ...), custom_call_target="tpu_custom_call" | custom-call | tf_op jit(solution)/shard_map/key_value_gradient_sum/pallas_call | solution.py:411
  (1 shorter events, 0.0 us)
Async XLA Ops:
  0.6 23.5 %collective-permute-start = (bf16[128,2048]{1,0:T(8,128)(2,1)}, bf16[128,2048]{1,0:T(8,128)(2,1)S(1)}, u32[]{:S(2)}, u32[]{:S(2)}) collective-permute-start(bf16[128,2048]{1,0:T(8,128)(2,1)} %queries.1), channel_id=1, source_target_pairs={{0,1},{1,0},{2,3},{3,2},{4,5},{5,4},{6,7},{7,6},{8,9},{9,8},{10,11... | collective-permute-start | bytes 1572872 | tf_op jit(solution)/shard_map/ppermute | solution.py:33
  0.7 23.4 %collective-permute-start.1 = (bf16[128,2048]{1,0:T(8,128)(2,1)}, bf16[128,2048]{1,0:T(8,128)(2,1)S(1)}, u32[]{:S(2)}, u32[]{:S(2)}) collective-permute-start(bf16[128,2048]{1,0:T(8,128)(2,1)} %grads.1), channel_id=1, source_target_pairs={{0,1},{1,0},{2,3},{3,2},{4,5},{5,4},{6,7},{7,6},{8,9},{9,8},{10,11... | collective-permute-start | bytes 1572872 | tf_op jit(solution)/shard_map/ppermute | solution.py:33
  2.3 12.9 %collective-permute-start.5 = (bf16[64,1024]{1,0:T(8,128)(2,1)S(1)}, bf16[64,1024]{1,0:T(8,128)(2,1)S(1)}, u32[]{:S(2)}, u32[]{:S(2)}) collective-permute-start(bf16[64,1024]{1,0:T(8,128)(2,1)S(1)} %get-tuple-element.21), channel_id=1, source_target_pairs={{0,125},{1,4},{2,127},{3,6},{4,1},{5,8},{6,3},{7,10},{8,5},{9,12},... | collective-permute-start | bytes 393224 | tf_op jit(solution)/shard_map/ppermute | solution.py:33
  11.3 12.3 %collective-permute-start.4 = (bf16[128,1024]{1,0:T(8,128)(2,1)S(1)}, bf16[128,1024]{1,0:T(8,128)(2,1)S(1)}, u32[]{:S(2)}, u32[]{:S(2)}) collective-permute-start(bf16[128,1024]{1,0:T(8,128)(2,1)S(1)} %get-tuple-element.20.kv_own), channel_id=1, source_target_pairs={{0,127},{1,2},{2,1},{3,4},{4,3},{5,6},{6,5},{7,8},{8,7},{9,10},{10... | collective-permute-start | bytes 786440 | tf_op jit(solution)/shard_map/ppermute | solution.py:33
  11.3 12.8 %collective-permute-start.3 = (bf16[128,1024]{1,0:T(8,128)(2,1)S(1)}, bf16[128,1024]{1,0:T(8,128)(2,1)S(1)}, u32[]{:S(2)}, u32[]{:S(2)}) collective-permute-start(bf16[128,1024]{1,0:T(8,128)(2,1)S(1)} %get-tuple-element.20.kv_own), channel_id=1, source_target_pairs={{0,2},{1,127},{2,4},{3,1},{4,6},{5,3},{6,8},{7,5},{8,10},{9,7},{10... | collective-permute-start | bytes 786440 | tf_op jit(solution)/shard_map/ppermute | solution.py:33
  13.6 0.7 %copy-start = (s32[256]{0:T(256)S(1)}, s32[256]{0:T(256)}, u32[]{:S(2)}) copy-start(s32[256]{0:T(256)} %slots.3) | copy-start | bytes 3076
  14.3 5.2 %copy-start.2 = (s32[342]{0:T(512)S(1)}, s32[342]{0:T(512)}, u32[]{:S(2)}) copy-start(s32[342]{0:T(512)} %param.12) | copy-start | bytes 4108
  15.2 8.9 %collective-permute-start.2 = (bf16[128,1024]{1,0:T(8,128)(2,1)S(1)}, bf16[128,1024]{1,0:T(8,128)(2,1)S(1)}, u32[]{:S(2)}, u32[]{:S(2)}) collective-permute-start(bf16[128,1024]{1,0:T(8,128)(2,1)S(1)} %get-tuple-element.20.kv_own), channel_id=1, source_target_pairs={{0,1},{1,0},{2,3},{3,2},{4,5},{5,4},{6,7},{7,6},{8,9},{9,8},{10,11... | collective-permute-start | bytes 786440 | tf_op jit(solution)/shard_map/ppermute | solution.py:33
  19.7 0.7 %copy-start.1 = (s32[256,4]{0,1:T(4,128)S(1)}, s32[256,4]{0,1:T(4,128)}, u32[]{:S(2)}) copy-start(s32[256,4]{0,1:T(4,128)} %param.13) | copy-start | bytes 12292
  28.8 9.8 %collective-permute-start.6 = (bf16[2,64,2048]{2,1,0:T(8,128)(2,1)S(1)}, bf16[2,64,2048]{2,1,0:T(8,128)(2,1)S(1)}, u32[]{:S(2)}, u32[]{:S(2)}) collective-permute-start(bf16[2,64,2048]{2,1,0:T(8,128)(2,1)S(1)} %get-tuple-element.23.rest), channel_id=1, source_target_pairs={{0,1},{1,0},{2,3},{3,2},{4,5},{5,4},{6,7},{7,6},{8,9},{9,8},{10,11... | collective-permute-start | bytes 1572872 | tf_op jit(solution)/shard_map/ppermute | solution.py:33
  28.9 9.7 %collective-permute-start.7 = (bf16[64,1024]{1,0:T(8,128)(2,1)S(1)}, bf16[64,1024]{1,0:T(8,128)(2,1)S(1)}, u32[]{:S(2)}, u32[]{:S(2)}) collective-permute-start(bf16[64,1024]{1,0:T(8,128)(2,1)S(1)} %get-tuple-element.25), channel_id=1, source_target_pairs={{0,125},{1,4},{2,127},{3,6},{4,1},{5,8},{6,3},{7,10},{8,5},{9,12},... | collective-permute-start | bytes 393224 | tf_op jit(solution)/shard_map/ppermute | solution.py:33
  29.0 11.1 %collective-permute-start.8 = (bf16[128,1024]{1,0:T(8,128)(2,1)S(1)}, bf16[128,1024]{1,0:T(8,128)(2,1)S(1)}, u32[]{:S(2)}, u32[]{:S(2)}) collective-permute-start(bf16[128,1024]{1,0:T(8,128)(2,1)S(1)} %get-tuple-element.28), channel_id=1, source_target_pairs={{0,1},{1,0},{2,3},{3,2},{4,5},{5,4},{6,7},{7,6},{8,9},{9,8},{10,11... | collective-permute-start | bytes 786440 | tf_op jit(solution)/shard_map/ppermute | solution.py:33
  29.4 10.7 %collective-permute-start.9 = (bf16[128,1024]{1,0:T(8,128)(2,1)S(1)}, bf16[128,1024]{1,0:T(8,128)(2,1)S(1)}, u32[]{:S(2)}, u32[]{:S(2)}) collective-permute-start(bf16[128,1024]{1,0:T(8,128)(2,1)S(1)} %get-tuple-element.29), channel_id=1, source_target_pairs={{0,126},{1,3},{2,0},{3,5},{4,2},{5,7},{6,4},{7,9},{8,6},{9,11},{10... | collective-permute-start | bytes 786440 | tf_op jit(solution)/shard_map/ppermute | solution.py:33
  32.3 11.1 %collective-permute-start.10 = (bf16[128,1024]{1,0:T(8,128)(2,1)S(1)}, bf16[128,1024]{1,0:T(8,128)(2,1)S(1)}, u32[]{:S(2)}, u32[]{:S(2)}) collective-permute-start(bf16[128,1024]{1,0:T(8,128)(2,1)S(1)} %get-tuple-element.30), channel_id=1, source_target_pairs={{0,127},{1,2},{2,1},{3,4},{4,3},{5,6},{6,5},{7,8},{8,7},{9,10},{10... | collective-permute-start | bytes 786440 | tf_op jit(solution)/shard_map/ppermute | solution.py:33

commit v2 on v1

--- a/solution.py
+++ b/solution.py
@@ -37,7 +37,7 @@
     half = slots.shape[0] // 2
     middle_even = slots[chip_base] == half - 1
     middle_odd = slots[chip_base + 2] == half - 1
-    far_middle = jnp.logical_and(middle_odd, live[half * (REACH + 1) + REACH] == 1)
+    far_middle = jnp.logical_and(middle_odd, live[REACH, half] == 1)
     return middle_even, far_middle
 
 
@@ -52,8 +52,8 @@
     g_sib,
     kv_own,
     kv_sib,
+    kv_b,
     kv_a,
-    kv_b,
     kv_c,
     dq_first,
     dq_rest,
@@ -128,7 +128,7 @@
         for distance in range(REACH + 1):
             key_id = query_id - distance
             is_live = jnp.logical_and(
-                key_id >= 0, live[query_id * (REACH + 1) + distance] == 1
+                key_id >= 0, live[distance, query_id] == 1
             )
             index = jnp.int32(0)
             found = jnp.bool_(False)
@@ -202,33 +202,78 @@
     out_c[...] = total[TABLE_C * ROWS :, :].astype(jnp.bfloat16)
 
 
-def pack_kernel(place, keys, values, both, far, sems):
-    at = pl.ds(pl.multiple_of((1 - lax.rem(place[0], 2)) * ROWS, ROWS), ROWS)
+def pack_kernel(
+    place,
+    slots_hbm,
+    docs_hbm,
+    keys,
+    values,
+    queries,
+    grads,
+    both,
+    far,
+    q_own,
+    g_own,
+    row_start,
+    slots,
+    docs,
+    sems,
+):
+    parity = lax.rem(place[0], 2)
+    at = pl.ds(pl.multiple_of((1 - parity) * ROWS, ROWS), ROWS)
     copies = [
         pltpu.make_async_copy(source, target, sems.at[n])
         for n, (source, target) in enumerate(
             [
+                (slots_hbm, slots),
+                (docs_hbm, docs),
                 (keys.at[at, :], far.at[:, pl.ds(0, KV)]),
                 (values.at[at, :], far.at[:, pl.ds(KV, KV)]),
                 (keys, both.at[:, pl.ds(0, KV)]),
                 (values, both.at[:, pl.ds(KV, KV)]),
+                (queries, q_own),
+                (grads, g_own),
             ]
         )
     ]
     for copy in copies:
         copy.start()
-    for copy in copies:
-        copy.wait()
-
-
-def prefetch_kernel(queries, grads, q_own, g_own, sems):
-    copies = [
-        pltpu.make_async_copy(queries, q_own, sems.at[0]),
-        pltpu.make_async_copy(grads, g_own, sems.at[1]),
-    ]
-    for copy in copies:
-        copy.start()
-    for copy in copies:
+    copies[0].wait()
+    copies[1].wait()
+    count = docs.shape[0]
+    lane = lax.rem(lax.broadcasted_iota(jnp.int32, (1, GROUP * ROWS), 1), ROWS)
+    for entry in range(4):
+        first = slots[2 * (place[0] - parity) + entry] * ROWS
+
+        def halve(_, bounds):
+            low, high = bounds
+            middle = (low + high) // 2
+            begun = docs[middle] <= first
+            inside = low < high
+            return (
+                jnp.where(jnp.logical_and(inside, begun), middle + 1, low),
+                jnp.where(jnp.logical_and(inside, jnp.logical_not(begun)), middle, high),
+            )
+
+        begun, _ = lax.fori_loop(
+            0, count.bit_length(), halve, (jnp.int32(1), jnp.int32(count))
+        )
+
+        def more(state):
+            index, _ = state
+            start = docs[jnp.minimum(index, count - 1)]
+            return jnp.logical_and(index < count, start < first + ROWS)
+
+        def step(state):
+            index, row = state
+            start = docs[index]
+            return index + 1, jnp.where(lane + first >= start, start, row)
+
+        _, row = lax.while_loop(
+            more, step, (begun, jnp.full((1, GROUP * ROWS), docs[begun - 1]))
+        )
+        row_start[pl.ds(entry, 1), :] = row
+    for copy in copies[2:]:
         copy.wait()
 
 
@@ -303,50 +348,43 @@
 ):
     me = lax.axis_index("ctx")
     place = me.astype(jnp.int32).reshape(1)
-    live = block_live.reshape(-1)
+    live = block_live.T
     params = pltpu.CompilerParams(vmem_limit_bytes=VMEM_LIMIT)
 
     bf16 = functools.partial(jax.ShapeDtypeStruct, dtype=jnp.bfloat16)
-    kv, kv_far = pl.pallas_call(
+    kv, kv_far, q_own, g_own, row_start = pl.pallas_call(
         pack_kernel,
-        out_shape=(bf16((2 * ROWS, 2 * KV)), bf16((ROWS, 2 * KV))),
-        in_specs=smem(1) + hbm(2),
-        out_specs=tuple(vmem(2)),
-        scratch_shapes=[pltpu.SemaphoreType.DMA((4,))],
+        out_shape=(
+            bf16((2 * ROWS, 2 * KV)),
+            bf16((ROWS, 2 * KV)),
+            bf16((2 * ROWS, WIDE)),
+            bf16((2 * ROWS, WIDE)),
+            jax.ShapeDtypeStruct((4, GROUP * ROWS), jnp.int32),
+        ),
+        in_specs=smem(1) + hbm(6),
+        out_specs=tuple(vmem(5)),
+        scratch_shapes=[
+            pltpu.SMEM(slot_to_block.shape, jnp.int32),
+            pltpu.SMEM(doc_starts.shape, jnp.int32),
+            pltpu.SemaphoreType.DMA((8,)),
+        ],
         compiler_params=params,
-        name="key_value_pack",
-    )(place, in_hbm(key_rows_slotted), in_hbm(value_rows_slotted))
+        name="prepare",
+    )(
+        place,
+        in_hbm(slot_to_block),
+        in_hbm(doc_starts),
+        in_hbm(key_rows_slotted),
+        in_hbm(value_rows_slotted),
+        in_hbm(queries),
+        in_hbm(output_gradient),
+    )
     kv_c = send(kv_far, -3, 3)
     kv_a = send(kv, 2, -2)
     kv_b = send(kv, -1, 1)
     kv_sib = send(kv, 1, -1)
     q_sib = send(queries, 1, -1)
     g_sib = send(output_gradient, 1, -1)
-
-    q_own, g_own = pl.pallas_call(
-        prefetch_kernel,
-        out_shape=(bf16((2 * ROWS, WIDE)), bf16((2 * ROWS, WIDE))),
-        in_specs=hbm(2),
-        out_specs=tuple(vmem(2)),
-        scratch_shapes=[pltpu.SemaphoreType.DMA((2,))],
-        compiler_params=params,
-        cost_estimate=pl.CostEstimate(
-            flops=0, bytes_accessed=1 << 21, transcendentals=0
-        ),
-        name="own_rows",
-    )(in_hbm(queries), in_hbm(output_gradient))
-
-    ids = lax.dynamic_slice_in_dim(slot_to_block, 2 * (me - me % 2), 4, 0)
-    positions = ids[:, None] * ROWS + lax.iota(jnp.int32, ROWS)[None, :]
-    starts = jnp.max(
-        jnp.where(
-            doc_starts[None, None, :] <= positions[:, :, None],
-            doc_starts[None, None, :],
-            0,
-        ),
-        axis=2,
-    )
-    row_start = jnp.tile(starts, (1, GROUP))
 
     dq_first, dq_rest, own, sib, out_a, out_b, out_c = pl.pallas_call(
         attention_kernel,
@@ -373,7 +411,7 @@
         name="attention_items",
     )(
         place,
-        slot_to_block,
+        in_hbm(slot_to_block),
         live,
         row_start,
         q_own,
@@ -382,8 +420,8 @@
         g_sib,
         kv,
         kv_sib,
+        kv_b,
         kv_a,
-        kv_b,
         kv_c,
     )
 
@@ -406,7 +444,16 @@
             flops=1 << 36, bytes_accessed=1 << 22, transcendentals=0
         ),
         name="query_gradient_rows",
-    )(place, slot_to_block, live, dq_first, dq_rest, dq_sib, own, back_c)
+    )(
+        place,
+        in_hbm(slot_to_block),
+        live,
+        dq_first,
+        dq_rest,
+        dq_sib,
+        own,
+        back_c,
+    )
 
     key_gradient, value_gradient = pl.pallas_call(
         sum_kernel,

time: 44.4 us -> 45.8 us (1.032)
  waiting for transfers between devices: 11.1 us -> 19.1 us
  starting transfers between devices: 21.2 us -> 17.3 us
  local copies, waits for them, and re-layouts: 1.61 us -> 0.01 us
  Pallas kernels: 9.21 us -> 8.56 us
    ppermute x11, waiting for transfers between devices: 11.1 us -> 19.1 us  [send(): return lax.ppermute(array, 'ctx', pairs)]
    ppermute x11, starting transfers between devices: 21.2 us -> 17.3 us  [send(): return lax.ppermute(array, 'ctx', pairs)]
    unnamed x7 -> x2, local copies, waits for them, and re-layouts: 1.4 us -> 0.01 us
    pallas_call x1 -> x0, Pallas kernels: 1.22 us -> none  [shards(): pl.pallas_call(prefetch_kernel, out_shape=(bf16((2 * ROWS, WIDE)), bf16((...]
  transfers between devices with their start and end apart: 11 -> 11, of which waited for: 5 -> 5; matrix products, arithmetic and copies ran while one was open for 2% -> 0% of each run, Pallas kernels for 9% -> 7%
where the time goes in v2:
time: 45.8 us; the launch traced here: 45.7 us
  waiting for transfers between devices  19.1 us (42%)
  starting transfers between devices  17.3 us (38%)
  Pallas kernels  8.56 us (19%)
  between operations  0.69 us (2%)
    ppermute x11, waiting for transfers between devices, send(): return lax.ppermute(array, 'ctx', pairs)  19.1 us
    ppermute x11, starting transfers between devices, send(): return lax.ppermute(array, 'ctx', pairs)  17.3 us
    pallas_call x1, Pallas kernels, shards(): pl.pallas_call(attention_kernel, out_shape=(bf16((ROWS, WIDE)), bf16((2,...  4.73 us
    pallas_call x1, Pallas kernels, shards(): pl.pallas_call(early_kernel, out_shape=(bf16((2 * ROWS, WIDE)), jax.Shape...  1.58 us
    pallas_call x1, Pallas kernels, shards(): pl.pallas_call(pack_kernel, out_shape=(bf16((2 * ROWS, 2 * KV)), bf16((RO...  1.47 us
  transfers between devices with their start and end apart: 11, of which 5 were waited for; matrix products, arithmetic and copies ran while one was open for 0% of the time, Pallas kernels for 7%

profile of v2, /device:TPU:16, one launch (start us, length us, event | category | flops | bytes accessed | tf_op | source)
XLA Modules:
  0.0 45.7 jit_solution(3631015235818016882)
XLA Ops:
  0.6 0.1 collective-permute-start
  0.7 0.5 %collective-permute-start.1 = (bf16[128,2048]{1,0:T(8,128)(2,1)}, bf16[128,2048]{1,0:T(8,128)(2,1)S(1)}, u32[]{:S(2)}, u32[]{:S(2)}) collective-permute-start(bf16[128,2048]{1,0:T(8,128)(2,1)} %grads.1), channel_id=1, source_target_pairs={{0,1},{1,0},{2,3},{3,2},{4,5},{5,4},{6,7},{7,6},{8,9},{9,8},{10,11... | collective-permute-start | bytes 1572872 | tf_op jit(solution)/shard_map/ppermute | solution.py:33
  1.2 1.5 %prepare.1 = (bf16[128,1024]{1,0:T(8,128)(2,1)S(1)}, bf16[64,1024]{1,0:T(8,128)(2,1)S(1)}, bf16[128,2048]{1,0:T(8,128)(2,1)S(1)}, bf16[128,2048]{1,0:T(8,128)(2,1)S(1)}, s32[4,256]{1,0:T(4,128)S(1)}) custom-call(s32[1]{0:T(128)} %bitcast.place, s32[256]{0:T(256)} %slots.3, s32[342]{0:T(512)} %docs_hbm.1, bf16[128,512]{1,0:T(8,128)(2,1)} %keys.1, ...), custom_call_target="tpu_custom_call" | custom-call | tf_op jit(solution)/shard_map/prepare/pallas_call | solution.py:355
  2.7 9.0 %collective-permute-start.5 = (bf16[64,1024]{1,0:T(8,128)(2,1)S(1)}, bf16[64,1024]{1,0:T(8,128)(2,1)S(1)}, u32[]{:S(2)}, u32[]{:S(2)}) collective-permute-start(bf16[64,1024]{1,0:T(8,128)(2,1)S(1)} %get-tuple-element.23), channel_id=1, source_target_pairs={{0,125},{1,4},{2,127},{3,6},{4,1},{5,8},{6,3},{7,10},{8,5},{9,12},... | collective-permute-start | bytes 393224 | tf_op jit(solution)/shard_map/ppermute | solution.py:33
  11.7 0.0 copy-start
  11.7 1.0 %collective-permute-start.4 = (bf16[128,1024]{1,0:T(8,128)(2,1)S(1)}, bf16[128,1024]{1,0:T(8,128)(2,1)S(1)}, u32[]{:S(2)}, u32[]{:S(2)}) collective-permute-start(bf16[128,1024]{1,0:T(8,128)(2,1)S(1)} %get-tuple-element.22.kv_own), channel_id=1, source_target_pairs={{0,2},{1,127},{2,4},{3,1},{4,6},{5,3},{6,8},{7,5},{8,10},{9,7},{10... | collective-permute-start | bytes 786440 | tf_op jit(solution)/shard_map/ppermute | solution.py:33
  12.7 0.0 collective-permute-start.3
  12.7 4.3 %collective-permute-done.5.kv_c = bf16[64,1024]{1,0:T(8,128)(2,1)S(1)} collective-permute-done((bf16[64,1024]{1,0:T(8,128)(2,1)S(1)}, bf16[64,1024]{1,0:T(8,128)(2,1)S(1)}, u32[]{:S(2)}, u32[]{:S(2)}) %collective-permute-start.5) | collective-permute-done | bytes 131104 | tf_op jit(solution)/shard_map/ppermute | solution.py:33
  17.0 0.0 collective-permute-start.2
  17.0 7.8 %collective-permute-done.4.kv_a = bf16[128,1024]{1,0:T(8,128)(2,1)S(1)} collective-permute-done((bf16[128,1024]{1,0:T(8,128)(2,1)S(1)}, bf16[128,1024]{1,0:T(8,128)(2,1)S(1)}, u32[]{:S(2)}, u32[]{:S(2)}) %collective-permute-start.4) | collective-permute-done | bytes 262176 | tf_op jit(solution)/shard_map/ppermute | solution.py:33
  24.8 0.4 collective-permute-done.3.kv_b
  25.1 0.0 collective-permute-done.2.kv_sib
  25.1 0.0 collective-permute-done.q_sib
  25.1 0.0 collective-permute-done.1.g_sib
  25.1 0.0 copy-done
  25.1 4.7 %attention_items.1 = (bf16[64,2048]{1,0:T(8,128)(2,1)S(1)}, bf16[2,64,2048]{2,1,0:T(8,128)(2,1)S(1)}, f32[128,1024]{1,0:T(8,128)S(1)}, bf16[128,1024]{1,0:T(8,12...) custom-call(s32[1]{0:T(128)} %bitcast.place, s32[256]{0:T(256)} %slots.3, ...), custom_call_target="tpu_custom_call" | custom-call | tf_op jit(solution)/shard_map/attention_items/pallas_call | solution.py:389
  29.9 0.1 collective-permute-start.6
  30.0 0.6 %collective-permute-start.7 = (bf16[64,1024]{1,0:T(8,128)(2,1)S(1)}, bf16[64,1024]{1,0:T(8,128)(2,1)S(1)}, u32[]{:S(2)}, u32[]{:S(2)}) collective-permute-start(bf16[64,1024]{1,0:T(8,128)(2,1)S(1)} %get-tuple-element.27), channel_id=1, source_target_pairs={{0,125},{1,4},{2,127},{3,6},{4,1},{5,8},{6,3},{7,10},{8,5},{9,12},... | collective-permute-start | bytes 393224 | tf_op jit(solution)/shard_map/ppermute | solution.py:33
  30.5 0.0 collective-permute-start.8
  30.5 1.6 %collective-permute-start.9 = (bf16[128,1024]{1,0:T(8,128)(2,1)S(1)}, bf16[128,1024]{1,0:T(8,128)(2,1)S(1)}, u32[]{:S(2)}, u32[]{:S(2)}) collective-permute-start(bf16[128,1024]{1,0:T(8,128)(2,1)S(1)} %get-tuple-element.31), channel_id=1, source_target_pairs={{0,126},{1,3},{2,0},{3,5},{4,2},{5,7},{6,4},{7,9},{8,6},{9,11},{10... | collective-permute-start | bytes 786440 | tf_op jit(solution)/shard_map/ppermute | solution.py:33
  32.1 4.5 %collective-permute-start.10 = (bf16[128,1024]{1,0:T(8,128)(2,1)S(1)}, bf16[128,1024]{1,0:T(8,128)(2,1)S(1)}, u32[]{:S(2)}, u32[]{:S(2)}) collective-permute-start(bf16[128,1024]{1,0:T(8,128)(2,1)S(1)} %get-tuple-element.32), channel_id=1, source_target_pairs={{0,127},{1,2},{2,1},{3,4},{4,3},{5,6},{6,5},{7,8},{8,7},{9,10},{10... | collective-permute-start | bytes 786440 | tf_op jit(solution)/shard_map/ppermute | solution.py:33
  36.6 3.1 %collective-permute-done.7.back_c = bf16[64,1024]{1,0:T(8,128)(2,1)S(1)} collective-permute-done((bf16[64,1024]{1,0:T(8,128)(2,1)S(1)}, bf16[64,1024]{1,0:T(8,128)(2,1)S(1)}, u32[]{:S(2)}, u32[]{:S(2)}) %collective-permute-start.7) | collective-permute-done | bytes 131104 | tf_op jit(solution)/shard_map/ppermute | solution.py:33
  39.7 0.0 collective-permute-done.6.theirs
  39.7 1.6 %query_gradient_rows.1 = (bf16[128,2048]{1,0:T(8,128)(2,1)}, f32[128,1024]{1,0:T(8,128)S(1)}) custom-call(s32[1]{0:T(128)} %bitcast.place, s32[256]{0:T(256)} %slots.3, s32[4,256]{1,0:T(4,128)S(1)} %bitcast.3, bf16[64,2048]{1,0:T(8,128)(2,1)S(1)} %get-tuple-element.24.first, bf16[2,64,2048]{2,1,0:T(8,128)(2,1)S(1)} %get-tuple-element.25.rest, ...), custom_call_target="tpu_custom_call" | custom-call | flops 68719476736 | bytes 4194304 | tf_op jit(solution)/shard_map/query_gradient_rows/pallas_call | solution.py:434
  41.3 0.0 collective-permute-done.8.sib
  41.3 0.0 collective-permute-done.9.back_a
  41.3 3.6 %collective-permute-done.10.back_b = bf16[128,1024]{1,0:T(8,128)(2,1)S(1)} collective-permute-done((bf16[128,1024]{1,0:T(8,128)(2,1)S(1)}, bf16[128,1024]{1,0:T(8,128)(2,1)S(1)}, u32[]{:S(2)}, u32[]{:S(2)}) %collective-permute-start.10) | collective-permute-done | bytes 262176 | tf_op jit(solution)/shard_map/ppermute | solution.py:33
  44.9 0.8 %key_value_gradient_sum.1 = (bf16[128,512]{1,0:T(8,128)(2,1)}, bf16[128,512]{1,0:T(8,128)(2,1)}) custom-call(f32[128,1024]{1,0:T(8,128)S(1)} %get-tuple-element.29.own, bf16[128,1024]{1,0:T(8,128)(2,1)S(1)} %collective-permute-done.8.sib, bf16[128,1024]{1,0:T(8,128)(2,1)S(1)} %collective-permute-done.9.back_a, ...), custom_call_target="tpu_custom_call" | custom-call | tf_op jit(solution)/shard_map/key_value_gradient_sum/pallas_call | solution.py:458
Async XLA Ops:
  0.6 24.5 %collective-permute-start = (bf16[128,2048]{1,0:T(8,128)(2,1)}, bf16[128,2048]{1,0:T(8,128)(2,1)S(1)}, u32[]{:S(2)}, u32[]{:S(2)}) collective-permute-start(bf16[128,2048]{1,0:T(8,128)(2,1)} %queries.1), channel_id=1, source_target_pairs={{0,1},{1,0},{2,3},{3,2},{4,5},{5,4},{6,7},{7,6},{8,9},{9,8},{10,11... | collective-permute-start | bytes 1572872 | tf_op jit(solution)/shard_map/ppermute | solution.py:33
  0.7 24.4 %collective-permute-start.1 = (bf16[128,2048]{1,0:T(8,128)(2,1)}, bf16[128,2048]{1,0:T(8,128)(2,1)S(1)}, u32[]{:S(2)}, u32[]{:S(2)}) collective-permute-start(bf16[128,2048]{1,0:T(8,128)(2,1)} %grads.1), channel_id=1, source_target_pairs={{0,1},{1,0},{2,3},{3,2},{4,5},{5,4},{6,7},{7,6},{8,9},{9,8},{10,11... | collective-permute-start | bytes 1572872 | tf_op jit(solution)/shard_map/ppermute | solution.py:33
  2.7 14.3 %collective-permute-start.5 = (bf16[64,1024]{1,0:T(8,128)(2,1)S(1)}, bf16[64,1024]{1,0:T(8,128)(2,1)S(1)}, u32[]{:S(2)}, u32[]{:S(2)}) collective-permute-start(bf16[64,1024]{1,0:T(8,128)(2,1)S(1)} %get-tuple-element.23), channel_id=1, source_target_pairs={{0,125},{1,4},{2,127},{3,6},{4,1},{5,8},{6,3},{7,10},{8,5},{9,12},... | collective-permute-start | bytes 393224 | tf_op jit(solution)/shard_map/ppermute | solution.py:33
  11.7 13.4 %copy-start = (s32[256,4]{0,1:T(4,128)S(1)}, s32[256,4]{0,1:T(4,128)}, u32[]{:S(2)}) copy-start(s32[256,4]{0,1:T(4,128)} %param.13) | copy-start | bytes 12292
  11.7 13.0 %collective-permute-start.4 = (bf16[128,1024]{1,0:T(8,128)(2,1)S(1)}, bf16[128,1024]{1,0:T(8,128)(2,1)S(1)}, u32[]{:S(2)}, u32[]{:S(2)}) collective-permute-start(bf16[128,1024]{1,0:T(8,128)(2,1)S(1)} %get-tuple-element.22.kv_own), channel_id=1, source_target_pairs={{0,2},{1,127},{2,4},{3,1},{4,6},{5,3},{6,8},{7,5},{8,10},{9,7},{10... | collective-permute-start | bytes 786440 | tf_op jit(solution)/shard_map/ppermute | solution.py:33
  12.7 12.4 %collective-permute-start.3 = (bf16[128,1024]{1,0:T(8,128)(2,1)S(1)}, bf16[128,1024]{1,0:T(8,128)(2,1)S(1)}, u32[]{:S(2)}, u32[]{:S(2)}) collective-permute-start(bf16[128,1024]{1,0:T(8,128)(2,1)S(1)} %get-tuple-element.22.kv_own), channel_id=1, source_target_pairs={{0,127},{1,2},{2,1},{3,4},{4,3},{5,6},{6,5},{7,8},{8,7},{9,10},{10... | collective-permute-start | bytes 786440 | tf_op jit(solution)/shard_map/ppermute | solution.py:33
  17.0 8.1 %collective-permute-start.2 = (bf16[128,1024]{1,0:T(8,128)(2,1)S(1)}, bf16[128,1024]{1,0:T(8,128)(2,1)S(1)}, u32[]{:S(2)}, u32[]{:S(2)}) collective-permute-start(bf16[128,1024]{1,0:T(8,128)(2,1)S(1)} %get-tuple-element.22.kv_own), channel_id=1, source_target_pairs={{0,1},{1,0},{2,3},{3,2},{4,5},{5,4},{6,7},{7,6},{8,9},{9,8},{10,11... | collective-permute-start | bytes 786440 | tf_op jit(solution)/shard_map/ppermute | solution.py:33
  29.9 9.8 %collective-permute-start.6 = (bf16[2,64,2048]{2,1,0:T(8,128)(2,1)S(1)}, bf16[2,64,2048]{2,1,0:T(8,128)(2,1)S(1)}, u32[]{:S(2)}, u32[]{:S(2)}) collective-permute-start(bf16[2,64,2048]{2,1,0:T(8,128)(2,1)S(1)} %get-tuple-element.25.rest), channel_id=1, source_target_pairs={{0,1},{1,0},{2,3},{3,2},{4,5},{5,4},{6,7},{7,6},{8,9},{9,8},{10,11... | collective-permute-start | bytes 1572872 | tf_op jit(solution)/shard_map/ppermute | solution.py:33
  30.0 9.7 %collective-permute-start.7 = (bf16[64,1024]{1,0:T(8,128)(2,1)S(1)}, bf16[64,1024]{1,0:T(8,128)(2,1)S(1)}, u32[]{:S(2)}, u32[]{:S(2)}) collective-permute-start(bf16[64,1024]{1,0:T(8,128)(2,1)S(1)} %get-tuple-element.27), channel_id=1, source_target_pairs={{0,125},{1,4},{2,127},{3,6},{4,1},{5,8},{6,3},{7,10},{8,5},{9,12},... | collective-permute-start | bytes 393224 | tf_op jit(solution)/shard_map/ppermute | solution.py:33
  30.5 10.7 %collective-permute-start.8 = (bf16[128,1024]{1,0:T(8,128)(2,1)S(1)}, bf16[128,1024]{1,0:T(8,128)(2,1)S(1)}, u32[]{:S(2)}, u32[]{:S(2)}) collective-permute-start(bf16[128,1024]{1,0:T(8,128)(2,1)S(1)} %get-tuple-element.30), channel_id=1, source_target_pairs={{0,1},{1,0},{2,3},{3,2},{4,5},{5,4},{6,7},{7,6},{8,9},{9,8},{10,11... | collective-permute-start | bytes 786440 | tf_op jit(solution)/shard_map/ppermute | solution.py:33
  30.5 10.7 %collective-permute-start.9 = (bf16[128,1024]{1,0:T(8,128)(2,1)S(1)}, bf16[128,1024]{1,0:T(8,128)(2,1)S(1)}, u32[]{:S(2)}, u32[]{:S(2)}) collective-permute-start(bf16[128,1024]{1,0:T(8,128)(2,1)S(1)} %get-tuple-element.31), channel_id=1, source_target_pairs={{0,126},{1,3},{2,0},{3,5},{4,2},{5,7},{6,4},{7,9},{8,6},{9,11},{10... | collective-permute-start | bytes 786440 | tf_op jit(solution)/shard_map/ppermute | solution.py:33
  32.1 12.7 %collective-permute-start.10 = (bf16[128,1024]{1,0:T(8,128)(2,1)S(1)}, bf16[128,1024]{1,0:T(8,128)(2,1)S(1)}, u32[]{:S(2)}, u32[]{:S(2)}) collective-permute-start(bf16[128,1024]{1,0:T(8,128)(2,1)S(1)} %get-tuple-element.32), channel_id=1, source_target_pairs={{0,127},{1,2},{2,1},{3,4},{4,3},{5,6},{6,5},{7,8},{8,7},{9,10},{10... | collective-permute-start | bytes 786440 | tf_op jit(solution)/shard_map/ppermute | solution.py:33

commit v3 on v2

--- a/solution.py
+++ b/solution.py
@@ -52,8 +52,8 @@
     g_sib,
     kv_own,
     kv_sib,
+    kv_a,
     kv_b,
-    kv_a,
     kv_c,
     dq_first,
     dq_rest,
@@ -420,8 +420,8 @@
         g_sib,
         kv,
         kv_sib,
+        kv_a,
         kv_b,
-        kv_a,
         kv_c,
     )
 

time: 45.8 us -> 44.9 us (0.980)
  waiting for transfers between devices: 19.1 us -> 16.3 us
  starting transfers between devices: 17.3 us -> 19.2 us
    ppermute x11, waiting for transfers between devices: 19.1 us -> 16.3 us  [send(): return lax.ppermute(array, 'ctx', pairs)]
    ppermute x11, starting transfers between devices: 17.3 us -> 19.2 us  [send(): return lax.ppermute(array, 'ctx', pairs)]
where the time goes in v3:
time: 44.9 us; the launch traced here: 44.7 us
  starting transfers between devices  19.2 us (43%)
  waiting for transfers between devices  16.3 us (36%)
  Pallas kernels  8.56 us (19%)
  between operations  0.69 us (2%)
    ppermute x11, starting transfers between devices, send(): return lax.ppermute(array, 'ctx', pairs)  19.2 us
    ppermute x11, waiting for transfers between devices, send(): return lax.ppermute(array, 'ctx', pairs)  16.3 us
    pallas_call x1, Pallas kernels, shards(): pl.pallas_call(attention_kernel, out_shape=(bf16((ROWS, WIDE)), bf16((2,...  4.73 us
    pallas_call x1, Pallas kernels, shards(): pl.pallas_call(early_kernel, out_shape=(bf16((2 * ROWS, WIDE)), jax.Shape...  1.58 us
    pallas_call x1, Pallas kernels, shards(): pl.pallas_call(pack_kernel, out_shape=(bf16((2 * ROWS, 2 * KV)), bf16((RO...  1.47 us
  transfers between devices with their start and end apart: 11, of which 5 were waited for; matrix products, arithmetic and copies ran while one was open for 0% of the time, Pallas kernels for 7%

profile of v3, /device:TPU:16, one launch (start us, length us, event | category | flops | bytes accessed | tf_op | source)
XLA Modules:
  0.0 44.7 jit_solution(8809284161570363677)
XLA Ops:
  0.6 0.1 collective-permute-start
  0.7 0.5 %collective-permute-start.1 = (bf16[128,2048]{1,0:T(8,128)(2,1)}, bf16[128,2048]{1,0:T(8,128)(2,1)S(1)}, u32[]{:S(2)}, u32[]{:S(2)}) collective-permute-start(bf16[128,2048]{1,0:T(8,128)(2,1)} %grads.1), channel_id=1, source_target_pairs={{0,1},{1,0},{2,3},{3,2},{4,5},{5,4},{6,7},{7,6},{8,9},{9,8},{10,11... | collective-permute-start | bytes 1572872 | tf_op jit(solution)/shard_map/ppermute | solution.py:33
  1.2 1.5 %prepare.1 = (bf16[128,1024]{1,0:T(8,128)(2,1)S(1)}, bf16[64,1024]{1,0:T(8,128)(2,1)S(1)}, bf16[128,2048]{1,0:T(8,128)(2,1)S(1)}, bf16[128,2048]{1,0:T(8,128)(2,1)S(1)}, s32[4,256]{1,0:T(4,128)S(1)}) custom-call(s32[1]{0:T(128)} %bitcast.place, s32[256]{0:T(256)} %slots.3, s32[342]{0:T(512)} %docs_hbm.1, bf16[128,512]{1,0:T(8,128)(2,1)} %keys.1, ...), custom_call_target="tpu_custom_call" | custom-call | tf_op jit(solution)/shard_map/prepare/pallas_call | solution.py:355
  2.7 9.0 %collective-permute-start.5 = (bf16[64,1024]{1,0:T(8,128)(2,1)S(1)}, bf16[64,1024]{1,0:T(8,128)(2,1)S(1)}, u32[]{:S(2)}, u32[]{:S(2)}) collective-permute-start(bf16[64,1024]{1,0:T(8,128)(2,1)S(1)} %get-tuple-element.23), channel_id=1, source_target_pairs={{0,125},{1,4},{2,127},{3,6},{4,1},{5,8},{6,3},{7,10},{8,5},{9,12},... | collective-permute-start | bytes 393224 | tf_op jit(solution)/shard_map/ppermute | solution.py:33
  11.7 0.0 copy-start
  11.7 0.0 collective-permute-start.4
  11.7 1.0 %collective-permute-start.3 = (bf16[128,1024]{1,0:T(8,128)(2,1)S(1)}, bf16[128,1024]{1,0:T(8,128)(2,1)S(1)}, u32[]{:S(2)}, u32[]{:S(2)}) collective-permute-start(bf16[128,1024]{1,0:T(8,128)(2,1)S(1)} %get-tuple-element.22.kv_own), channel_id=1, source_target_pairs={{0,2},{1,127},{2,4},{3,1},{4,6},{5,3},{6,8},{7,5},{8,10},{9,7},{10... | collective-permute-start | bytes 786440 | tf_op jit(solution)/shard_map/ppermute | solution.py:33
  12.8 2.9 %collective-permute-done.5.kv_c = bf16[64,1024]{1,0:T(8,128)(2,1)S(1)} collective-permute-done((bf16[64,1024]{1,0:T(8,128)(2,1)S(1)}, bf16[64,1024]{1,0:T(8,128)(2,1)S(1)}, u32[]{:S(2)}, u32[]{:S(2)}) %collective-permute-start.5) | collective-permute-done | bytes 131104 | tf_op jit(solution)/shard_map/ppermute | solution.py:33
  15.6 2.2 %collective-permute-start.2 = (bf16[128,1024]{1,0:T(8,128)(2,1)S(1)}, bf16[128,1024]{1,0:T(8,128)(2,1)S(1)}, u32[]{:S(2)}, u32[]{:S(2)}) collective-permute-start(bf16[128,1024]{1,0:T(8,128)(2,1)S(1)} %get-tuple-element.22.kv_own), channel_id=1, source_target_pairs={{0,1},{1,0},{2,3},{3,2},{4,5},{5,4},{6,7},{7,6},{8,9},{9,8},{10,11... | collective-permute-start | bytes 786440 | tf_op jit(solution)/shard_map/ppermute | solution.py:33
  17.8 6.2 %collective-permute-done.4.kv_b = bf16[128,1024]{1,0:T(8,128)(2,1)S(1)} collective-permute-done((bf16[128,1024]{1,0:T(8,128)(2,1)S(1)}, bf16[128,1024]{1,0:T(8,128)(2,1)S(1)}, u32[]{:S(2)}, u32[]{:S(2)}) %collective-permute-start.4) | collective-permute-done | bytes 262176 | tf_op jit(solution)/shard_map/ppermute | solution.py:33
  24.0 0.6 %collective-permute-done.3.kv_a = bf16[128,1024]{1,0:T(8,128)(2,1)S(1)} collective-permute-done((bf16[128,1024]{1,0:T(8,128)(2,1)S(1)}, bf16[128,1024]{1,0:T(8,128)(2,1)S(1)}, u32[]{:S(2)}, u32[]{:S(2)}) %collective-permute-start.3) | collective-permute-done | bytes 262176 | tf_op jit(solution)/shard_map/ppermute | solution.py:33
  24.5 0.0 collective-permute-done.2.kv_sib
  24.5 0.0 collective-permute-done.q_sib
  24.6 0.0 collective-permute-done.1.g_sib
  24.6 0.0 copy-done
  24.6 4.7 %attention_items.1 = (bf16[64,2048]{1,0:T(8,128)(2,1)S(1)}, bf16[2,64,2048]{2,1,0:T(8,128)(2,1)S(1)}, f32[128,1024]{1,0:T(8,128)S(1)}, bf16[128,1024]{1,0:T(8,12...) custom-call(s32[1]{0:T(128)} %bitcast.place, s32[256]{0:T(256)} %slots.3, ...), custom_call_target="tpu_custom_call" | custom-call | tf_op jit(solution)/shard_map/attention_items/pallas_call | solution.py:389
  29.3 0.1 collective-permute-start.6
  29.4 0.1 collective-permute-start.7
  29.5 0.4 collective-permute-start.8
  29.9 2.9 %collective-permute-start.9 = (bf16[128,1024]{1,0:T(8,128)(2,1)S(1)}, bf16[128,1024]{1,0:T(8,128)(2,1)S(1)}, u32[]{:S(2)}, u32[]{:S(2)}) collective-permute-start(bf16[128,1024]{1,0:T(8,128)(2,1)S(1)} %get-tuple-element.31), channel_id=1, source_target_pairs={{0,126},{1,3},{2,0},{3,5},{4,2},{5,7},{6,4},{7,9},{8,6},{9,11},{10... | collective-permute-start | bytes 786440 | tf_op jit(solution)/shard_map/ppermute | solution.py:33
  32.8 2.9 %collective-permute-start.10 = (bf16[128,1024]{1,0:T(8,128)(2,1)S(1)}, bf16[128,1024]{1,0:T(8,128)(2,1)S(1)}, u32[]{:S(2)}, u32[]{:S(2)}) collective-permute-start(bf16[128,1024]{1,0:T(8,128)(2,1)S(1)} %get-tuple-element.32), channel_id=1, source_target_pairs={{0,127},{1,2},{2,1},{3,4},{4,3},{5,6},{6,5},{7,8},{8,7},{9,10},{10... | collective-permute-start | bytes 786440 | tf_op jit(solution)/shard_map/ppermute | solution.py:33
  35.7 3.4 %collective-permute-done.7.back_c = bf16[64,1024]{1,0:T(8,128)(2,1)S(1)} collective-permute-done((bf16[64,1024]{1,0:T(8,128)(2,1)S(1)}, bf16[64,1024]{1,0:T(8,128)(2,1)S(1)}, u32[]{:S(2)}, u32[]{:S(2)}) %collective-permute-start.7) | collective-permute-done | bytes 131104 | tf_op jit(solution)/shard_map/ppermute | solution.py:33
  39.1 0.0 collective-permute-done.6.theirs
  39.1 1.6 %query_gradient_rows.1 = (bf16[128,2048]{1,0:T(8,128)(2,1)}, f32[128,1024]{1,0:T(8,128)S(1)}) custom-call(s32[1]{0:T(128)} %bitcast.place, s32[256]{0:T(256)} %slots.3, s32[4,256]{1,0:T(4,128)S(1)} %bitcast.3, bf16[64,2048]{1,0:T(8,128)(2,1)S(1)} %get-tuple-element.24.first, bf16[2,64,2048]{2,1,0:T(8,128)(2,1)S(1)} %get-tuple-element.25.rest, ...), custom_call_target="tpu_custom_call" | custom-call | flops 68719476736 | bytes 4194304 | tf_op jit(solution)/shard_map/query_gradient_rows/pallas_call | solution.py:434
  40.7 0.0 collective-permute-done.8.sib
  40.7 0.0 collective-permute-done.9.back_a
  40.7 3.2 %collective-permute-done.10.back_b = bf16[128,1024]{1,0:T(8,128)(2,1)S(1)} collective-permute-done((bf16[128,1024]{1,0:T(8,128)(2,1)S(1)}, bf16[128,1024]{1,0:T(8,128)(2,1)S(1)}, u32[]{:S(2)}, u32[]{:S(2)}) %collective-permute-start.10) | collective-permute-done | bytes 262176 | tf_op jit(solution)/shard_map/ppermute | solution.py:33
  43.9 0.8 %key_value_gradient_sum.1 = (bf16[128,512]{1,0:T(8,128)(2,1)}, bf16[128,512]{1,0:T(8,128)(2,1)}) custom-call(f32[128,1024]{1,0:T(8,128)S(1)} %get-tuple-element.29.own, bf16[128,1024]{1,0:T(8,128)(2,1)S(1)} %collective-permute-done.8.sib, bf16[128,1024]{1,0:T(8,128)(2,1)S(1)} %collective-permute-done.9.back_a, ...), custom_call_target="tpu_custom_call" | custom-call | tf_op jit(solution)/shard_map/key_value_gradient_sum/pallas_call | solution.py:458
Async XLA Ops:
  0.6 23.9 %collective-permute-start = (bf16[128,2048]{1,0:T(8,128)(2,1)}, bf16[128,2048]{1,0:T(8,128)(2,1)S(1)}, u32[]{:S(2)}, u32[]{:S(2)}) collective-permute-start(bf16[128,2048]{1,0:T(8,128)(2,1)} %queries.1), channel_id=1, source_target_pairs={{0,1},{1,0},{2,3},{3,2},{4,5},{5,4},{6,7},{7,6},{8,9},{9,8},{10,11... | collective-permute-start | bytes 1572872 | tf_op jit(solution)/shard_map/ppermute | solution.py:33
  0.7 23.8 %collective-permute-start.1 = (bf16[128,2048]{1,0:T(8,128)(2,1)}, bf16[128,2048]{1,0:T(8,128)(2,1)S(1)}, u32[]{:S(2)}, u32[]{:S(2)}) collective-permute-start(bf16[128,2048]{1,0:T(8,128)(2,1)} %grads.1), channel_id=1, source_target_pairs={{0,1},{1,0},{2,3},{3,2},{4,5},{5,4},{6,7},{7,6},{8,9},{9,8},{10,11... | collective-permute-start | bytes 1572872 | tf_op jit(solution)/shard_map/ppermute | solution.py:33
  2.7 12.9 %collective-permute-start.5 = (bf16[64,1024]{1,0:T(8,128)(2,1)S(1)}, bf16[64,1024]{1,0:T(8,128)(2,1)S(1)}, u32[]{:S(2)}, u32[]{:S(2)}) collective-permute-start(bf16[64,1024]{1,0:T(8,128)(2,1)S(1)} %get-tuple-element.23), channel_id=1, source_target_pairs={{0,125},{1,4},{2,127},{3,6},{4,1},{5,8},{6,3},{7,10},{8,5},{9,12},... | collective-permute-start | bytes 393224 | tf_op jit(solution)/shard_map/ppermute | solution.py:33
  11.7 12.8 %copy-start = (s32[256,4]{0,1:T(4,128)S(1)}, s32[256,4]{0,1:T(4,128)}, u32[]{:S(2)}) copy-start(s32[256,4]{0,1:T(4,128)} %param.13) | copy-start | bytes 12292
  11.7 12.3 %collective-permute-start.4 = (bf16[128,1024]{1,0:T(8,128)(2,1)S(1)}, bf16[128,1024]{1,0:T(8,128)(2,1)S(1)}, u32[]{:S(2)}, u32[]{:S(2)}) collective-permute-start(bf16[128,1024]{1,0:T(8,128)(2,1)S(1)} %get-tuple-element.22.kv_own), channel_id=1, source_target_pairs={{0,127},{1,2},{2,1},{3,4},{4,3},{5,6},{6,5},{7,8},{8,7},{9,10},{10... | collective-permute-start | bytes 786440 | tf_op jit(solution)/shard_map/ppermute | solution.py:33
  11.7 12.8 %collective-permute-start.3 = (bf16[128,1024]{1,0:T(8,128)(2,1)S(1)}, bf16[128,1024]{1,0:T(8,128)(2,1)S(1)}, u32[]{:S(2)}, u32[]{:S(2)}) collective-permute-start(bf16[128,1024]{1,0:T(8,128)(2,1)S(1)} %get-tuple-element.22.kv_own), channel_id=1, source_target_pairs={{0,2},{1,127},{2,4},{3,1},{4,6},{5,3},{6,8},{7,5},{8,10},{9,7},{10... | collective-permute-start | bytes 786440 | tf_op jit(solution)/shard_map/ppermute | solution.py:33
  15.6 8.9 %collective-permute-start.2 = (bf16[128,1024]{1,0:T(8,128)(2,1)S(1)}, bf16[128,1024]{1,0:T(8,128)(2,1)S(1)}, u32[]{:S(2)}, u32[]{:S(2)}) collective-permute-start(bf16[128,1024]{1,0:T(8,128)(2,1)S(1)} %get-tuple-element.22.kv_own), channel_id=1, source_target_pairs={{0,1},{1,0},{2,3},{3,2},{4,5},{5,4},{6,7},{7,6},{8,9},{9,8},{10,11... | collective-permute-start | bytes 786440 | tf_op jit(solution)/shard_map/ppermute | solution.py:33
  29.3 9.8 %collective-permute-start.6 = (bf16[2,64,2048]{2,1,0:T(8,128)(2,1)S(1)}, bf16[2,64,2048]{2,1,0:T(8,128)(2,1)S(1)}, u32[]{:S(2)}, u32[]{:S(2)}) collective-permute-start(bf16[2,64,2048]{2,1,0:T(8,128)(2,1)S(1)} %get-tuple-element.25.rest), channel_id=1, source_target_pairs={{0,1},{1,0},{2,3},{3,2},{4,5},{5,4},{6,7},{7,6},{8,9},{9,8},{10,11... | collective-permute-start | bytes 1572872 | tf_op jit(solution)/shard_map/ppermute | solution.py:33
  29.4 9.7 %collective-permute-start.7 = (bf16[64,1024]{1,0:T(8,128)(2,1)S(1)}, bf16[64,1024]{1,0:T(8,128)(2,1)S(1)}, u32[]{:S(2)}, u32[]{:S(2)}) collective-permute-start(bf16[64,1024]{1,0:T(8,128)(2,1)S(1)} %get-tuple-element.27), channel_id=1, source_target_pairs={{0,125},{1,4},{2,127},{3,6},{4,1},{5,8},{6,3},{7,10},{8,5},{9,12},... | collective-permute-start | bytes 393224 | tf_op jit(solution)/shard_map/ppermute | solution.py:33
  29.5 11.2 %collective-permute-start.8 = (bf16[128,1024]{1,0:T(8,128)(2,1)S(1)}, bf16[128,1024]{1,0:T(8,128)(2,1)S(1)}, u32[]{:S(2)}, u32[]{:S(2)}) collective-permute-start(bf16[128,1024]{1,0:T(8,128)(2,1)S(1)} %get-tuple-element.30), channel_id=1, source_target_pairs={{0,1},{1,0},{2,3},{3,2},{4,5},{5,4},{6,7},{7,6},{8,9},{9,8},{10,11... | collective-permute-start | bytes 786440 | tf_op jit(solution)/shard_map/ppermute | solution.py:33
  29.9 10.8 %collective-permute-start.9 = (bf16[128,1024]{1,0:T(8,128)(2,1)S(1)}, bf16[128,1024]{1,0:T(8,128)(2,1)S(1)}, u32[]{:S(2)}, u32[]{:S(2)}) collective-permute-start(bf16[128,1024]{1,0:T(8,128)(2,1)S(1)} %get-tuple-element.31), channel_id=1, source_target_pairs={{0,126},{1,3},{2,0},{3,5},{4,2},{5,7},{6,4},{7,9},{8,6},{9,11},{10... | collective-permute-start | bytes 786440 | tf_op jit(solution)/shard_map/ppermute | solution.py:33
  32.8 11.1 %collective-permute-start.10 = (bf16[128,1024]{1,0:T(8,128)(2,1)S(1)}, bf16[128,1024]{1,0:T(8,128)(2,1)S(1)}, u32[]{:S(2)}, u32[]{:S(2)}) collective-permute-start(bf16[128,1024]{1,0:T(8,128)(2,1)S(1)} %get-tuple-element.32), channel_id=1, source_target_pairs={{0,127},{1,2},{2,1},{3,4},{4,3},{5,6},{6,5},{7,8},{8,7},{9,10},{10... | collective-permute-start | bytes 786440 | tf_op jit(solution)/shard_map/ppermute | solution.py:33

commit v4 on v3

--- a/solution.py
+++ b/solution.py
@@ -21,10 +21,10 @@
 EXP2_SCALE = SCALE * math.log2(math.e)
 MASKED = -1e30
 FAR = 1 << 30
-ENTRIES = 9
+ENTRIES = 7
 VMEM_LIMIT = 24 * 1024 * 1024
 
-TABLE_A, TABLE_B, TABLE_C = 4, 6, 8
+TABLE_A, TABLE_B, TABLE_C = 4, 5, 6
 
 
 def send(array, even_by, odd_by):
@@ -42,6 +42,7 @@
 
 
 def attention_kernel(
+    leading,
     place,
     slots,
     live,
@@ -54,21 +55,15 @@
     kv_sib,
     kv_a,
     kv_b,
-    kv_c,
-    dq_first,
-    dq_rest,
-    out_own,
-    out_sib,
-    out_a,
-    out_b,
-    out_c,
-    table,
-    total,
-    q_work,
-    g_work,
-    dq,
-    bias,
+    *refs,
 ):
+    if leading:
+        dq_rest, total, table, q_work, g_work, bias = refs
+        dq = dq_rest
+    else:
+        kv_c, total_in, dq_first, out_own, out_sib, out_a, out_b, out_c = refs[:8]
+        total, table, q_work, g_work, bias = refs[8:]
+        dq = dq_first
     me = place[0]
     count = slots.shape[0] // 2
     parity = lax.rem(me, 2)
@@ -82,57 +77,60 @@
     table[pl.ds(sib_at, 128), :] = kv_sib[...]
     table[TABLE_A * ROWS : TABLE_B * ROWS, :] = kv_a[...]
     table[TABLE_B * ROWS : TABLE_C * ROWS, :] = kv_b[...]
-    table[TABLE_C * ROWS :, :] = kv_c[...]
-    total[...] = jnp.zeros_like(total)
 
     toward = jnp.where(is_odd, 1, -1)
     near_a = lax.rem(me + 2 * toward + count, count)
     near_b = lax.rem(me + toward + count, count)
     far = lax.rem(me + 3 * toward + count, count)
+    passed_odd = jnp.logical_and(is_odd, slots[2 * near_a] == count - 1)
+    passed_even = jnp.logical_and(is_odd, slots[2 * near_b] == count - 1)
     entry_ids = [slots[chip_base + e] for e in range(4)]
-    entry_ids += [slots[2 * near_a], slots[2 * near_a + 1]]
-    entry_ids += [slots[2 * near_b], slots[2 * near_b + 1]]
-    entry_ids += [slots[2 * far + parity]]
+    entry_ids += [jnp.where(passed_even, count - 1, slots[2 * near_a + parity])]
+    entry_ids += [slots[2 * near_b + parity]]
+    if not leading:
+        table[TABLE_C * ROWS :, :] = kv_c[...]
+        entry_ids += [jnp.where(passed_odd, count - 1, slots[2 * far + parity])]
 
     own_row = pl.multiple_of(parity * ROWS, ROWS)
     other_row = pl.multiple_of((1 - parity) * ROWS, ROWS)
-    q_work[0] = q_own[pl.ds(own_row, ROWS), :]
-    g_work[0] = g_own[pl.ds(own_row, ROWS), :]
-
-    @pl.when(middle_even)
-    def _():
-        q_work[1] = q_own[pl.ds(other_row, ROWS), :]
-        g_work[1] = g_own[pl.ds(other_row, ROWS), :]
-
-    @pl.when(jnp.logical_not(middle_even))
-    def _():
-        q_work[1] = q_sib[pl.ds(own_row, ROWS), :]
-        g_work[1] = g_sib[pl.ds(own_row, ROWS), :]
-
-    @pl.when(far_middle)
-    def _():
-        q_work[2] = q_sib[ROWS:, :]
-        g_work[2] = g_sib[ROWS:, :]
-
-    first = jnp.where(jnp.logical_and(far_middle, is_odd), 1, 0)
-    last = jnp.where(jnp.logical_and(far_middle, jnp.logical_not(is_odd)), 3, 2)
-
-    own_entry = 3 * parity
-    other_entry = jnp.where(middle_even, 1 + parity, jnp.where(is_odd, 1, 2))
+    if leading:
+        total[...] = jnp.zeros_like(total)
+
+        @pl.when(middle_even)
+        def _():
+            q_work[0] = q_own[pl.ds(other_row, ROWS), :]
+            g_work[0] = g_own[pl.ds(other_row, ROWS), :]
+
+        @pl.when(jnp.logical_not(middle_even))
+        def _():
+            q_work[0] = q_sib[pl.ds(own_row, ROWS), :]
+            g_work[0] = g_sib[pl.ds(own_row, ROWS), :]
+
+        @pl.when(far_middle)
+        def _():
+            q_work[1] = q_sib[ROWS:, :]
+            g_work[1] = g_sib[ROWS:, :]
+
+        first = 0
+        last = jnp.where(jnp.logical_and(far_middle, jnp.logical_not(is_odd)), 2, 1)
+        other_entry = jnp.where(middle_even, 1 + parity, jnp.where(is_odd, 1, 2))
+    else:
+        q_work[0] = q_own[pl.ds(own_row, ROWS), :]
+        g_work[0] = g_own[pl.ds(own_row, ROWS), :]
+        first = 0
+        last = jnp.where(jnp.logical_and(far_middle, is_odd), 0, 1)
 
     def work_item(item, carry):
-        entry = jnp.where(item == 0, own_entry, jnp.where(item == 1, other_entry, 3))
+        entry = jnp.where(item == 0, other_entry, 3) if leading else 3 * parity
         query_id = slots[chip_base + entry]
         indices = []
         key_base = []
         for distance in range(REACH + 1):
             key_id = query_id - distance
-            is_live = jnp.logical_and(
-                key_id >= 0, live[distance, query_id] == 1
-            )
+            is_live = jnp.logical_and(key_id >= 0, live[distance, query_id] == 1)
             index = jnp.int32(0)
             found = jnp.bool_(False)
-            for e in range(ENTRIES):
+            for e in range(len(entry_ids)):
                 match = entry_ids[e] == key_id
                 index = jnp.where(match, e, index)
                 found = jnp.logical_or(found, match)
@@ -191,15 +189,31 @@
                 total[at, vcols] += value_add[part]
         return carry
 
+    if not leading:
+        total[...] = total_in[...]
     lax.fori_loop(first, last, work_item, 0)
-
-    dq_first[...] = dq[0]
-    dq_rest[...] = dq[1:]
+    if leading:
+        return
+    low = jnp.bfloat16
     out_own[...] = total[pl.ds(own_at, 128), :]
-    out_sib[...] = total[pl.ds(sib_at, 128), :].astype(jnp.bfloat16)
-    out_a[...] = total[TABLE_A * ROWS : TABLE_B * ROWS, :].astype(jnp.bfloat16)
-    out_b[...] = total[TABLE_B * ROWS : TABLE_C * ROWS, :].astype(jnp.bfloat16)
-    out_c[...] = total[TABLE_C * ROWS :, :].astype(jnp.bfloat16)
+    out_sib[...] = total[pl.ds(sib_at, 128), :].astype(low)
+    nothing = jnp.zeros((ROWS, 2 * KV), low)
+    passed = slice(TABLE_C * ROWS, ENTRIES * ROWS)
+    out_a[pl.ds(own_row, ROWS), :] = total[TABLE_A * ROWS : TABLE_B * ROWS, :].astype(low)
+    out_b[pl.ds(own_row, ROWS), :] = total[TABLE_B * ROWS : TABLE_C * ROWS, :].astype(low)
+    out_a[pl.ds(other_row, ROWS), :] = nothing
+    out_b[pl.ds(other_row, ROWS), :] = nothing
+    out_c[...] = total[passed, :].astype(low)
+
+    @pl.when(passed_odd)
+    def _():
+        out_a[pl.ds(other_row, ROWS), :] = total[passed, :].astype(low)
+        out_c[...] = nothing
+
+    @pl.when(passed_even)
+    def _():
+        out_b[pl.ds(other_row, ROWS), :] = out_a[pl.ds(own_row, ROWS), :]
+        out_a[pl.ds(own_row, ROWS), :] = nothing
 
 
 def pack_kernel(
@@ -211,7 +225,8 @@
     queries,
     grads,
     both,
-    far,
+    chain,
+    cross,
     q_own,
     g_own,
     row_start,
@@ -220,15 +235,18 @@
     sems,
 ):
     parity = lax.rem(place[0], 2)
-    at = pl.ds(pl.multiple_of((1 - parity) * ROWS, ROWS), ROWS)
+    own_rows = pl.ds(pl.multiple_of(parity * ROWS, ROWS), ROWS)
+    other_rows = pl.ds(pl.multiple_of((1 - parity) * ROWS, ROWS), ROWS)
     copies = [
         pltpu.make_async_copy(source, target, sems.at[n])
         for n, (source, target) in enumerate(
             [
                 (slots_hbm, slots),
                 (docs_hbm, docs),
-                (keys.at[at, :], far.at[:, pl.ds(0, KV)]),
-                (values.at[at, :], far.at[:, pl.ds(KV, KV)]),
+                (keys.at[other_rows, :], cross.at[:, pl.ds(0, KV)]),
+                (values.at[other_rows, :], cross.at[:, pl.ds(KV, KV)]),
+                (keys.at[own_rows, :], chain.at[:, pl.ds(0, KV)]),
+                (values.at[own_rows, :], chain.at[:, pl.ds(KV, KV)]),
                 (keys, both.at[:, pl.ds(0, KV)]),
                 (values, both.at[:, pl.ds(KV, KV)]),
                 (queries, q_own),
@@ -292,7 +310,7 @@
 
     @pl.when(jnp.logical_not(moved))
     def _():
-        out[pl.ds(own_row, ROWS), :] = first[...]
+        out[pl.ds(own_row, ROWS), :] = first[0]
 
     @pl.when(middle_even)
     def _():
@@ -352,21 +370,22 @@
     params = pltpu.CompilerParams(vmem_limit_bytes=VMEM_LIMIT)
 
     bf16 = functools.partial(jax.ShapeDtypeStruct, dtype=jnp.bfloat16)
-    kv, kv_far, q_own, g_own, row_start = pl.pallas_call(
+    kv, kv_chain, kv_cross, q_own, g_own, row_start = pl.pallas_call(
         pack_kernel,
         out_shape=(
             bf16((2 * ROWS, 2 * KV)),
+            bf16((ROWS, 2 * KV)),
             bf16((ROWS, 2 * KV)),
             bf16((2 * ROWS, WIDE)),
             bf16((2 * ROWS, WIDE)),
             jax.ShapeDtypeStruct((4, GROUP * ROWS), jnp.int32),
         ),
         in_specs=smem(1) + hbm(6),
-        out_specs=tuple(vmem(5)),
+        out_specs=tuple(vmem(6)),
         scratch_shapes=[
             pltpu.SMEM(slot_to_block.shape, jnp.int32),
             pltpu.SMEM(doc_starts.shape, jnp.int32),
-            pltpu.SemaphoreType.DMA((8,)),
+            pltpu.SemaphoreType.DMA((10,)),
         ],
         compiler_params=params,
         name="prepare",
@@ -379,37 +398,26 @@
         in_hbm(queries),
         in_hbm(output_gradient),
     )
-    kv_c = send(kv_far, -3, 3)
-    kv_a = send(kv, 2, -2)
-    kv_b = send(kv, -1, 1)
     kv_sib = send(kv, 1, -1)
+    kv_b = send(kv_cross, -1, 1)
     q_sib = send(queries, 1, -1)
     g_sib = send(output_gradient, 1, -1)
-
-    dq_first, dq_rest, own, sib, out_a, out_b, out_c = pl.pallas_call(
-        attention_kernel,
-        out_shape=(
-            bf16((ROWS, WIDE)),
-            bf16((2, ROWS, WIDE)),
-            jax.ShapeDtypeStruct((2 * ROWS, 2 * KV), jnp.float32),
-            bf16((2 * ROWS, 2 * KV)),
-            bf16((2 * ROWS, 2 * KV)),
-            bf16((2 * ROWS, 2 * KV)),
-            bf16((ROWS, 2 * KV)),
-        ),
-        in_specs=smem(3) + vmem(10),
-        out_specs=tuple(vmem(7)),
-        scratch_shapes=[
-            pltpu.VMEM((ENTRIES * ROWS, 2 * KV), jnp.bfloat16),
-            pltpu.VMEM((ENTRIES * ROWS, 2 * KV), jnp.float32),
-            pltpu.VMEM((3, ROWS, WIDE), jnp.bfloat16),
-            pltpu.VMEM((3, ROWS, WIDE), jnp.bfloat16),
-            pltpu.VMEM((3, ROWS, WIDE), jnp.bfloat16),
-            pltpu.VMEM((SPAN, GROUP * ROWS), jnp.float32),
-        ],
-        compiler_params=params,
-        name="attention_items",
-    )(
+    chip_ids = lax.dynamic_slice_in_dim(slot_to_block, 2 * (me - me % 2), 4, 0)
+    middle = slot_to_block.shape[0] // 2 - 1
+    is_odd = me % 2 == 1
+    swapped = jnp.logical_and(is_odd, chip_ids[0] == middle)
+    kv_a = send(jnp.where(swapped, kv_sib[:ROWS], kv_chain), 2, -2)
+    holds = jnp.logical_and(is_odd, chip_ids[2] == middle)
+    kv_c = send(jnp.where(holds, kv[:ROWS], kv_b), 2, -2)
+
+    work = [
+        pltpu.VMEM((ENTRIES * ROWS, 2 * KV), jnp.bfloat16),
+        pltpu.VMEM((2, ROWS, WIDE), jnp.bfloat16),
+        pltpu.VMEM((2, ROWS, WIDE), jnp.bfloat16),
+        pltpu.VMEM((SPAN, GROUP * ROWS), jnp.float32),
+    ]
+    sums = jax.ShapeDtypeStruct((ENTRIES * ROWS, 2 * KV), jnp.float32)
+    operands = (
         place,
         in_hbm(slot_to_block),
         live,
@@ -422,13 +430,41 @@
         kv_sib,
         kv_a,
         kv_b,
-        kv_c,
     )
+    dq_rest, total = pl.pallas_call(
+        functools.partial(attention_kernel, True),
+        out_shape=(bf16((2, ROWS, WIDE)), sums),
+        in_specs=smem(3) + vmem(9),
+        out_specs=tuple(vmem(2)),
+        scratch_shapes=work,
+        compiler_params=params,
+        cost_estimate=pl.CostEstimate(
+            flops=1 << 36, bytes_accessed=1 << 22, transcendentals=1 << 18
+        ),
+        name="attention_leading",
+    )(*operands)
+    dq_first, own, sib, out_a, out_b, out_c = pl.pallas_call(
+        functools.partial(attention_kernel, False),
+        out_shape=(
+            bf16((1, ROWS, WIDE)),
+            jax.ShapeDtypeStruct((2 * ROWS, 2 * KV), jnp.float32),
+            bf16((2 * ROWS, 2 * KV)),
+            bf16((2 * ROWS, 2 * KV)),
+            bf16((2 * ROWS, 2 * KV)),
+            bf16((ROWS, 2 * KV)),
+        ),
+        in_specs=smem(3) + vmem(11),
+        out_specs=tuple(vmem(6)),
+        scratch_shapes=[pltpu.VMEM(sums.shape, jnp.float32)] + work,
+        compiler_params=params,
+        name="attention_last",
+    )(*operands, kv_c, total)
 
     back_c = send(out_c, -3, 3)
     back_a = send(out_a, -2, 2)
     back_b = send(out_b, -1, 1)
     back_sib = send(sib, 1, -1)
+    dq_rest, _ = lax.optimization_barrier((dq_rest, out_c))
     dq_sib = send(dq_rest, 1, -1)
 
     query_grad, own = pl.pallas_call(

time: 44.9 us -> 44.8 us (level)
  starting transfers between devices: 19.2 us -> 16 us
  between operations: 0.69 us -> 2.06 us
  local copies, waits for them, and re-layouts: 0.01 us -> 1.34 us
  Pallas kernels: 8.56 us -> 9.43 us
  waiting for transfers between devices: 16.3 us -> 15.7 us
    ppermute x11, starting transfers between devices: 19.2 us -> 16 us  [send(): return lax.ppermute(array, 'ctx', pairs)]
    pallas_call x1 -> x2, Pallas kernels: 4.73 us -> 5.51 us  [the longest x1 2.82 us: shards(): pl.pallas_call(functools.partial(attention_kernel, False), out_shape=(bf1...]
    dynamic_slice x0 -> x1, local copies, waits for them, and re-layouts: none -> 0.75 us  [shards(): chip_ids = lax.dynamic_slice_in_dim(slot_to_block, 2 * (me - me % 2), 4, 0)]
    slice x0 -> x1, local copies, waits for them, and re-layouts: none -> 0.58 us  [shards(): holds = jnp.logical_and(is_odd, chip_ids[2] == middle)]
    ppermute x11, waiting for transfers between devices: 16.3 us -> 15.7 us  [send(): return lax.ppermute(array, 'ctx', pairs)]
  transfers between devices with their start and end apart: 11 -> 11, of which waited for: 5 -> 3; matrix products, arithmetic and copies ran while one was open for 0% -> 3% of each run, Pallas kernels for 7% -> 10%
where the time goes in v4:
time: 44.8 us; the launch traced here: 44.6 us
  starting transfers between devices  16 us (36%)
  waiting for transfers between devices  15.7 us (35%)
  Pallas kernels  9.43 us (21%)
  between operations  2.06 us (5%)
  local copies, waits for them, and re-layouts  1.34 us (3%)
    ppermute x11, starting transfers between devices, send(): return lax.ppermute(array, 'ctx', pairs)  16 us
    ppermute x11, waiting for transfers between devices, send(): return lax.ppermute(array, 'ctx', pairs)  15.7 us
    pallas_call x1, Pallas kernels, shards(): pl.pallas_call(functools.partial(attention_kernel, False), out_shape=(bf1...  2.82 us
    pallas_call x1, Pallas kernels, shards(): pl.pallas_call(functools.partial(attention_kernel, True), out_shape=(bf16...  2.69 us
    pallas_call x1, Pallas kernels, shards(): pl.pallas_call(early_kernel, out_shape=(bf16((2 * ROWS, WIDE)), jax.Shape...  1.58 us
    pallas_call x1, Pallas kernels, shards(): pl.pallas_call(pack_kernel, out_shape=(bf16((2 * ROWS, 2 * KV)), bf16((RO...  1.57 us
  transfers between devices with their start and end apart: 11, of which 3 were waited for; matrix products, arithmetic and copies ran while one was open for 3% of the time, Pallas kernels for 10%

profile of v4, /device:TPU:16, one launch (start us, length us, event | category | flops | bytes accessed | tf_op | source)
XLA Modules:
  0.0 44.6 jit_solution(14342793733998372251)
XLA Ops:
  0.6 0.0 copy-start
  0.6 1.6 %prepare.1 = (bf16[128,1024]{1,0:T(8,128)(2,1)S(1)}, bf16[64,1024]{1,0:T(8,128)(2,1)S(1)}, bf16[64,1024]{1,0:T(8,128)(2,1)S(1)}, bf16[128,2048]{1,0:T(8,128)(2,1...) custom-call(s32[1]{0:T(128)} %bitcast.place, s32[256]{0:T(256)} %slots.5, s32[342]{0:T(512)} %docs_hbm.1, ...), custom_call_target="tpu_custom_call" | custom-call | tf_op jit(solution)/shard_map/prepare/pallas_call | solution.py:373
  2.2 0.1 collective-permute-start.2
  2.3 0.5 %collective-permute-start = (bf16[128,2048]{1,0:T(8,128)(2,1)}, bf16[128,2048]{1,0:T(8,128)(2,1)S(1)}, u32[]{:S(2)}, u32[]{:S(2)}) collective-permute-start(bf16[128,2048]{1,0:T(8,128)(2,1)} %queries.1), channel_id=1, source_target_pairs={{0,1},{1,0},{2,3},{3,2},{4,5},{5,4},{6,7},{7,6},{8,9},{9,8},{10,11... | collective-permute-start | bytes 1572872 | tf_op jit(solution)/shard_map/ppermute | solution.py:33
  2.8 0.1 collective-permute-start.1
  2.9 8.8 %collective-permute-start.4 = (bf16[64,1024]{1,0:T(8,128)(2,1)S(1)}, bf16[64,1024]{1,0:T(8,128)(2,1)S(1)}, u32[]{:S(2)}, u32[]{:S(2)}) collective-permute-start(bf16[64,1024]{1,0:T(8,128)(2,1)S(1)} %get-tuple-element.27), channel_id=1, source_target_pairs={{0,127},{1,2},{2,1},{3,4},{4,3},{5,6},{6,5},{7,8},{8,7},{9,10},{10... | collective-permute-start | bytes 393224 | tf_op jit(solution)/shard_map/ppermute | solution.py:33
  11.7 0.8 %dynamic_slice.3 = s32[4]{0:T(128)S(1)} dynamic-slice(s32[256]{0:T(256)} %slots.5, s32[]{:T(128)S(6)} %select_n.27), dynamic_slice_sizes={4} | dynamic-slice | bytes 36 | tf_op jit(solution)/shard_map/dynamic_slice | solution.py:405
  12.5 0.6 %fusion = (s32[1]{0:T(128)}, s32[1]{0:T(128)}) fusion(s32[4]{0:T(128)S(1)} %dynamic_slice.3), kind=kLoop, calls=%fused_computation.2 | loop fusion | bytes 16 | tf_op jit(solution)/shard_map/slice | solution.py:410
  14.3 0.0 collective-permute-done.2.kv_sib
  14.4 0.1 collective-permute-start.3
  14.5 0.0 collective-permute-done.4.kv_b
  14.5 0.1 collective-permute-start.5
  14.6 9.0 %collective-permute-done.3.kv_a = bf16[64,1024]{1,0:T(8,128)(2,1)S(1)} collective-permute-done((bf16[64,1024]{1,0:T(8,128)(2,1)S(1)}, bf16[64,1024]{1,0:T(8,128)(2,1)S(1)}, u32[]{:S(2)}, u32[]{:S(2)}) %collective-permute-start.3) | collective-permute-done | bytes 131104 | tf_op jit(solution)/shard_map/ppermute | solution.py:33
  23.6 0.0 collective-permute-done.q_sib
  23.7 0.0 collective-permute-done.1.g_sib
  23.7 0.0 copy-done
  23.7 2.7 %attention_leading.1 = (bf16[2,64,2048]{2,1,0:T(8,128)(2,1)S(1)}, f32[448,1024]{1,0:T(8,128)S(1)}) custom-call(s32[1]{0:T(128)} %bitcast.place, s32[256]{0:T(256)} %slots.5, s32[4,256]{1,0:T(4,128)S(1)} %bitcast.4, s32[4,256]{1,0:T(4,128)S(1)} %get-tuple-element.22.row_start, bf16[128,2048]{1,0:T(8,128)(2,1)S(1)} %get-tuple-element.23.q_own, ...), custom_call_target="tpu_custom_call" | custom-call | flops 68719476736 | bytes 4194304 | tf_op jit(solution)/shard_map/attention_leading/pallas_call | solution.py:434
  26.4 0.0 collective-permute-done.5.refs_0_
  26.4 2.8 %attention_last.1 = (bf16[1,64,2048]{2,1,0:T(8,128)(2,1)S(1)}, f32[128,1024]{1,0:T(8,128)S(1)}, bf16[128,1024]{1,0:T(8,128)(2,1)S(1)}, bf16[128,1024]{1,0:T(8,12...) custom-call(s32[1]{0:T(128)} %bitcast.place, s32[256]{0:T(256)} %slots.5, s32[4,256]{1,0:T(4,128)S(1)} %bitcast.5, ...), custom_call_target="tpu_custom_call" | custom-call | tf_op jit(solution)/shard_map/attention_last/pallas_call | solution.py:446
  29.2 0.1 collective-permute-start.6
  29.3 0.1 collective-permute-start.7
  29.4 0.4 collective-permute-start.8
  29.8 2.2 %collective-permute-start.9 = (bf16[128,1024]{1,0:T(8,128)(2,1)S(1)}, bf16[128,1024]{1,0:T(8,128)(2,1)S(1)}, u32[]{:S(2)}, u32[]{:S(2)}) collective-permute-start(bf16[128,1024]{1,0:T(8,128)(2,1)S(1)} %get-tuple-element.37), channel_id=1, source_target_pairs={{0,126},{1,3},{2,0},{3,5},{4,2},{5,7},{6,4},{7,9},{8,6},{9,11},{10... | collective-permute-start | bytes 786440 | tf_op jit(solution)/shard_map/ppermute | solution.py:33
  31.9 3.6 %collective-permute-start.10 = (bf16[128,1024]{1,0:T(8,128)(2,1)S(1)}, bf16[128,1024]{1,0:T(8,128)(2,1)S(1)}, u32[]{:S(2)}, u32[]{:S(2)}) collective-permute-start(bf16[128,1024]{1,0:T(8,128)(2,1)S(1)} %get-tuple-element.38), channel_id=1, source_target_pairs={{0,127},{1,2},{2,1},{3,4},{4,3},{5,6},{6,5},{7,8},{8,7},{9,10},{10... | collective-permute-start | bytes 786440 | tf_op jit(solution)/shard_map/ppermute | solution.py:33
  35.6 3.4 %collective-permute-done.7.back_c = bf16[64,1024]{1,0:T(8,128)(2,1)S(1)} collective-permute-done((bf16[64,1024]{1,0:T(8,128)(2,1)S(1)}, bf16[64,1024]{1,0:T(8,128)(2,1)S(1)}, u32[]{:S(2)}, u32[]{:S(2)}) %collective-permute-start.7) | collective-permute-done | bytes 131104 | tf_op jit(solution)/shard_map/ppermute | solution.py:33
  39.0 0.0 collective-permute-done.6.theirs
  39.0 1.6 %query_gradient_rows.1 = (bf16[128,2048]{1,0:T(8,128)(2,1)}, f32[128,1024]{1,0:T(8,128)S(1)}) custom-call(s32[1]{0:T(128)} %bitcast.place, s32[256]{0:T(256)} %slots.5, s32[4,256]{1,0:T(4,128)S(1)} %bitcast.6, bf16[1,64,2048]{2,1,0:T(8,128)(2,1)S(1)} %get-tuple-element.29.first, bf16[2,64,2048]{2,1,0:T(8,128)(2,1)S(1)} %get-tuple-element.32.rest, ...), custom_call_target="tpu_custom_call" | custom-call | flops 68719476736 | bytes 4194304 | tf_op jit(solution)/shard_map/query_gradient_rows/pallas_call | solution.py:470
  40.6 0.0 collective-permute-done.8.sib
  40.6 0.0 collective-permute-done.9.back_a
  40.6 3.2 %collective-permute-done.10.back_b = bf16[128,1024]{1,0:T(8,128)(2,1)S(1)} collective-permute-done((bf16[128,1024]{1,0:T(8,128)(2,1)S(1)}, bf16[128,1024]{1,0:T(8,128)(2,1)S(1)}, u32[]{:S(2)}, u32[]{:S(2)}) %collective-permute-start.10) | collective-permute-done | bytes 262176 | tf_op jit(solution)/shard_map/ppermute | solution.py:33
  43.8 0.8 %key_value_gradient_sum.1 = (bf16[128,512]{1,0:T(8,128)(2,1)}, bf16[128,512]{1,0:T(8,128)(2,1)}) custom-call(f32[128,1024]{1,0:T(8,128)S(1)} %get-tuple-element.35.own, bf16[128,1024]{1,0:T(8,128)(2,1)S(1)} %collective-permute-done.8.sib, bf16[128,1024]{1,0:T(8,128)(2,1)S(1)} %collective-permute-done.9.back_a, ...), custom_call_target="tpu_custom_call" | custom-call | tf_op jit(solution)/shard_map/key_value_gradient_sum/pallas_call | solution.py:494
  (2 shorter events, 0.0 us)
Async XLA Ops:
  0.6 23.0 %copy-start = (s32[256,4]{0,1:T(4,128)S(1)}, s32[256,4]{0,1:T(4,128)}, u32[]{:S(2)}) copy-start(s32[256,4]{0,1:T(4,128)} %param.13) | copy-start | bytes 12292
  2.2 12.1 %collective-permute-start.2 = (bf16[128,1024]{1,0:T(8,128)(2,1)S(1)}, bf16[128,1024]{1,0:T(8,128)(2,1)S(1)}, u32[]{:S(2)}, u32[]{:S(2)}) collective-permute-start(bf16[128,1024]{1,0:T(8,128)(2,1)S(1)} %get-tuple-element.25.kv_own), channel_id=1, source_target_pairs={{0,1},{1,0},{2,3},{3,2},{4,5},{5,4},{6,7},{7,6},{8,9},{9,8},{10,11... | collective-permute-start | bytes 786440 | tf_op jit(solution)/shard_map/ppermute | solution.py:33
  2.3 21.3 %collective-permute-start = (bf16[128,2048]{1,0:T(8,128)(2,1)}, bf16[128,2048]{1,0:T(8,128)(2,1)S(1)}, u32[]{:S(2)}, u32[]{:S(2)}) collective-permute-start(bf16[128,2048]{1,0:T(8,128)(2,1)} %queries.1), channel_id=1, source_target_pairs={{0,1},{1,0},{2,3},{3,2},{4,5},{5,4},{6,7},{7,6},{8,9},{9,8},{10,11... | collective-permute-start | bytes 1572872 | tf_op jit(solution)/shard_map/ppermute | solution.py:33
  2.8 20.8 %collective-permute-start.1 = (bf16[128,2048]{1,0:T(8,128)(2,1)}, bf16[128,2048]{1,0:T(8,128)(2,1)S(1)}, u32[]{:S(2)}, u32[]{:S(2)}) collective-permute-start(bf16[128,2048]{1,0:T(8,128)(2,1)} %grads.1), channel_id=1, source_target_pairs={{0,1},{1,0},{2,3},{3,2},{4,5},{5,4},{6,7},{7,6},{8,9},{9,8},{10,11... | collective-permute-start | bytes 1572872 | tf_op jit(solution)/shard_map/ppermute | solution.py:33
  2.9 11.6 %collective-permute-start.4 = (bf16[64,1024]{1,0:T(8,128)(2,1)S(1)}, bf16[64,1024]{1,0:T(8,128)(2,1)S(1)}, u32[]{:S(2)}, u32[]{:S(2)}) collective-permute-start(bf16[64,1024]{1,0:T(8,128)(2,1)S(1)} %get-tuple-element.27), channel_id=1, source_target_pairs={{0,127},{1,2},{2,1},{3,4},{4,3},{5,6},{6,5},{7,8},{8,7},{9,10},{10... | collective-permute-start | bytes 393224 | tf_op jit(solution)/shard_map/ppermute | solution.py:33
  14.4 9.3 %collective-permute-start.3 = (bf16[64,1024]{1,0:T(8,128)(2,1)S(1)}, bf16[64,1024]{1,0:T(8,128)(2,1)S(1)}, u32[]{:S(2)}, u32[]{:S(2)}) collective-permute-start(bf16[64,1024]{1,0:T(8,128)(2,1)S(1)} %slice_select_fusion), channel_id=1, source_target_pairs={{0,2},{1,127},{2,4},{3,1},{4,6},{5,3},{6,8},{7,5},{8,10},{9,7},{10... | collective-permute-start | bytes 393224 | tf_op jit(solution)/shard_map/ppermute | solution.py:33
  14.5 11.8 %collective-permute-start.5 = (bf16[64,1024]{1,0:T(8,128)(2,1)S(1)}, bf16[64,1024]{1,0:T(8,128)(2,1)S(1)}, u32[]{:S(2)}, u32[]{:S(2)}) collective-permute-start(bf16[64,1024]{1,0:T(8,128)(2,1)S(1)} %slice_select_fusion.1), channel_id=1, source_target_pairs={{0,2},{1,127},{2,4},{3,1},{4,6},{5,3},{6,8},{7,5},{8,10},{9,7},{10... | collective-permute-start | bytes 393224 | tf_op jit(solution)/shard_map/ppermute | solution.py:33
  29.2 9.8 %collective-permute-start.6 = (bf16[2,64,2048]{2,1,0:T(8,128)(2,1)S(1)}, bf16[2,64,2048]{2,1,0:T(8,128)(2,1)S(1)}, u32[]{:S(2)}, u32[]{:S(2)}) collective-permute-start(bf16[2,64,2048]{2,1,0:T(8,128)(2,1)S(1)} %get-tuple-element.32.rest), channel_id=1, source_target_pairs={{0,1},{1,0},{2,3},{3,2},{4,5},{5,4},{6,7},{7,6},{8,9},{9,8},{10,11... | collective-permute-start | bytes 1572872 | tf_op jit(solution)/shard_map/ppermute | solution.py:33
  29.3 9.7 %collective-permute-start.7 = (bf16[64,1024]{1,0:T(8,128)(2,1)S(1)}, bf16[64,1024]{1,0:T(8,128)(2,1)S(1)}, u32[]{:S(2)}, u32[]{:S(2)}) collective-permute-start(bf16[64,1024]{1,0:T(8,128)(2,1)S(1)} %get-tuple-element.31), channel_id=1, source_target_pairs={{0,125},{1,4},{2,127},{3,6},{4,1},{5,8},{6,3},{7,10},{8,5},{9,12},... | collective-permute-start | bytes 393224 | tf_op jit(solution)/shard_map/ppermute | solution.py:33
  29.4 11.2 %collective-permute-start.8 = (bf16[128,1024]{1,0:T(8,128)(2,1)S(1)}, bf16[128,1024]{1,0:T(8,128)(2,1)S(1)}, u32[]{:S(2)}, u32[]{:S(2)}) collective-permute-start(bf16[128,1024]{1,0:T(8,128)(2,1)S(1)} %get-tuple-element.36), channel_id=1, source_target_pairs={{0,1},{1,0},{2,3},{3,2},{4,5},{5,4},{6,7},{7,6},{8,9},{9,8},{10,11... | collective-permute-start | bytes 786440 | tf_op jit(solution)/shard_map/ppermute | solution.py:33
  29.8 10.8 %collective-permute-start.9 = (bf16[128,1024]{1,0:T(8,128)(2,1)S(1)}, bf16[128,1024]{1,0:T(8,128)(2,1)S(1)}, u32[]{:S(2)}, u32[]{:S(2)}) collective-permute-start(bf16[128,1024]{1,0:T(8,128)(2,1)S(1)} %get-tuple-element.37), channel_id=1, source_target_pairs={{0,126},{1,3},{2,0},{3,5},{4,2},{5,7},{6,4},{7,9},{8,6},{9,11},{10... | collective-permute-start | bytes 786440 | tf_op jit(solution)/shard_map/ppermute | solution.py:33
  31.9 11.9 %collective-permute-start.10 = (bf16[128,1024]{1,0:T(8,128)(2,1)S(1)}, bf16[128,1024]{1,0:T(8,128)(2,1)S(1)}, u32[]{:S(2)}, u32[]{:S(2)}) collective-permute-start(bf16[128,1024]{1,0:T(8,128)(2,1)S(1)} %get-tuple-element.38), channel_id=1, source_target_pairs={{0,127},{1,2},{2,1},{3,4},{4,3},{5,6},{6,5},{7,8},{8,7},{9,10},{10... | collective-permute-start | bytes 786440 | tf_op jit(solution)/shard_map/ppermute | solution.py:33

commit v5 on v4

--- a/solution.py
+++ b/solution.py
@@ -58,12 +58,12 @@
     *refs,
 ):
     if leading:
-        dq_rest, total, table, q_work, g_work, bias = refs
-        dq = dq_rest
+        dq, total, table, q_work, g_work, bias = refs
     else:
-        kv_c, total_in, dq_first, out_own, out_sib, out_a, out_b, out_c = refs[:8]
-        total, table, q_work, g_work, bias = refs[8:]
-        dq = dq_first
+        kv_c, dq_in, total_in, dq_first, dq_rest, out_own, out_sib, out_a, out_b, out_c = (
+            refs[:10]
+        )
+        dq, total, table, q_work, g_work, bias = refs[10:]
     me = place[0]
     count = slots.shape[0] // 2
     parity = lax.rem(me, 2)
@@ -85,43 +85,48 @@
     passed_odd = jnp.logical_and(is_odd, slots[2 * near_a] == count - 1)
     passed_even = jnp.logical_and(is_odd, slots[2 * near_b] == count - 1)
     entry_ids = [slots[chip_base + e] for e in range(4)]
-    entry_ids += [jnp.where(passed_even, count - 1, slots[2 * near_a + parity])]
-    entry_ids += [slots[2 * near_b + parity]]
+    entry_ids += [slots[2 * near_a + parity], slots[2 * near_b + parity]]
     if not leading:
         table[TABLE_C * ROWS :, :] = kv_c[...]
-        entry_ids += [jnp.where(passed_odd, count - 1, slots[2 * far + parity])]
+        passed_middle = jnp.logical_or(passed_odd, passed_even)
+        entry_ids += [jnp.where(passed_middle, count - 1, slots[2 * far + parity])]
 
     own_row = pl.multiple_of(parity * ROWS, ROWS)
     other_row = pl.multiple_of((1 - parity) * ROWS, ROWS)
+    other_entry = jnp.where(middle_even, 1 + parity, jnp.where(is_odd, 1, 2))
+    slot = 0 if leading else 1
+
+    @pl.when(middle_even)
+    def _():
+        q_work[slot] = q_own[pl.ds(other_row, ROWS), :]
+        g_work[slot] = g_own[pl.ds(other_row, ROWS), :]
+
+    @pl.when(jnp.logical_not(middle_even))
+    def _():
+        q_work[slot] = q_sib[pl.ds(own_row, ROWS), :]
+        g_work[slot] = g_sib[pl.ds(own_row, ROWS), :]
+
     if leading:
         total[...] = jnp.zeros_like(total)
-
-        @pl.when(middle_even)
-        def _():
-            q_work[0] = q_own[pl.ds(other_row, ROWS), :]
-            g_work[0] = g_own[pl.ds(other_row, ROWS), :]
-
-        @pl.when(jnp.logical_not(middle_even))
-        def _():
-            q_work[0] = q_sib[pl.ds(own_row, ROWS), :]
-            g_work[0] = g_sib[pl.ds(own_row, ROWS), :]
 
         @pl.when(far_middle)
         def _():
             q_work[1] = q_sib[ROWS:, :]
             g_work[1] = g_sib[ROWS:, :]
 
-        first = 0
+        entries = (other_entry, 3)
+        first = jnp.where(passed_even, 1, 0)
         last = jnp.where(jnp.logical_and(far_middle, jnp.logical_not(is_odd)), 2, 1)
-        other_entry = jnp.where(middle_even, 1 + parity, jnp.where(is_odd, 1, 2))
     else:
+        total[...] = total_in[...]
         q_work[0] = q_own[pl.ds(own_row, ROWS), :]
         g_work[0] = g_own[pl.ds(own_row, ROWS), :]
-        first = 0
-        last = jnp.where(jnp.logical_and(far_middle, is_odd), 0, 1)
+        entries = (3 * parity, other_entry)
+        first = jnp.where(jnp.logical_and(far_middle, is_odd), 1, 0)
+        last = jnp.where(passed_even, 2, 1)
 
     def work_item(item, carry):
-        entry = jnp.where(item == 0, other_entry, 3) if leading else 3 * parity
+        entry = jnp.where(item == 0, *entries)
         query_id = slots[chip_base + entry]
         indices = []
         key_base = []
@@ -189,12 +194,17 @@
                 total[at, vcols] += value_add[part]
         return carry
 
-    if not leading:
-        total[...] = total_in[...]
     lax.fori_loop(first, last, work_item, 0)
     if leading:
         return
     low = jnp.bfloat16
+    dq_first[...] = dq[0]
+    dq_rest[...] = dq_in[...]
+
+    @pl.when(passed_even)
+    def _():
+        dq_rest[0] = dq[1]
+
     out_own[...] = total[pl.ds(own_at, 128), :]
     out_sib[...] = total[pl.ds(sib_at, 128), :].astype(low)
     nothing = jnp.zeros((ROWS, 2 * KV), low)
@@ -212,8 +222,8 @@
 
     @pl.when(passed_even)
     def _():
-        out_b[pl.ds(other_row, ROWS), :] = out_a[pl.ds(own_row, ROWS), :]
-        out_a[pl.ds(own_row, ROWS), :] = nothing
+        out_b[pl.ds(other_row, ROWS), :] = total[passed, :].astype(low)
+        out_c[...] = nothing
 
 
 def pack_kernel(
@@ -230,6 +240,7 @@
     q_own,
     g_own,
     row_start,
+    fold,
     slots,
     docs,
     sems,
@@ -258,10 +269,16 @@
         copy.start()
     copies[0].wait()
     copies[1].wait()
+    middle = slots.shape[0] // 2 - 1
+    chip_base = 2 * (place[0] - parity)
+    holder = jnp.where(
+        slots[chip_base + 2] == middle, 1, jnp.where(slots[chip_base] == middle, 2, 0)
+    )
+    fold[...] = jnp.full(fold.shape, jnp.where(parity == 1, holder, 0))
     count = docs.shape[0]
     lane = lax.rem(lax.broadcasted_iota(jnp.int32, (1, GROUP * ROWS), 1), ROWS)
     for entry in range(4):
-        first = slots[2 * (place[0] - parity) + entry] * ROWS
+        first = slots[chip_base + entry] * ROWS
 
         def halve(_, bounds):
             low, high = bounds
@@ -310,7 +327,7 @@
 
     @pl.when(jnp.logical_not(moved))
     def _():
-        out[pl.ds(own_row, ROWS), :] = first[0]
+        out[pl.ds(own_row, ROWS), :] = first[...]
 
     @pl.when(middle_even)
     def _():
@@ -370,7 +387,7 @@
     params = pltpu.CompilerParams(vmem_limit_bytes=VMEM_LIMIT)
 
     bf16 = functools.partial(jax.ShapeDtypeStruct, dtype=jnp.bfloat16)
-    kv, kv_chain, kv_cross, q_own, g_own, row_start = pl.pallas_call(
+    kv, kv_chain, kv_cross, q_own, g_own, row_start, fold = pl.pallas_call(
         pack_kernel,
         out_shape=(
             bf16((2 * ROWS, 2 * KV)),
@@ -379,9 +396,10 @@
             bf16((2 * ROWS, WIDE)),
             bf16((2 * ROWS, WIDE)),
             jax.ShapeDtypeStruct((4, GROUP * ROWS), jnp.int32),
+            jax.ShapeDtypeStruct((8, 128), jnp.int32),
         ),
         in_specs=smem(1) + hbm(6),
-        out_specs=tuple(vmem(6)),
+        out_specs=tuple(vmem(7)),
         scratch_shapes=[
             pltpu.SMEM(slot_to_block.shape, jnp.int32),
             pltpu.SMEM(doc_starts.shape, jnp.int32),
@@ -398,19 +416,17 @@
         in_hbm(queries),
         in_hbm(output_gradient),
     )
+    kv_a = send(kv_chain, 2, -2)
+    kv_b = send(kv_cross, -1, 1)
     kv_sib = send(kv, 1, -1)
-    kv_b = send(kv_cross, -1, 1)
     q_sib = send(queries, 1, -1)
     g_sib = send(output_gradient, 1, -1)
-    chip_ids = lax.dynamic_slice_in_dim(slot_to_block, 2 * (me - me % 2), 4, 0)
-    middle = slot_to_block.shape[0] // 2 - 1
-    is_odd = me % 2 == 1
-    swapped = jnp.logical_and(is_odd, chip_ids[0] == middle)
-    kv_a = send(jnp.where(swapped, kv_sib[:ROWS], kv_chain), 2, -2)
-    holds = jnp.logical_and(is_odd, chip_ids[2] == middle)
-    kv_c = send(jnp.where(holds, kv[:ROWS], kv_b), 2, -2)
+    which = fold[:1, :1]
+    passed = jnp.where(which == 1, kv[:ROWS], jnp.where(which == 2, kv_sib[:ROWS], kv_b))
+    kv_c = send(passed, 2, -2)
 
     work = [
+        pltpu.VMEM((2, ROWS, WIDE), jnp.bfloat16),
         pltpu.VMEM((ENTRIES * ROWS, 2 * KV), jnp.bfloat16),
         pltpu.VMEM((2, ROWS, WIDE), jnp.bfloat16),
         pltpu.VMEM((2, ROWS, WIDE), jnp.bfloat16),
@@ -431,40 +447,40 @@
         kv_a,
         kv_b,
     )
-    dq_rest, total = pl.pallas_call(
+    dq_leading, total = pl.pallas_call(
         functools.partial(attention_kernel, True),
         out_shape=(bf16((2, ROWS, WIDE)), sums),
         in_specs=smem(3) + vmem(9),
         out_specs=tuple(vmem(2)),
-        scratch_shapes=work,
+        scratch_shapes=work[1:],
         compiler_params=params,
         cost_estimate=pl.CostEstimate(
             flops=1 << 36, bytes_accessed=1 << 22, transcendentals=1 << 18
         ),
         name="attention_leading",
     )(*operands)
-    dq_first, own, sib, out_a, out_b, out_c = pl.pallas_call(
+    dq_first, dq_rest, own, sib, out_a, out_b, out_c = pl.pallas_call(
         functools.partial(attention_kernel, False),
         out_shape=(
-            bf16((1, ROWS, WIDE)),
+            bf16((ROWS, WIDE)),
+            bf16((2, ROWS, WIDE)),
             jax.ShapeDtypeStruct((2 * ROWS, 2 * KV), jnp.float32),
             bf16((2 * ROWS, 2 * KV)),
             bf16((2 * ROWS, 2 * KV)),
             bf16((2 * ROWS, 2 * KV)),
             bf16((ROWS, 2 * KV)),
         ),
-        in_specs=smem(3) + vmem(11),
-        out_specs=tuple(vmem(6)),
-        scratch_shapes=[pltpu.VMEM(sums.shape, jnp.float32)] + work,
+        in_specs=smem(3) + vmem(12),
+        out_specs=tuple(vmem(7)),
+        scratch_shapes=work[:1] + [pltpu.VMEM(sums.shape, jnp.float32)] + work[1:],
         compiler_params=params,
         name="attention_last",
-    )(*operands, kv_c, total)
+    )(*operands, kv_c, dq_leading, total)
 
     back_c = send(out_c, -3, 3)
     back_a = send(out_a, -2, 2)
     back_b = send(out_b, -1, 1)
     back_sib = send(sib, 1, -1)
-    dq_rest, _ = lax.optimization_barrier((dq_rest, out_c))
     dq_sib = send(dq_rest, 1, -1)
 
     query_grad, own = pl.pallas_call(

time: 44.8 us -> 44.9 us (level)
  the two profiles are of different devices: /device:TPU:16 before, /device:TPU:1 now
where the time goes in v5:
time: 44.9 us; the launch traced here: 44.7 us
  starting transfers between devices  25.7 us (57%)
  Pallas kernels  9.54 us (21%)
  waiting for transfers between devices  6.91 us (15%)
  between operations  2.01 us (4%)
  local copies, waits for them, and re-layouts  0.52 us (1%)
    ppermute x11, starting transfers between devices, send(): return lax.ppermute(array, 'ctx', pairs)  25.7 us
    ppermute x11, waiting for transfers between devices, send(): return lax.ppermute(array, 'ctx', pairs)  6.91 us
    pallas_call x1, Pallas kernels, shards(): pl.pallas_call(functools.partial(attention_kernel, False), out_shape=(bf1...  2.93 us
    pallas_call x1, Pallas kernels, shards(): pl.pallas_call(functools.partial(attention_kernel, True), out_shape=(bf16...  2.7 us
    pallas_call x1, Pallas kernels, shards(): pl.pallas_call(early_kernel, out_shape=(bf16((2 * ROWS, WIDE)), jax.Shape...  1.59 us
    pallas_call x1, Pallas kernels, shards(): pl.pallas_call(pack_kernel, out_shape=(bf16((2 * ROWS, 2 * KV)), bf16((RO...  1.56 us
  transfers between devices with their start and end apart: 11, of which 2 were waited for; matrix products, arithmetic and copies ran while one was open for 1% of the time, Pallas kernels for 13%

profile of v5, /device:TPU:1, one launch (start us, length us, event | category | flops | bytes accessed | tf_op | source)
XLA Modules:
  0.0 44.7 jit_solution(6353967729285691503)
XLA Ops:
  0.6 0.0 copy-start
  0.6 3.3 %collective-permute-start = (bf16[128,2048]{1,0:T(8,128)(2,1)}, bf16[128,2048]{1,0:T(8,128)(2,1)S(1)}, u32[]{:S(2)}, u32[]{:S(2)}) collective-permute-start(bf16[128,2048]{1,0:T(8,128)(2,1)} %queries.1), channel_id=1, source_target_pairs={{0,1},{1,0},{2,3},{3,2},{4,5},{5,4},{6,7},{7,6},{8,9},{9,8},{10,11... | collective-permute-start | bytes 1572872 | tf_op jit(solution)/shard_map/ppermute | solution.py:33
  4.0 0.1 collective-permute-start.1
  4.1 1.6 %prepare.1 = (bf16[128,1024]{1,0:T(8,128)(2,1)S(1)}, bf16[64,1024]{1,0:T(8,128)(2,1)S(1)}, bf16[64,1024]{1,0:T(8,128)(2,1)S(1)}, bf16[128,2048]{1,0:T(8,128)(2,1...) custom-call(s32[1]{0:T(128)} %bitcast.place, s32[256]{0:T(256)} %slots.5, ...), custom_call_target="tpu_custom_call" | custom-call | tf_op jit(solution)/shard_map/prepare/pallas_call | solution.py:390
  5.6 0.5 %collective-permute-start.2 = (bf16[128,1024]{1,0:T(8,128)(2,1)S(1)}, bf16[128,1024]{1,0:T(8,128)(2,1)S(1)}, u32[]{:S(2)}, u32[]{:S(2)}) collective-permute-start(bf16[128,1024]{1,0:T(8,128)(2,1)S(1)} %get-tuple-element.26.kv_own), channel_id=1, source_target_pairs={{0,1},{1,0},{2,3},{3,2},{4,5},{5,4},{6,7},{7,6},{8,9},{9,8},{10,11... | collective-permute-start | bytes 786440 | tf_op jit(solution)/shard_map/ppermute | solution.py:33
  6.1 0.0 collective-permute-start.4
  6.1 7.1 %collective-permute-start.3 = (bf16[64,1024]{1,0:T(8,128)(2,1)S(1)}, bf16[64,1024]{1,0:T(8,128)(2,1)S(1)}, u32[]{:S(2)}, u32[]{:S(2)}) collective-permute-start(bf16[64,1024]{1,0:T(8,128)(2,1)S(1)} %get-tuple-element.27), channel_id=1, source_target_pairs={{0,2},{1,127},{2,4},{3,1},{4,6},{5,3},{6,8},{7,5},{8,10},{9,7},{10... | collective-permute-start | bytes 393224 | tf_op jit(solution)/shard_map/ppermute | solution.py:33
  13.2 0.5 %slice.9 = s32[1,1]{1,0:T(1,128)} slice(s32[8,128]{1,0:T(8,128)S(1)} %get-tuple-element.29), slice={[0:1], [0:1]} | slice | bytes 8 | tf_op jit(solution)/shard_map/slice | solution.py:424
  15.0 0.0 collective-permute-done.4.kv_b
  15.0 0.0 collective-permute-done.2.kv_sib
  15.1 7.7 %collective-permute-start.5 = (bf16[64,1024]{1,0:T(8,128)(2,1)S(1)}, bf16[64,1024]{1,0:T(8,128)(2,1)S(1)}, u32[]{:S(2)}, u32[]{:S(2)}) collective-permute-start(bf16[64,1024]{1,0:T(8,128)(2,1)S(1)} %fusion), channel_id=1, source_target_pairs={{0,2},{1,127},{2,4},{3,1},{4,6},{5,3},{6,8},{7,5},{8,10},{9,7},{10... | collective-permute-start | bytes 393224 | tf_op jit(solution)/shard_map/ppermute | solution.py:33
  22.8 0.0 collective-permute-done.3.kv_a
  22.8 0.0 collective-permute-done.q_sib
  22.8 0.0 collective-permute-done.1.g_sib
  22.8 0.0 copy-done
  22.8 2.7 %attention_leading.1 = (bf16[2,64,2048]{2,1,0:T(8,128)(2,1)S(1)}, f32[448,1024]{1,0:T(8,128)S(1)}) custom-call(s32[1]{0:T(128)} %bitcast.place, s32[256]{0:T(256)} %slots.5, s32[4,256]{1,0:T(4,128)S(1)} %bitcast.4, s32[4,256]{1,0:T(4,128)S(1)} %get-tuple-element.23.row_start, bf16[128,2048]{1,0:T(8,128)(2,1)S(1)} %get-tuple-element.24.q_own, ...), custom_call_target="tpu_custom_call" | custom-call | flops 68719476736 | bytes 4194304 | tf_op jit(solution)/shard_map/attention_leading/pallas_call | solution.py:450
  25.5 0.0 collective-permute-done.5.refs_0_
  25.5 2.9 %attention_last.1 = (bf16[64,2048]{1,0:T(8,128)(2,1)S(1)}, bf16[2,64,2048]{2,1,0:T(8,128)(2,1)S(1)}, f32[128,1024]{1,0:T(8,128)S(1)}, bf16[128,1024]{1,0:T(8,128...) custom-call(s32[1]{0:T(128)} %bitcast.place, s32[256]{0:T(256)} %slots.5, ...), custom_call_target="tpu_custom_call" | custom-call | tf_op jit(solution)/shard_map/attention_last/pallas_call | solution.py:462
  28.4 0.8 %collective-permute-start.6 = (bf16[2,64,2048]{2,1,0:T(8,128)(2,1)S(1)}, bf16[2,64,2048]{2,1,0:T(8,128)(2,1)S(1)}, u32[]{:S(2)}, u32[]{:S(2)}) collective-permute-start(bf16[2,64,2048]{2,1,0:T(8,128)(2,1)S(1)} %get-tuple-element.33.rest), channel_id=1, source_target_pairs={{0,1},{1,0},{2,3},{3,2},{4,5},{5,4},{6,7},{7,6},{8,9},{9,8},{10,11... | collective-permute-start | bytes 1572872 | tf_op jit(solution)/shard_map/ppermute | solution.py:33
  29.2 0.0 collective-permute-start.7
  29.2 0.6 %collective-permute-start.8 = (bf16[128,1024]{1,0:T(8,128)(2,1)S(1)}, bf16[128,1024]{1,0:T(8,128)(2,1)S(1)}, u32[]{:S(2)}, u32[]{:S(2)}) collective-permute-start(bf16[128,1024]{1,0:T(8,128)(2,1)S(1)} %get-tuple-element.38), channel_id=1, source_target_pairs={{0,1},{1,0},{2,3},{3,2},{4,5},{5,4},{6,7},{7,6},{8,9},{9,8},{10,11... | collective-permute-start | bytes 786440 | tf_op jit(solution)/shard_map/ppermute | solution.py:33
  29.8 5.7 %collective-permute-start.9 = (bf16[128,1024]{1,0:T(8,128)(2,1)S(1)}, bf16[128,1024]{1,0:T(8,128)(2,1)S(1)}, u32[]{:S(2)}, u32[]{:S(2)}) collective-permute-start(bf16[128,1024]{1,0:T(8,128)(2,1)S(1)} %get-tuple-element.39), channel_id=1, source_target_pairs={{0,126},{1,3},{2,0},{3,5},{4,2},{5,7},{6,4},{7,9},{8,6},{9,11},{10... | collective-permute-start | bytes 786440 | tf_op jit(solution)/shard_map/ppermute | solution.py:33
  35.5 0.0 collective-permute-start.10
  35.5 0.0 collective-permute-done.7.back_c
  35.5 0.0 collective-permute-done.6.theirs
  35.5 1.6 %query_gradient_rows.1 = (bf16[128,2048]{1,0:T(8,128)(2,1)}, f32[128,1024]{1,0:T(8,128)S(1)}) custom-call(s32[1]{0:T(128)} %bitcast.place, s32[256]{0:T(256)} %slots.5, s32[4,256]{1,0:T(4,128)S(1)} %bitcast.6, bf16[64,2048]{1,0:T(8,128)(2,1)S(1)} %get-tuple-element.32.first, bf16[2,64,2048]{2,1,0:T(8,128)(2,1)S(1)} %get-tuple-element.33.rest, ...), custom_call_target="tpu_custom_call" | custom-call | flops 68719476736 | bytes 4194304 | tf_op jit(solution)/shard_map/query_gradient_rows/pallas_call | solution.py:486
  37.1 0.0 collective-permute-done.8.sib
  37.1 3.6 %collective-permute-done.9.back_a = bf16[128,1024]{1,0:T(8,128)(2,1)S(1)} collective-permute-done((bf16[128,1024]{1,0:T(8,128)(2,1)S(1)}, bf16[128,1024]{1,0:T(8,128)(2,1)S(1)}, u32[]{:S(2)}, u32[]{:S(2)}) %collective-permute-start.9) | collective-permute-done | bytes 262176 | tf_op jit(solution)/shard_map/ppermute | solution.py:33
  40.7 3.3 %collective-permute-done.10.back_b = bf16[128,1024]{1,0:T(8,128)(2,1)S(1)} collective-permute-done((bf16[128,1024]{1,0:T(8,128)(2,1)S(1)}, bf16[128,1024]{1,0:T(8,128)(2,1)S(1)}, u32[]{:S(2)}, u32[]{:S(2)}) %collective-permute-start.10) | collective-permute-done | bytes 262176 | tf_op jit(solution)/shard_map/ppermute | solution.py:33
  44.0 0.8 %key_value_gradient_sum.1 = (bf16[128,512]{1,0:T(8,128)(2,1)}, bf16[128,512]{1,0:T(8,128)(2,1)}) custom-call(f32[128,1024]{1,0:T(8,128)S(1)} %get-tuple-element.37.own, bf16[128,1024]{1,0:T(8,128)(2,1)S(1)} %collective-permute-done.8.sib, bf16[128,1024]{1,0:T(8,128)(2,1)S(1)} %collective-permute-done.9.back_a, ...), custom_call_target="tpu_custom_call" | custom-call | tf_op jit(solution)/shard_map/key_value_gradient_sum/pallas_call | solution.py:510
  (1 shorter events, 0.0 us)
Async XLA Ops:
  0.6 22.1 %copy-start = (s32[256,4]{0,1:T(4,128)S(1)}, s32[256,4]{0,1:T(4,128)}, u32[]{:S(2)}) copy-start(s32[256,4]{0,1:T(4,128)} %param.13) | copy-start | bytes 12292
  0.6 22.1 %collective-permute-start = (bf16[128,2048]{1,0:T(8,128)(2,1)}, bf16[128,2048]{1,0:T(8,128)(2,1)S(1)}, u32[]{:S(2)}, u32[]{:S(2)}) collective-permute-start(bf16[128,2048]{1,0:T(8,128)(2,1)} %queries.1), channel_id=1, source_target_pairs={{0,1},{1,0},{2,3},{3,2},{4,5},{5,4},{6,7},{7,6},{8,9},{9,8},{10,11... | collective-permute-start | bytes 1572872 | tf_op jit(solution)/shard_map/ppermute | solution.py:33
  4.0 18.8 %collective-permute-start.1 = (bf16[128,2048]{1,0:T(8,128)(2,1)}, bf16[128,2048]{1,0:T(8,128)(2,1)S(1)}, u32[]{:S(2)}, u32[]{:S(2)}) collective-permute-start(bf16[128,2048]{1,0:T(8,128)(2,1)} %grads.1), channel_id=1, source_target_pairs={{0,1},{1,0},{2,3},{3,2},{4,5},{5,4},{6,7},{7,6},{8,9},{9,8},{10,11... | collective-permute-start | bytes 1572872 | tf_op jit(solution)/shard_map/ppermute | solution.py:33
  5.6 9.4 %collective-permute-start.2 = (bf16[128,1024]{1,0:T(8,128)(2,1)S(1)}, bf16[128,1024]{1,0:T(8,128)(2,1)S(1)}, u32[]{:S(2)}, u32[]{:S(2)}) collective-permute-start(bf16[128,1024]{1,0:T(8,128)(2,1)S(1)} %get-tuple-element.26.kv_own), channel_id=1, source_target_pairs={{0,1},{1,0},{2,3},{3,2},{4,5},{5,4},{6,7},{7,6},{8,9},{9,8},{10,11... | collective-permute-start | bytes 786440 | tf_op jit(solution)/shard_map/ppermute | solution.py:33
  6.1 8.9 %collective-permute-start.4 = (bf16[64,1024]{1,0:T(8,128)(2,1)S(1)}, bf16[64,1024]{1,0:T(8,128)(2,1)S(1)}, u32[]{:S(2)}, u32[]{:S(2)}) collective-permute-start(bf16[64,1024]{1,0:T(8,128)(2,1)S(1)} %get-tuple-element.28), channel_id=1, source_target_pairs={{0,127},{1,2},{2,1},{3,4},{4,3},{5,6},{6,5},{7,8},{8,7},{9,10},{10... | collective-permute-start | bytes 393224 | tf_op jit(solution)/shard_map/ppermute | solution.py:33
  6.1 16.6 %collective-permute-start.3 = (bf16[64,1024]{1,0:T(8,128)(2,1)S(1)}, bf16[64,1024]{1,0:T(8,128)(2,1)S(1)}, u32[]{:S(2)}, u32[]{:S(2)}) collective-permute-start(bf16[64,1024]{1,0:T(8,128)(2,1)S(1)} %get-tuple-element.27), channel_id=1, source_target_pairs={{0,2},{1,127},{2,4},{3,1},{4,6},{5,3},{6,8},{7,5},{8,10},{9,7},{10... | collective-permute-start | bytes 393224 | tf_op jit(solution)/shard_map/ppermute | solution.py:33
  15.1 10.4 %collective-permute-start.5 = (bf16[64,1024]{1,0:T(8,128)(2,1)S(1)}, bf16[64,1024]{1,0:T(8,128)(2,1)S(1)}, u32[]{:S(2)}, u32[]{:S(2)}) collective-permute-start(bf16[64,1024]{1,0:T(8,128)(2,1)S(1)} %fusion), channel_id=1, source_target_pairs={{0,2},{1,127},{2,4},{3,1},{4,6},{5,3},{6,8},{7,5},{8,10},{9,7},{10... | collective-permute-start | bytes 393224 | tf_op jit(solution)/shard_map/ppermute | solution.py:33
  28.4 7.1 %collective-permute-start.6 = (bf16[2,64,2048]{2,1,0:T(8,128)(2,1)S(1)}, bf16[2,64,2048]{2,1,0:T(8,128)(2,1)S(1)}, u32[]{:S(2)}, u32[]{:S(2)}) collective-permute-start(bf16[2,64,2048]{2,1,0:T(8,128)(2,1)S(1)} %get-tuple-element.33.rest), channel_id=1, source_target_pairs={{0,1},{1,0},{2,3},{3,2},{4,5},{5,4},{6,7},{7,6},{8,9},{9,8},{10,11... | collective-permute-start | bytes 1572872 | tf_op jit(solution)/shard_map/ppermute | solution.py:33
  29.2 6.3 %collective-permute-start.7 = (bf16[64,1024]{1,0:T(8,128)(2,1)S(1)}, bf16[64,1024]{1,0:T(8,128)(2,1)S(1)}, u32[]{:S(2)}, u32[]{:S(2)}) collective-permute-start(bf16[64,1024]{1,0:T(8,128)(2,1)S(1)} %get-tuple-element.35), channel_id=1, source_target_pairs={{0,125},{1,4},{2,127},{3,6},{4,1},{5,8},{6,3},{7,10},{8,5},{9,12},... | collective-permute-start | bytes 393224 | tf_op jit(solution)/shard_map/ppermute | solution.py:33
  29.2 7.9 %collective-permute-start.8 = (bf16[128,1024]{1,0:T(8,128)(2,1)S(1)}, bf16[128,1024]{1,0:T(8,128)(2,1)S(1)}, u32[]{:S(2)}, u32[]{:S(2)}) collective-permute-start(bf16[128,1024]{1,0:T(8,128)(2,1)S(1)} %get-tuple-element.38), channel_id=1, source_target_pairs={{0,1},{1,0},{2,3},{3,2},{4,5},{5,4},{6,7},{7,6},{8,9},{9,8},{10,11... | collective-permute-start | bytes 786440 | tf_op jit(solution)/shard_map/ppermute | solution.py:33
  29.8 10.8 %collective-permute-start.9 = (bf16[128,1024]{1,0:T(8,128)(2,1)S(1)}, bf16[128,1024]{1,0:T(8,128)(2,1)S(1)}, u32[]{:S(2)}, u32[]{:S(2)}) collective-permute-start(bf16[128,1024]{1,0:T(8,128)(2,1)S(1)} %get-tuple-element.39), channel_id=1, source_target_pairs={{0,126},{1,3},{2,0},{3,5},{4,2},{5,7},{6,4},{7,9},{8,6},{9,11},{10... | collective-permute-start | bytes 786440 | tf_op jit(solution)/shard_map/ppermute | solution.py:33
  35.5 8.5 %collective-permute-start.10 = (bf16[128,1024]{1,0:T(8,128)(2,1)S(1)}, bf16[128,1024]{1,0:T(8,128)(2,1)S(1)}, u32[]{:S(2)}, u32[]{:S(2)}) collective-permute-start(bf16[128,1024]{1,0:T(8,128)(2,1)S(1)} %get-tuple-element.40), channel_id=1, source_target_pairs={{0,127},{1,2},{2,1},{3,4},{4,3},{5,6},{6,5},{7,8},{8,7},{9,10},{10... | collective-permute-start | bytes 786440 | tf_op jit(solution)/shard_map/ppermute | solution.py:33

commit v6 on v3

--- a/solution.py
+++ b/solution.py
@@ -21,15 +21,18 @@
 EXP2_SCALE = SCALE * math.log2(math.e)
 MASKED = -1e30
 FAR = 1 << 30
-ENTRIES = 9
+ENTRIES = 8
 VMEM_LIMIT = 24 * 1024 * 1024
 
-TABLE_A, TABLE_B, TABLE_C = 4, 6, 8
+TABLE_A, TABLE_B, TABLE_C, TABLE_X = 4, 5, 6, 7
+PACK_KV = 4 * ROWS
+PACK_ROWS = 5 * ROWS
 
 
 def send(array, even_by, odd_by):
     count = lax.axis_size("ctx")
-    pairs = [(i, (i + (odd_by if i % 2 else even_by)) % count) for i in range(count)]
+    steps = [odd_by if i % 2 else even_by for i in range(count)]
+    pairs = [(i, (i + by) % count) for i, by in enumerate(steps) if by is not None]
     return lax.ppermute(array, "ctx", pairs)
 
 
@@ -46,27 +49,23 @@
     slots,
     live,
     row_start,
-    q_own,
-    q_sib,
-    g_own,
-    g_sib,
-    kv_own,
-    kv_sib,
-    kv_a,
+    pack_own,
+    pack_sib,
+    kv_x,
     kv_b,
     kv_c,
-    dq_first,
-    dq_rest,
+    kv_a,
+    dq_own,
     out_own,
     out_sib,
     out_a,
     out_b,
     out_c,
+    dq,
+    total,
     table,
-    total,
     q_work,
     g_work,
-    dq,
     bias,
 ):
     me = place[0]
@@ -78,45 +77,53 @@
 
     own_at = pl.multiple_of(parity * 128, 128)
     sib_at = pl.multiple_of((1 - parity) * 128, 128)
-    table[pl.ds(own_at, 128), :] = kv_own[...]
-    table[pl.ds(sib_at, 128), :] = kv_sib[...]
-    table[TABLE_A * ROWS : TABLE_B * ROWS, :] = kv_a[...]
-    table[TABLE_B * ROWS : TABLE_C * ROWS, :] = kv_b[...]
-    table[TABLE_C * ROWS :, :] = kv_c[...]
+    for at, pack in ((own_at, pack_own), (sib_at, pack_sib)):
+        table[pl.ds(at, ROWS), :] = pack[PACK_KV:, : 2 * KV]
+        table[pl.ds(at + ROWS, ROWS), :] = pack[PACK_KV:, 2 * KV :]
+    for entry, block in (
+        (TABLE_A, kv_a),
+        (TABLE_B, kv_b),
+        (TABLE_C, kv_c),
+        (TABLE_X, kv_x),
+    ):
+        table[entry * ROWS : (entry + 1) * ROWS, :] = block[...]
     total[...] = jnp.zeros_like(total)
 
     toward = jnp.where(is_odd, 1, -1)
     near_a = lax.rem(me + 2 * toward + count, count)
     near_b = lax.rem(me + toward + count, count)
     far = lax.rem(me + 3 * toward + count, count)
+    before_middle = jnp.logical_and(
+        is_odd,
+        jnp.logical_or(slots[2 * near_a] == count - 1, slots[2 * near_b] == count - 1),
+    )
     entry_ids = [slots[chip_base + e] for e in range(4)]
-    entry_ids += [slots[2 * near_a], slots[2 * near_a + 1]]
-    entry_ids += [slots[2 * near_b], slots[2 * near_b + 1]]
-    entry_ids += [slots[2 * far + parity]]
+    entry_ids += [slots[2 * i + parity] for i in (near_a, near_b, far)]
+    entry_ids += [jnp.where(before_middle, count - 1, -1)]
 
     own_row = pl.multiple_of(parity * ROWS, ROWS)
     other_row = pl.multiple_of((1 - parity) * ROWS, ROWS)
-    q_work[0] = q_own[pl.ds(own_row, ROWS), :]
-    g_work[0] = g_own[pl.ds(own_row, ROWS), :]
+    grads_at = 2 * ROWS
+    q_work[0] = pack_own[pl.ds(own_row, ROWS), :]
+    g_work[0] = pack_own[pl.ds(grads_at + own_row, ROWS), :]
 
     @pl.when(middle_even)
     def _():
-        q_work[1] = q_own[pl.ds(other_row, ROWS), :]
-        g_work[1] = g_own[pl.ds(other_row, ROWS), :]
+        q_work[1] = pack_own[pl.ds(other_row, ROWS), :]
+        g_work[1] = pack_own[pl.ds(grads_at + other_row, ROWS), :]
 
     @pl.when(jnp.logical_not(middle_even))
     def _():
-        q_work[1] = q_sib[pl.ds(own_row, ROWS), :]
-        g_work[1] = g_sib[pl.ds(own_row, ROWS), :]
+        q_work[1] = pack_sib[pl.ds(own_row, ROWS), :]
+        g_work[1] = pack_sib[pl.ds(grads_at + own_row, ROWS), :]
 
     @pl.when(far_middle)
     def _():
-        q_work[2] = q_sib[ROWS:, :]
-        g_work[2] = g_sib[ROWS:, :]
+        q_work[2] = pack_sib[ROWS : 2 * ROWS, :]
+        g_work[2] = pack_sib[grads_at + ROWS : grads_at + 2 * ROWS, :]
 
     first = jnp.where(jnp.logical_and(far_middle, is_odd), 1, 0)
     last = jnp.where(jnp.logical_and(far_middle, jnp.logical_not(is_odd)), 3, 2)
-
     own_entry = 3 * parity
     other_entry = jnp.where(middle_even, 1 + parity, jnp.where(is_odd, 1, 2))
 
@@ -127,12 +134,10 @@
         key_base = []
         for distance in range(REACH + 1):
             key_id = query_id - distance
-            is_live = jnp.logical_and(
-                key_id >= 0, live[distance, query_id] == 1
-            )
+            is_live = jnp.logical_and(key_id >= 0, live[distance, query_id] == 1)
             index = jnp.int32(0)
             found = jnp.bool_(False)
-            for e in range(ENTRIES):
+            for e in range(len(entry_ids)):
                 match = entry_ids[e] == key_id
                 index = jnp.where(match, e, index)
                 found = jnp.logical_or(found, match)
@@ -192,14 +197,20 @@
         return carry
 
     lax.fori_loop(first, last, work_item, 0)
-
-    dq_first[...] = dq[0]
-    dq_rest[...] = dq[1:]
+    low = jnp.bfloat16
+    dq_own[...] = dq[:2]
     out_own[...] = total[pl.ds(own_at, 128), :]
-    out_sib[...] = total[pl.ds(sib_at, 128), :].astype(jnp.bfloat16)
-    out_a[...] = total[TABLE_A * ROWS : TABLE_B * ROWS, :].astype(jnp.bfloat16)
-    out_b[...] = total[TABLE_B * ROWS : TABLE_C * ROWS, :].astype(jnp.bfloat16)
-    out_c[...] = total[TABLE_C * ROWS :, :].astype(jnp.bfloat16)
+    out_sib[:ROWS, :] = dq[1]
+    out_sib[ROWS : 2 * ROWS, :] = dq[2]
+    out_sib[2 * ROWS :, : 2 * KV] = total[pl.ds(sib_at, ROWS), :].astype(low)
+    out_sib[2 * ROWS :, 2 * KV :] = total[pl.ds(sib_at + ROWS, ROWS), :].astype(low)
+    for entry, out in (
+        (TABLE_A, out_a.at[:ROWS, :]),
+        (TABLE_X, out_a.at[ROWS:, :]),
+        (TABLE_B, out_b),
+        (TABLE_C, out_c),
+    ):
+        out[...] = total[entry * ROWS : (entry + 1) * ROWS, :].astype(low)
 
 
 def pack_kernel(
@@ -210,29 +221,38 @@
     values,
     queries,
     grads,
-    both,
-    far,
-    q_own,
-    g_own,
+    chain,
+    cross,
+    pack,
     row_start,
+    fold,
     slots,
     docs,
     sems,
 ):
     parity = lax.rem(place[0], 2)
-    at = pl.ds(pl.multiple_of((1 - parity) * ROWS, ROWS), ROWS)
+    own_rows = pl.ds(pl.multiple_of(parity * ROWS, ROWS), ROWS)
+    other_rows = pl.ds(pl.multiple_of((1 - parity) * ROWS, ROWS), ROWS)
     copies = [
         pltpu.make_async_copy(source, target, sems.at[n])
         for n, (source, target) in enumerate(
             [
                 (slots_hbm, slots),
                 (docs_hbm, docs),
-                (keys.at[at, :], far.at[:, pl.ds(0, KV)]),
-                (values.at[at, :], far.at[:, pl.ds(KV, KV)]),
-                (keys, both.at[:, pl.ds(0, KV)]),
-                (values, both.at[:, pl.ds(KV, KV)]),
-                (queries, q_own),
-                (grads, g_own),
+                (keys.at[other_rows, :], cross.at[:, pl.ds(0, KV)]),
+                (values.at[other_rows, :], cross.at[:, pl.ds(KV, KV)]),
+                (keys.at[own_rows, :], chain.at[:, pl.ds(0, KV)]),
+                (values.at[own_rows, :], chain.at[:, pl.ds(KV, KV)]),
+                (queries, pack.at[pl.ds(0, 2 * ROWS), :]),
+                (grads, pack.at[pl.ds(2 * ROWS, 2 * ROWS), :]),
+            ]
+            + [
+                (
+                    source.at[pl.ds(block * ROWS, ROWS), :],
+                    pack.at[pl.ds(PACK_KV, ROWS), pl.ds((2 * block + n) * KV, KV)],
+                )
+                for block in range(2)
+                for n, source in enumerate((keys, values))
             ]
         )
     ]
@@ -240,10 +260,14 @@
         copy.start()
     copies[0].wait()
     copies[1].wait()
+    middle = slots.shape[0] // 2 - 1
+    chip_base = 2 * (place[0] - parity)
+    lends = jnp.logical_and(parity == 1, slots[chip_base] == middle)
+    fold[...] = jnp.full(fold.shape, jnp.where(lends, 1.0, 0.0))
     count = docs.shape[0]
     lane = lax.rem(lax.broadcasted_iota(jnp.int32, (1, GROUP * ROWS), 1), ROWS)
     for entry in range(4):
-        first = slots[2 * (place[0] - parity) + entry] * ROWS
+        first = slots[chip_base + entry] * ROWS
 
         def halve(_, bounds):
             low, high = bounds
@@ -277,48 +301,47 @@
         copy.wait()
 
 
-def early_kernel(place, slots, live, first, rest, theirs, own, back_c, out, acc):
+def final_kernel(
+    place, slots, live, mine, own, lent, back_a, back_c, back_b, theirs, *outs
+):
+    query_out, key_out, value_out = outs
     me = place[0]
     parity = lax.rem(me, 2)
     is_odd = parity == 1
-    middle_even, far_middle = fold_flags(2 * (me - parity), slots, live)
-    own_row = pl.multiple_of(parity * ROWS, ROWS)
-    other_row = pl.multiple_of((1 - parity) * ROWS, ROWS)
+    chip_base = 2 * (me - parity)
+    middle_even, far_middle = fold_flags(chip_base, slots, live)
+    own_rows = pl.ds(pl.multiple_of(parity * ROWS, ROWS), ROWS)
+    other_rows = pl.ds(pl.multiple_of((1 - parity) * ROWS, ROWS), ROWS)
     moved = jnp.logical_and(far_middle, is_odd)
 
     @pl.when(moved)
     def _():
-        out[pl.ds(own_row, ROWS), :] = theirs[1]
+        query_out[own_rows, :] = theirs[ROWS : 2 * ROWS, :]
 
     @pl.when(jnp.logical_not(moved))
     def _():
-        out[pl.ds(own_row, ROWS), :] = first[...]
+        query_out[own_rows, :] = mine[0]
 
     @pl.when(middle_even)
     def _():
-        out[pl.ds(other_row, ROWS), :] = rest[0]
+        query_out[other_rows, :] = mine[1]
 
     @pl.when(jnp.logical_not(middle_even))
     def _():
-        out[pl.ds(other_row, ROWS), :] = theirs[0]
-
-    acc[pl.ds(own_row, ROWS), :] = own[pl.ds(own_row, ROWS), :]
-    acc[pl.ds(other_row, ROWS), :] = own[pl.ds(other_row, ROWS), :] + back_c[
-        ...
-    ].astype(jnp.float32)
-
-
-def sum_kernel(own, sib, back_a, back_b, key_out, value_out):
-    def total(columns):
-        return (
-            own[:, columns]
-            + sib[:, columns].astype(jnp.float32)
-            + back_a[:, columns].astype(jnp.float32)
-            + back_b[:, columns].astype(jnp.float32)
-        ).astype(jnp.bfloat16)
-
-    key_out[...] = total(slice(0, KV))
-    value_out[...] = total(slice(KV, 2 * KV))
+        query_out[other_rows, :] = theirs[:ROWS, :]
+
+    keeps = jnp.logical_and(is_odd, slots[chip_base + 2] == slots.shape[0] // 2 - 1)
+    kept = jnp.where(keeps, 1.0, 0.0)
+    f32 = jnp.float32
+    for out, first in ((key_out, 0), (value_out, KV)):
+        columns = slice(first, first + KV)
+        chain = back_a[:ROWS, columns].astype(f32)
+        cross = back_b[:, columns].astype(f32) + back_c[:, columns].astype(f32)
+        low = own[:ROWS, columns] + theirs[2 * ROWS :, columns].astype(f32)
+        low = low + lent[:, columns].astype(f32) + kept * back_a[ROWS:, columns].astype(f32)
+        high = own[ROWS:, columns] + theirs[2 * ROWS :, 2 * KV + first : 3 * KV + first].astype(f32)
+        out[:ROWS, :] = (low + jnp.where(is_odd, cross, chain)).astype(out.dtype)
+        out[ROWS:, :] = (high + jnp.where(is_odd, chain, cross)).astype(out.dtype)
 
 
 def vmem(count):
@@ -352,21 +375,21 @@
     params = pltpu.CompilerParams(vmem_limit_bytes=VMEM_LIMIT)
 
     bf16 = functools.partial(jax.ShapeDtypeStruct, dtype=jnp.bfloat16)
-    kv, kv_far, q_own, g_own, row_start = pl.pallas_call(
+    kv_chain, kv_cross, pack, row_start, fold = pl.pallas_call(
         pack_kernel,
         out_shape=(
-            bf16((2 * ROWS, 2 * KV)),
             bf16((ROWS, 2 * KV)),
-            bf16((2 * ROWS, WIDE)),
-            bf16((2 * ROWS, WIDE)),
+            bf16((ROWS, 2 * KV)),
+            bf16((PACK_ROWS, WIDE)),
             jax.ShapeDtypeStruct((4, GROUP * ROWS), jnp.int32),
+            jax.ShapeDtypeStruct((ROWS, 2 * KV), jnp.float32),
         ),
         in_specs=smem(1) + hbm(6),
         out_specs=tuple(vmem(5)),
         scratch_shapes=[
             pltpu.SMEM(slot_to_block.shape, jnp.int32),
             pltpu.SMEM(doc_starts.shape, jnp.int32),
-            pltpu.SemaphoreType.DMA((8,)),
+            pltpu.SemaphoreType.DMA((12,)),
         ],
         compiler_params=params,
         name="prepare",
@@ -379,30 +402,30 @@
         in_hbm(queries),
         in_hbm(output_gradient),
     )
-    kv_c = send(kv_far, -3, 3)
-    kv_a = send(kv, 2, -2)
-    kv_b = send(kv, -1, 1)
-    kv_sib = send(kv, 1, -1)
-    q_sib = send(queries, 1, -1)
-    g_sib = send(output_gradient, 1, -1)
-
-    dq_first, dq_rest, own, sib, out_a, out_b, out_c = pl.pallas_call(
+    kv_a = send(kv_chain, 2, -2)
+    kv_b = send(kv_cross, -1, 1)
+    kv_c = send(kv_cross, -3, 3)
+    pack_sib = send(pack, 1, -1)
+    low_rows = (slice(PACK_KV, None), slice(0, 2 * KV))
+    kv_x = send(jnp.where(fold > 0, pack_sib[low_rows], pack[low_rows]), None, -2)
+
+    wide = jax.ShapeDtypeStruct((2 * ROWS, 2 * KV), jnp.float32)
+    dq_own, own, out_sib, out_a, out_b, out_c = pl.pallas_call(
         attention_kernel,
         out_shape=(
-            bf16((ROWS, WIDE)),
             bf16((2, ROWS, WIDE)),
-            jax.ShapeDtypeStruct((2 * ROWS, 2 * KV), jnp.float32),
-            bf16((2 * ROWS, 2 * KV)),
-            bf16((2 * ROWS, 2 * KV)),
+            wide,
+            bf16((3 * ROWS, WIDE)),
             bf16((2 * ROWS, 2 * KV)),
             bf16((ROWS, 2 * KV)),
+            bf16((ROWS, 2 * KV)),
         ),
-        in_specs=smem(3) + vmem(10),
-        out_specs=tuple(vmem(7)),
+        in_specs=smem(3) + vmem(7),
+        out_specs=tuple(vmem(6)),
         scratch_shapes=[
+            pltpu.VMEM((3, ROWS, WIDE), jnp.bfloat16),
+            pltpu.VMEM((ENTRIES * ROWS, 2 * KV), jnp.float32),
             pltpu.VMEM((ENTRIES * ROWS, 2 * KV), jnp.bfloat16),
-            pltpu.VMEM((ENTRIES * ROWS, 2 * KV), jnp.float32),
-            pltpu.VMEM((3, ROWS, WIDE), jnp.bfloat16),
             pltpu.VMEM((3, ROWS, WIDE), jnp.bfloat16),
             pltpu.VMEM((3, ROWS, WIDE), jnp.bfloat16),
             pltpu.VMEM((SPAN, GROUP * ROWS), jnp.float32),
@@ -414,55 +437,40 @@
         in_hbm(slot_to_block),
         live,
         row_start,
-        q_own,
-        q_sib,
-        g_own,
-        g_sib,
-        kv,
-        kv_sib,
-        kv_a,
+        pack,
+        pack_sib,
+        kv_x,
         kv_b,
         kv_c,
+        kv_a,
     )
 
+    back_a = send(out_a, -2, 2)
     back_c = send(out_c, -3, 3)
-    back_a = send(out_a, -2, 2)
     back_b = send(out_b, -1, 1)
-    back_sib = send(sib, 1, -1)
-    dq_sib = send(dq_rest, 1, -1)
-
-    query_grad, own = pl.pallas_call(
-        early_kernel,
-        out_shape=(
-            bf16((2 * ROWS, WIDE)),
-            jax.ShapeDtypeStruct((2 * ROWS, 2 * KV), jnp.float32),
-        ),
-        in_specs=smem(3) + vmem(5),
-        out_specs=tuple(vmem(2)),
+    back_sib = send(out_sib, 1, -1)
+    lent = send(jnp.where(fold > 0, back_a[ROWS:], 0), None, -1)
+
+    query_grad, key_gradient, value_gradient = pl.pallas_call(
+        final_kernel,
+        out_shape=(bf16((2 * ROWS, WIDE)), bf16((2 * ROWS, KV)), bf16((2 * ROWS, KV))),
+        in_specs=smem(3) + vmem(7),
+        out_specs=tuple(vmem(3)),
+        scratch_shapes=[],
         compiler_params=params,
-        cost_estimate=pl.CostEstimate(
-            flops=1 << 36, bytes_accessed=1 << 22, transcendentals=0
-        ),
-        name="query_gradient_rows",
+        name="gradients_out",
     )(
         place,
         in_hbm(slot_to_block),
         live,
-        dq_first,
-        dq_rest,
-        dq_sib,
+        dq_own,
         own,
+        lent,
+        back_a,
         back_c,
+        back_b,
+        back_sib,
     )
-
-    key_gradient, value_gradient = pl.pallas_call(
-        sum_kernel,
-        out_shape=(bf16((2 * ROWS, KV)), bf16((2 * ROWS, KV))),
-        in_specs=vmem(4),
-        out_specs=tuple(vmem(2)),
-        compiler_params=params,
-        name="key_value_gradient_sum",
-    )(own, back_sib, back_a, back_b)
     return query_grad, key_gradient, value_gradient
 
 

time: 44.9 us -> 45.5 us (1.013)
  starting transfers between devices: 19.2 us -> 21.8 us
  waiting for transfers between devices: 16.3 us -> 14.9 us
  Pallas kernels: 8.56 us -> 7.84 us
    ppermute x11 -> x10, starting transfers between devices: 19.2 us -> 21.8 us  [send(): return lax.ppermute(array, 'ctx', pairs)]
    ppermute x11 -> x10, waiting for transfers between devices: 16.3 us -> 14.9 us  [send(): return lax.ppermute(array, 'ctx', pairs)]
    pallas_call x4 -> x3, Pallas kernels: 8.56 us -> 7.84 us  [the longest x1 4.75 us: shards(): pl.pallas_call(attention_kernel, out_shape=(bf16((2, ROWS, WIDE)), wide,...]
  transfers between devices with their start and end apart: 11 -> 10, of which waited for: 5 -> 4; matrix products, arithmetic and copies ran while one was open for 0% -> 0% of each run, Pallas kernels for 7% -> 0%
where the time goes in v6:
time: 45.5 us; the launch traced here: 45.3 us
  starting transfers between devices  21.8 us (48%)
  waiting for transfers between devices  14.9 us (33%)
  Pallas kernels  7.84 us (17%)
  between operations  0.71 us (2%)
    ppermute x10, starting transfers between devices, send(): return lax.ppermute(array, 'ctx', pairs)  21.8 us
    ppermute x10, waiting for transfers between devices, send(): return lax.ppermute(array, 'ctx', pairs)  14.9 us
    pallas_call x1, Pallas kernels, shards(): pl.pallas_call(attention_kernel, out_shape=(bf16((2, ROWS, WIDE)), wide,...  4.75 us
    pallas_call x1, Pallas kernels, shards(): pl.pallas_call(final_kernel, out_shape=(bf16((2 * ROWS, WIDE)), bf16((2 *...  1.63 us
    pallas_call x1, Pallas kernels, shards(): pl.pallas_call(pack_kernel, out_shape=(bf16((ROWS, 2 * KV)), bf16((ROWS,...  1.47 us
  transfers between devices with their start and end apart: 10, of which 4 were waited for; matrix products, arithmetic and copies ran while one was open for 0% of the time, Pallas kernels for 0%

profile of v6, /device:TPU:16, one launch (start us, length us, event | category | flops | bytes accessed | tf_op | source)
XLA Modules:
  0.0 45.3 jit_solution(18194888362421342776)
XLA Ops:
  0.6 0.0 copy-start
  0.6 1.5 %prepare.1 = (bf16[64,1024]{1,0:T(8,128)(2,1)S(1)}, bf16[64,1024]{1,0:T(8,128)(2,1)S(1)}, bf16[320,2048]{1,0:T(8,128)(2,1)S(1)}, s32[4,256]{1,0:T(4,128)S(1)}, f32[64,1024]{1,0:T(8,128)S(1)}) custom-call(s32[1]{0:T(128)} %bitcast.place, s32[256]{0:T(256)} %slots.3, s32[342]{0:T(512)} %docs_hbm.1, bf16[128,512]{1,0:T(8,128)(2,1)} %keys.1, ...), custom_call_target="tpu_custom_call" | custom-call | tf_op jit(solution)/shard_map/prepare/pallas_call | solution.py:378
  2.1 0.1 collective-permute-start
  2.2 9.3 %collective-permute-start.3 = (bf16[64,1024]{1,0:T(8,128)(2,1)S(1)}, bf16[64,1024]{1,0:T(8,128)(2,1)S(1)}, u32[]{:S(2)}, u32[]{:S(2)}) collective-permute-start(bf16[64,1024]{1,0:T(8,128)(2,1)S(1)} %get-tuple-element.17), channel_id=1, source_target_pairs={{0,125},{1,4},{2,127},{3,6},{4,1},{5,8},{6,3},{7,10},{8,5},{9,12},... | collective-permute-start | bytes 393224 | tf_op jit(solution)/shard_map/ppermute | solution.py:36
  11.5 0.0 collective-permute-start.2
  11.5 1.0 %collective-permute-start.4 = (bf16[64,1024]{1,0:T(8,128)(2,1)S(1)}, bf16[64,1024]{1,0:T(8,128)(2,1)S(1)}, u32[]{:S(2)}, u32[]{:S(2)}) collective-permute-start(bf16[64,1024]{1,0:T(8,128)(2,1)S(1)} %get-tuple-element.18), channel_id=1, source_target_pairs={{0,2},{1,127},{2,4},{3,1},{4,6},{5,3},{6,8},{7,5},{8,10},{9,7},{10... | collective-permute-start | bytes 393224 | tf_op jit(solution)/shard_map/ppermute | solution.py:36
  12.6 0.0 collective-permute-done.pack_sib
  12.6 0.1 slice_select_fusion.1
  12.7 0.7 %collective-permute-start.1 = (bf16[64,1024]{1,0:T(8,128)(2,1)S(1)}, bf16[64,1024]{1,0:T(8,128)(2,1)S(1)}, u32[]{:S(2)}, u32[]{:S(2)}) collective-permute-start(bf16[64,1024]{1,0:T(8,128)(2,1)S(1)} %get-tuple-element.25), channel_id=1, source_target_pairs={{1,127},{3,1},{5,3},{7,5},{9,7},{11,9},{13,11},{15,13},{17,15},{19... | collective-permute-start | bytes 393224 | tf_op jit(solution)/shard_map/ppermute | solution.py:36
  13.3 8.2 %collective-permute-done.4.kv_a = bf16[64,1024]{1,0:T(8,128)(2,1)S(1)} collective-permute-done((bf16[64,1024]{1,0:T(8,128)(2,1)S(1)}, bf16[64,1024]{1,0:T(8,128)(2,1)S(1)}, u32[]{:S(2)}, u32[]{:S(2)}) %collective-permute-start.4) | collective-permute-done | bytes 131104 | tf_op jit(solution)/shard_map/ppermute | solution.py:36
  21.6 0.0 collective-permute-done.3.kv_c
  21.6 0.0 collective-permute-done.2.kv_b
  21.6 0.0 collective-permute-done.1.kv_x
  21.6 0.0 copy-done
  21.6 4.7 %attention_items.1 = (bf16[2,64,2048]{2,1,0:T(8,128)(2,1)S(1)}, f32[128,1024]{1,0:T(8,128)S(1)}, bf16[192,2048]{1,0:T(8,128)(2,1)S(1)}, bf16[128,1024]{1,0:T(8,1...) custom-call(s32[1]{0:T(128)} %bitcast.place, s32[256]{0:T(256)} %slots.3, s32[4,256]{1,0:T(4,128)S(1)} %bitcast.2, ...), custom_call_target="tpu_custom_call" | custom-call | tf_op jit(solution)/shard_map/attention_items/pallas_call | solution.py:413
  26.3 1.9 %collective-permute-start.9 = (bf16[192,2048]{1,0:T(8,128)(2,1)S(1)}, bf16[192,2048]{1,0:T(8,128)(2,1)S(1)}, u32[]{:S(2)}, u32[]{:S(2)}) collective-permute-start(bf16[192,2048]{1,0:T(8,128)(2,1)S(1)} %get-tuple-element.24), channel_id=1, source_target_pairs={{0,1},{1,0},{2,3},{3,2},{4,5},{5,4},{6,7},{7,6},{8,9},{9,8},{10,11... | collective-permute-start | bytes 2359304 | tf_op jit(solution)/shard_map/ppermute | solution.py:36
  28.2 4.5 %collective-permute-start.5 = (bf16[128,1024]{1,0:T(8,128)(2,1)S(1)}, bf16[128,1024]{1,0:T(8,128)(2,1)S(1)}, u32[]{:S(2)}, u32[]{:S(2)}) collective-permute-start(bf16[128,1024]{1,0:T(8,128)(2,1)S(1)} %get-tuple-element.21), channel_id=1, source_target_pairs={{0,126},{1,3},{2,0},{3,5},{4,2},{5,7},{6,4},{7,9},{8,6},{9,11},{10... | collective-permute-start | bytes 786440 | tf_op jit(solution)/shard_map/ppermute | solution.py:36
  32.7 0.9 %collective-permute-start.7 = (bf16[64,1024]{1,0:T(8,128)(2,1)S(1)}, bf16[64,1024]{1,0:T(8,128)(2,1)S(1)}, u32[]{:S(2)}, u32[]{:S(2)}) collective-permute-start(bf16[64,1024]{1,0:T(8,128)(2,1)S(1)} %get-tuple-element.22), channel_id=1, source_target_pairs={{0,125},{1,4},{2,127},{3,6},{4,1},{5,8},{6,3},{7,10},{8,5},{9,12},... | collective-permute-start | bytes 393224 | tf_op jit(solution)/shard_map/ppermute | solution.py:36
  33.6 2.0 %collective-permute-start.8 = (bf16[64,1024]{1,0:T(8,128)(2,1)S(1)}, bf16[64,1024]{1,0:T(8,128)(2,1)S(1)}, u32[]{:S(2)}, u32[]{:S(2)}) collective-permute-start(bf16[64,1024]{1,0:T(8,128)(2,1)S(1)} %get-tuple-element.23), channel_id=1, source_target_pairs={{0,127},{1,2},{2,1},{3,4},{4,3},{5,6},{6,5},{7,8},{8,7},{9,10},{10... | collective-permute-start | bytes 393224 | tf_op jit(solution)/shard_map/ppermute | solution.py:36
  35.7 2.4 %collective-permute-done.5.back_a = bf16[128,1024]{1,0:T(8,128)(2,1)S(1)} collective-permute-done((bf16[128,1024]{1,0:T(8,128)(2,1)S(1)}, bf16[128,1024]{1,0:T(8,128)(2,1)S(1)}, u32[]{:S(2)}, u32[]{:S(2)}) %collective-permute-start.5) | collective-permute-done | bytes 262176 | tf_op jit(solution)/shard_map/ppermute | solution.py:36
  38.1 1.3 %collective-permute-start.6 = (bf16[64,1024]{1,0:T(8,128)(2,1)S(1)}, bf16[64,1024]{1,0:T(8,128)(2,1)S(1)}, u32[]{:S(2)}, u32[]{:S(2)}) collective-permute-start(bf16[64,1024]{1,0:T(8,128)(2,1)S(1)} %slice_select_fusion), channel_id=1, source_target_pairs={{1,0},{3,2},{5,4},{7,6},{9,8},{11,10},{13,12},{15,14},{17,16},{19,... | collective-permute-start | bytes 393224 | tf_op jit(solution)/shard_map/ppermute | solution.py:36
  39.4 3.0 %collective-permute-done.7.back_c = bf16[64,1024]{1,0:T(8,128)(2,1)S(1)} collective-permute-done((bf16[64,1024]{1,0:T(8,128)(2,1)S(1)}, bf16[64,1024]{1,0:T(8,128)(2,1)S(1)}, u32[]{:S(2)}, u32[]{:S(2)}) %collective-permute-start.7) | collective-permute-done | bytes 131104 | tf_op jit(solution)/shard_map/ppermute | solution.py:36
  42.4 1.3 %collective-permute-done.8.back_b = bf16[64,1024]{1,0:T(8,128)(2,1)S(1)} collective-permute-done((bf16[64,1024]{1,0:T(8,128)(2,1)S(1)}, bf16[64,1024]{1,0:T(8,128)(2,1)S(1)}, u32[]{:S(2)}, u32[]{:S(2)}) %collective-permute-start.8) | collective-permute-done | bytes 131104 | tf_op jit(solution)/shard_map/ppermute | solution.py:36
  43.6 0.0 collective-permute-done.6.lent
  43.6 0.0 collective-permute-done.9.theirs
  43.6 1.6 %gradients_out.1 = (bf16[128,2048]{1,0:T(8,128)(2,1)}, bf16[128,512]{1,0:T(8,128)(2,1)}, bf16[128,512]{1,0:T(8,128)(2,1)}) custom-call(s32[1]{0:T(128)} %bitcast.place, s32[256]{0:T(256)} %slots.3, s32[4,256]{1,0:T(4,128)S(1)} %bitcast.3, bf16[2,64,2048]{2,1,0:T(8,128)(2,1)S(1)} %get-tuple-element.19.mine, f32[128,1024]{1,0:T(8,128)S(1)} %get-tuple-element.20.own, ...), custom_call_target="tpu_custom_call" | custom-call | tf_op jit(solution)/shard_map/gradients_out/pallas_call | solution.py:454
  (1 shorter events, 0.0 us)
Async XLA Ops:
  0.6 20.9 %copy-start = (s32[256,4]{0,1:T(4,128)S(1)}, s32[256,4]{0,1:T(4,128)}, u32[]{:S(2)}) copy-start(s32[256,4]{0,1:T(4,128)} %param.13) | copy-start | bytes 12292
  2.1 10.5 %collective-permute-start = (bf16[320,2048]{1,0:T(8,128)(2,1)S(1)}, bf16[320,2048]{1,0:T(8,128)(2,1)S(1)}, u32[]{:S(2)}, u32[]{:S(2)}) collective-permute-start(bf16[320,2048]{1,0:T(8,128)(2,1)S(1)} %get-tuple-element.15.pack_own), channel_id=1, source_target_pairs={{0,1},{1,0},{2,3},{3,2},{4,5},{5,4},{6,7},{7,6},{8,9},{9,8},{10,11... | collective-permute-start | bytes 3932168 | tf_op jit(solution)/shard_map/ppermute | solution.py:36
  2.2 19.3 %collective-permute-start.3 = (bf16[64,1024]{1,0:T(8,128)(2,1)S(1)}, bf16[64,1024]{1,0:T(8,128)(2,1)S(1)}, u32[]{:S(2)}, u32[]{:S(2)}) collective-permute-start(bf16[64,1024]{1,0:T(8,128)(2,1)S(1)} %get-tuple-element.17), channel_id=1, source_target_pairs={{0,125},{1,4},{2,127},{3,6},{4,1},{5,8},{6,3},{7,10},{8,5},{9,12},... | collective-permute-start | bytes 393224 | tf_op jit(solution)/shard_map/ppermute | solution.py:36
  11.5 10.0 %collective-permute-start.2 = (bf16[64,1024]{1,0:T(8,128)(2,1)S(1)}, bf16[64,1024]{1,0:T(8,128)(2,1)S(1)}, u32[]{:S(2)}, u32[]{:S(2)}) collective-permute-start(bf16[64,1024]{1,0:T(8,128)(2,1)S(1)} %get-tuple-element.17), channel_id=1, source_target_pairs={{0,127},{1,2},{2,1},{3,4},{4,3},{5,6},{6,5},{7,8},{8,7},{9,10},{10... | collective-permute-start | bytes 393224 | tf_op jit(solution)/shard_map/ppermute | solution.py:36
  11.5 10.0 %collective-permute-start.4 = (bf16[64,1024]{1,0:T(8,128)(2,1)S(1)}, bf16[64,1024]{1,0:T(8,128)(2,1)S(1)}, u32[]{:S(2)}, u32[]{:S(2)}) collective-permute-start(bf16[64,1024]{1,0:T(8,128)(2,1)S(1)} %get-tuple-element.18), channel_id=1, source_target_pairs={{0,2},{1,127},{2,4},{3,1},{4,6},{5,3},{6,8},{7,5},{8,10},{9,7},{10... | collective-permute-start | bytes 393224 | tf_op jit(solution)/shard_map/ppermute | solution.py:36
  12.7 8.9 %collective-permute-start.1 = (bf16[64,1024]{1,0:T(8,128)(2,1)S(1)}, bf16[64,1024]{1,0:T(8,128)(2,1)S(1)}, u32[]{:S(2)}, u32[]{:S(2)}) collective-permute-start(bf16[64,1024]{1,0:T(8,128)(2,1)S(1)} %get-tuple-element.25), channel_id=1, source_target_pairs={{1,127},{3,1},{5,3},{7,5},{9,7},{11,9},{13,11},{15,13},{17,15},{19... | collective-permute-start | bytes 393224 | tf_op jit(solution)/shard_map/ppermute | solution.py:36
  26.3 17.3 %collective-permute-start.9 = (bf16[192,2048]{1,0:T(8,128)(2,1)S(1)}, bf16[192,2048]{1,0:T(8,128)(2,1)S(1)}, u32[]{:S(2)}, u32[]{:S(2)}) collective-permute-start(bf16[192,2048]{1,0:T(8,128)(2,1)S(1)} %get-tuple-element.24), channel_id=1, source_target_pairs={{0,1},{1,0},{2,3},{3,2},{4,5},{5,4},{6,7},{7,6},{8,9},{9,8},{10,11... | collective-permute-start | bytes 2359304 | tf_op jit(solution)/shard_map/ppermute | solution.py:36
  28.2 9.8 %collective-permute-start.5 = (bf16[128,1024]{1,0:T(8,128)(2,1)S(1)}, bf16[128,1024]{1,0:T(8,128)(2,1)S(1)}, u32[]{:S(2)}, u32[]{:S(2)}) collective-permute-start(bf16[128,1024]{1,0:T(8,128)(2,1)S(1)} %get-tuple-element.21), channel_id=1, source_target_pairs={{0,126},{1,3},{2,0},{3,5},{4,2},{5,7},{6,4},{7,9},{8,6},{9,11},{10... | collective-permute-start | bytes 786440 | tf_op jit(solution)/shard_map/ppermute | solution.py:36
  32.7 9.6 %collective-permute-start.7 = (bf16[64,1024]{1,0:T(8,128)(2,1)S(1)}, bf16[64,1024]{1,0:T(8,128)(2,1)S(1)}, u32[]{:S(2)}, u32[]{:S(2)}) collective-permute-start(bf16[64,1024]{1,0:T(8,128)(2,1)S(1)} %get-tuple-element.22), channel_id=1, source_target_pairs={{0,125},{1,4},{2,127},{3,6},{4,1},{5,8},{6,3},{7,10},{8,5},{9,12},... | collective-permute-start | bytes 393224 | tf_op jit(solution)/shard_map/ppermute | solution.py:36
  33.6 10.0 %collective-permute-start.8 = (bf16[64,1024]{1,0:T(8,128)(2,1)S(1)}, bf16[64,1024]{1,0:T(8,128)(2,1)S(1)}, u32[]{:S(2)}, u32[]{:S(2)}) collective-permute-start(bf16[64,1024]{1,0:T(8,128)(2,1)S(1)} %get-tuple-element.23), channel_id=1, source_target_pairs={{0,127},{1,2},{2,1},{3,4},{4,3},{5,6},{6,5},{7,8},{8,7},{9,10},{10... | collective-permute-start | bytes 393224 | tf_op jit(solution)/shard_map/ppermute | solution.py:36
  38.1 5.5 %collective-permute-start.6 = (bf16[64,1024]{1,0:T(8,128)(2,1)S(1)}, bf16[64,1024]{1,0:T(8,128)(2,1)S(1)}, u32[]{:S(2)}, u32[]{:S(2)}) collective-permute-start(bf16[64,1024]{1,0:T(8,128)(2,1)S(1)} %slice_select_fusion), channel_id=1, source_target_pairs={{1,0},{3,2},{5,4},{7,6},{9,8},{11,10},{13,12},{15,14},{17,16},{19,... | collective-permute-start | bytes 393224 | tf_op jit(solution)/shard_map/ppermute | solution.py:36

commit v7 on v6

--- a/solution.py
+++ b/solution.py
@@ -24,6 +24,7 @@
 ENTRIES = 8
 VMEM_LIMIT = 24 * 1024 * 1024
 
+NEAR_COST = 1 << 34
 TABLE_A, TABLE_B, TABLE_C, TABLE_X = 4, 5, 6, 7
 PACK_KV = 4 * ROWS
 PACK_ROWS = 5 * ROWS
@@ -301,9 +302,20 @@
         copy.wait()
 
 
-def final_kernel(
-    place, slots, live, mine, own, lent, back_a, back_c, back_b, theirs, *outs
-):
+def near_kernel(place, slots, own, back_a, out):
+    parity = lax.rem(place[0], 2)
+    is_odd = parity == 1
+    own_rows = pl.ds(pl.multiple_of(parity * ROWS, ROWS), ROWS)
+    out[...] = own[...]
+    out[own_rows, :] += back_a[:ROWS, :].astype(jnp.float32)
+    holder = slots[2 * (place[0] - parity) + 2] == slots.shape[0] // 2 - 1
+
+    @pl.when(jnp.logical_and(is_odd, holder))
+    def _():
+        out[:ROWS, :] += back_a[ROWS:, :].astype(jnp.float32)
+
+
+def final_kernel(place, slots, live, mine, own, lent, back_c, back_b, theirs, *outs):
     query_out, key_out, value_out = outs
     me = place[0]
     parity = lax.rem(me, 2)
@@ -330,18 +342,15 @@
     def _():
         query_out[other_rows, :] = theirs[:ROWS, :]
 
-    keeps = jnp.logical_and(is_odd, slots[chip_base + 2] == slots.shape[0] // 2 - 1)
-    kept = jnp.where(keeps, 1.0, 0.0)
     f32 = jnp.float32
     for out, first in ((key_out, 0), (value_out, KV)):
         columns = slice(first, first + KV)
-        chain = back_a[:ROWS, columns].astype(f32)
         cross = back_b[:, columns].astype(f32) + back_c[:, columns].astype(f32)
         low = own[:ROWS, columns] + theirs[2 * ROWS :, columns].astype(f32)
-        low = low + lent[:, columns].astype(f32) + kept * back_a[ROWS:, columns].astype(f32)
+        low = low + lent[:, columns].astype(f32) + jnp.where(is_odd, cross, 0.0)
         high = own[ROWS:, columns] + theirs[2 * ROWS :, 2 * KV + first : 3 * KV + first].astype(f32)
-        out[:ROWS, :] = (low + jnp.where(is_odd, cross, chain)).astype(out.dtype)
-        out[ROWS:, :] = (high + jnp.where(is_odd, chain, cross)).astype(out.dtype)
+        out[:ROWS, :] = low.astype(out.dtype)
+        out[ROWS:, :] = (high + jnp.where(is_odd, 0.0, cross)).astype(out.dtype)
 
 
 def vmem(count):
@@ -403,9 +412,9 @@
         in_hbm(output_gradient),
     )
     kv_a = send(kv_chain, 2, -2)
+    pack_sib, kv_cross = lax.optimization_barrier((send(pack, 1, -1), kv_cross))
     kv_b = send(kv_cross, -1, 1)
     kv_c = send(kv_cross, -3, 3)
-    pack_sib = send(pack, 1, -1)
     low_rows = (slice(PACK_KV, None), slice(0, 2 * KV))
     kv_x = send(jnp.where(fold > 0, pack_sib[low_rows], pack[low_rows]), None, -2)
 
@@ -451,10 +460,22 @@
     back_sib = send(out_sib, 1, -1)
     lent = send(jnp.where(fold > 0, back_a[ROWS:], 0), None, -1)
 
+    own = pl.pallas_call(
+        near_kernel,
+        out_shape=wide,
+        in_specs=smem(2) + vmem(2),
+        out_specs=vmem(1)[0],
+        compiler_params=params,
+        cost_estimate=pl.CostEstimate(
+            flops=NEAR_COST, bytes_accessed=1 << 20, transcendentals=0
+        ),
+        name="two_away_sum",
+    )(place, in_hbm(slot_to_block), own, back_a)
+
     query_grad, key_gradient, value_gradient = pl.pallas_call(
         final_kernel,
         out_shape=(bf16((2 * ROWS, WIDE)), bf16((2 * ROWS, KV)), bf16((2 * ROWS, KV))),
-        in_specs=smem(3) + vmem(7),
+        in_specs=smem(3) + vmem(6),
         out_specs=tuple(vmem(3)),
         scratch_shapes=[],
         compiler_params=params,
@@ -466,7 +487,6 @@
         dq_own,
         own,
         lent,
-        back_a,
         back_c,
         back_b,
         back_sib,

time: 45.5 us -> 45 us (0.989)
  waiting for transfers between devices: 14.9 us -> 12.8 us
  starting transfers between devices: 21.8 us -> 22.6 us
  Pallas kernels: 7.84 us -> 8.6 us
    ppermute x10, waiting for transfers between devices: 14.9 us -> 12.8 us  [send(): return lax.ppermute(array, 'ctx', pairs)]
    ppermute x10, starting transfers between devices: 21.8 us -> 22.6 us  [send(): return lax.ppermute(array, 'ctx', pairs)]
    pallas_call x0 -> x1, Pallas kernels: none -> 0.75 us  [shards(): pl.pallas_call(near_kernel, out_shape=wide, in_specs=smem(2) + vmem(2), o...]
  transfers between devices with their start and end apart: 10 -> 10, of which waited for: 4 -> 6; matrix products, arithmetic and copies ran while one was open for 0% -> 0% of each run, Pallas kernels for 0% -> 2%
where the time goes in v7:
time: 45 us; the launch traced here: 44.8 us
  starting transfers between devices  22.6 us (50%)
  waiting for transfers between devices  12.8 us (28%)
  Pallas kernels  8.6 us (19%)
  between operations  0.72 us (2%)
    ppermute x10, starting transfers between devices, send(): return lax.ppermute(array, 'ctx', pairs)  22.6 us
    ppermute x10, waiting for transfers between devices, send(): return lax.ppermute(array, 'ctx', pairs)  12.8 us
    pallas_call x1, Pallas kernels, shards(): pl.pallas_call(attention_kernel, out_shape=(bf16((2, ROWS, WIDE)), wide,...  4.74 us
    pallas_call x1, Pallas kernels, shards(): pl.pallas_call(final_kernel, out_shape=(bf16((2 * ROWS, WIDE)), bf16((2 *...  1.64 us
    pallas_call x1, Pallas kernels, shards(): pl.pallas_call(pack_kernel, out_shape=(bf16((ROWS, 2 * KV)), bf16((ROWS,...  1.47 us
  transfers between devices with their start and end apart: 10, of which 6 were waited for; matrix products, arithmetic and copies ran while one was open for 0% of the time, Pallas kernels for 2%

profile of v7, /device:TPU:16, one launch (start us, length us, event | category | flops | bytes accessed | tf_op | source)
XLA Modules:
  0.0 44.8 jit_solution(8261876153415145498)
XLA Ops:
  0.6 0.0 copy-start
  0.6 1.5 %prepare.1 = (bf16[64,1024]{1,0:T(8,128)(2,1)S(1)}, bf16[64,1024]{1,0:T(8,128)(2,1)S(1)}, bf16[320,2048]{1,0:T(8,128)(2,1)S(1)}, s32[4,256]{1,0:T(4,128)S(1)}, f32[64,1024]{1,0:T(8,128)S(1)}) custom-call(s32[1]{0:T(128)} %bitcast.place, s32[256]{0:T(256)} %slots.5, s32[342]{0:T(512)} %docs_hbm.1, bf16[128,512]{1,0:T(8,128)(2,1)} %keys.1, ...), custom_call_target="tpu_custom_call" | custom-call | tf_op jit(solution)/shard_map/prepare/pallas_call | solution.py:387
  2.1 0.1 collective-permute-start
  2.2 2.0 %collective-permute-start.4 = (bf16[64,1024]{1,0:T(8,128)(2,1)S(1)}, bf16[64,1024]{1,0:T(8,128)(2,1)S(1)}, u32[]{:S(2)}, u32[]{:S(2)}) collective-permute-start(bf16[64,1024]{1,0:T(8,128)(2,1)S(1)} %get-tuple-element.22), channel_id=1, source_target_pairs={{0,2},{1,127},{2,4},{3,1},{4,6},{5,3},{6,8},{7,5},{8,10},{9,7},{10... | collective-permute-start | bytes 393224 | tf_op jit(solution)/shard_map/ppermute | solution.py:37
  4.2 1.0 %collective-permute-done.pack_sib = bf16[320,2048]{1,0:T(8,128)(2,1)S(1)} collective-permute-done((bf16[320,2048]{1,0:T(8,128)(2,1)S(1)}, bf16[320,2048]{1,0:T(8,128)(2,1)S(1)}, u32[]{:S(2)}, u32[]{:S(2)}) %collective-permute-start) | collective-permute-done | bytes 1310752 | tf_op jit(solution)/shard_map/ppermute | solution.py:37
  5.2 0.1 slice_select_fusion.1
  5.3 0.7 %collective-permute-start.1 = (bf16[64,1024]{1,0:T(8,128)(2,1)S(1)}, bf16[64,1024]{1,0:T(8,128)(2,1)S(1)}, u32[]{:S(2)}, u32[]{:S(2)}) collective-permute-start(bf16[64,1024]{1,0:T(8,128)(2,1)S(1)} %get-tuple-element.29), channel_id=1, source_target_pairs={{1,127},{3,1},{5,3},{7,5},{9,7},{11,9},{13,11},{15,13},{17,15},{19... | collective-permute-start | bytes 393224 | tf_op jit(solution)/shard_map/ppermute | solution.py:37
  6.0 11.0 %collective-permute-start.3 = (bf16[64,1024]{1,0:T(8,128)(2,1)S(1)}, bf16[64,1024]{1,0:T(8,128)(2,1)S(1)}, u32[]{:S(2)}, u32[]{:S(2)}) collective-permute-start(bf16[64,1024]{1,0:T(8,128)(2,1)S(1)} %get-tuple-element.21), channel_id=1, source_target_pairs={{0,125},{1,4},{2,127},{3,6},{4,1},{5,8},{6,3},{7,10},{8,5},{9,12},... | collective-permute-start | bytes 393224 | tf_op jit(solution)/shard_map/ppermute | solution.py:37
  17.0 0.0 collective-permute-start.2
  17.0 0.0 collective-permute-done.4.kv_a
  17.0 0.0 collective-permute-done.1.kv_x
  17.0 3.2 %collective-permute-done.3.kv_c = bf16[64,1024]{1,0:T(8,128)(2,1)S(1)} collective-permute-done((bf16[64,1024]{1,0:T(8,128)(2,1)S(1)}, bf16[64,1024]{1,0:T(8,128)(2,1)S(1)}, u32[]{:S(2)}, u32[]{:S(2)}) %collective-permute-start.3) | collective-permute-done | bytes 131104 | tf_op jit(solution)/shard_map/ppermute | solution.py:37
  20.2 5.4 %collective-permute-done.2.kv_b = bf16[64,1024]{1,0:T(8,128)(2,1)S(1)} collective-permute-done((bf16[64,1024]{1,0:T(8,128)(2,1)S(1)}, bf16[64,1024]{1,0:T(8,128)(2,1)S(1)}, u32[]{:S(2)}, u32[]{:S(2)}) %collective-permute-start.2) | collective-permute-done | bytes 131104 | tf_op jit(solution)/shard_map/ppermute | solution.py:37
  25.6 0.0 copy-done
  25.6 4.7 %attention_items.1 = (bf16[2,64,2048]{2,1,0:T(8,128)(2,1)S(1)}, f32[128,1024]{1,0:T(8,128)S(1)}, bf16[192,2048]{1,0:T(8,128)(2,1)S(1)}, bf16[128,1024]{1,0:T(8,1...) custom-call(s32[1]{0:T(128)} %bitcast.place, s32[256]{0:T(256)} %slots.5, s32[4,256]{1,0:T(4,128)S(1)} %bitcast.2, ...), custom_call_target="tpu_custom_call" | custom-call | tf_op jit(solution)/shard_map/attention_items/pallas_call | solution.py:422
  30.4 0.1 collective-permute-start.5
  30.5 4.0 %collective-permute-start.7 = (bf16[64,1024]{1,0:T(8,128)(2,1)S(1)}, bf16[64,1024]{1,0:T(8,128)(2,1)S(1)}, u32[]{:S(2)}, u32[]{:S(2)}) collective-permute-start(bf16[64,1024]{1,0:T(8,128)(2,1)S(1)} %get-tuple-element.26), channel_id=1, source_target_pairs={{0,125},{1,4},{2,127},{3,6},{4,1},{5,8},{6,3},{7,10},{8,5},{9,12},... | collective-permute-start | bytes 393224 | tf_op jit(solution)/shard_map/ppermute | solution.py:37
  34.4 3.4 %collective-permute-start.8 = (bf16[64,1024]{1,0:T(8,128)(2,1)S(1)}, bf16[64,1024]{1,0:T(8,128)(2,1)S(1)}, u32[]{:S(2)}, u32[]{:S(2)}) collective-permute-start(bf16[64,1024]{1,0:T(8,128)(2,1)S(1)} %get-tuple-element.27), channel_id=1, source_target_pairs={{0,127},{1,2},{2,1},{3,4},{4,3},{5,6},{6,5},{7,8},{8,7},{9,10},{10... | collective-permute-start | bytes 393224 | tf_op jit(solution)/shard_map/ppermute | solution.py:37
  37.9 0.0 collective-permute-start.9
  37.9 0.3 collective-permute-done.5.back_a
  38.2 1.3 %collective-permute-start.6 = (bf16[64,1024]{1,0:T(8,128)(2,1)S(1)}, bf16[64,1024]{1,0:T(8,128)(2,1)S(1)}, u32[]{:S(2)}, u32[]{:S(2)}) collective-permute-start(bf16[64,1024]{1,0:T(8,128)(2,1)S(1)} %slice_select_fusion), channel_id=1, source_target_pairs={{1,0},{3,2},{5,4},{7,6},{9,8},{11,10},{13,12},{15,14},{17,16},{19,... | collective-permute-start | bytes 393224 | tf_op jit(solution)/shard_map/ppermute | solution.py:37
  39.5 0.8 %two_away_sum.1.own = f32[128,1024]{1,0:T(8,128)S(1)} custom-call(s32[1]{0:T(128)} %bitcast.place, s32[256]{0:T(256)} %slots.5, f32[128,1024]{1,0:T(8,128)S(1)} %get-tuple-element.24.own, bf16[128,1024]{1,0:T(8,128)(2,1)S(1)} %collective-permute-done.5.back_a), custom_call_target="tpu_custom_call" | custom-call | flops 17179869184 | bytes 1048576 | tf_op jit(solution)/shard_map/two_away_sum/pallas_call | solution.py:463
  40.2 1.3 %collective-permute-done.7.back_c = bf16[64,1024]{1,0:T(8,128)(2,1)S(1)} collective-permute-done((bf16[64,1024]{1,0:T(8,128)(2,1)S(1)}, bf16[64,1024]{1,0:T(8,128)(2,1)S(1)}, u32[]{:S(2)}, u32[]{:S(2)}) %collective-permute-start.7) | collective-permute-done | bytes 131104 | tf_op jit(solution)/shard_map/ppermute | solution.py:37
  41.6 1.6 %collective-permute-done.8.back_b = bf16[64,1024]{1,0:T(8,128)(2,1)S(1)} collective-permute-done((bf16[64,1024]{1,0:T(8,128)(2,1)S(1)}, bf16[64,1024]{1,0:T(8,128)(2,1)S(1)}, u32[]{:S(2)}, u32[]{:S(2)}) %collective-permute-start.8) | collective-permute-done | bytes 131104 | tf_op jit(solution)/shard_map/ppermute | solution.py:37
  43.2 0.0 collective-permute-done.6.lent
  43.2 0.0 collective-permute-done.9.theirs
  43.2 1.6 %gradients_out.1 = (bf16[128,2048]{1,0:T(8,128)(2,1)}, bf16[128,512]{1,0:T(8,128)(2,1)}, bf16[128,512]{1,0:T(8,128)(2,1)}) custom-call(s32[1]{0:T(128)} %bitcast.place, s32[256]{0:T(256)} %slots.5, s32[4,256]{1,0:T(4,128)S(1)} %bitcast.3, bf16[2,64,2048]{2,1,0:T(8,128)(2,1)S(1)} %get-tuple-element.23.mine, f32[128,1024]{1,0:T(8,128)S(1)} %two_away_sum.1.own, ...), custom_call_target="tpu_custom_call" | custom-call | tf_op jit(solution)/shard_map/gradients_out/pallas_call | solution.py:475
  (1 shorter events, 0.0 us)
Async XLA Ops:
  0.6 25.0 %copy-start = (s32[256,4]{0,1:T(4,128)S(1)}, s32[256,4]{0,1:T(4,128)}, u32[]{:S(2)}) copy-start(s32[256,4]{0,1:T(4,128)} %param.13) | copy-start | bytes 12292
  2.1 3.1 %collective-permute-start = (bf16[320,2048]{1,0:T(8,128)(2,1)S(1)}, bf16[320,2048]{1,0:T(8,128)(2,1)S(1)}, u32[]{:S(2)}, u32[]{:S(2)}) collective-permute-start(bf16[320,2048]{1,0:T(8,128)(2,1)S(1)} %get-tuple-element.17.pack_own), channel_id=1, source_target_pairs={{0,1},{1,0},{2,3},{3,2},{4,5},{5,4},{6,7},{7,6},{8,9},{9,8},{10,11... | collective-permute-start | bytes 3932168 | tf_op jit(solution)/shard_map/ppermute | solution.py:37
  2.2 14.8 %collective-permute-start.4 = (bf16[64,1024]{1,0:T(8,128)(2,1)S(1)}, bf16[64,1024]{1,0:T(8,128)(2,1)S(1)}, u32[]{:S(2)}, u32[]{:S(2)}) collective-permute-start(bf16[64,1024]{1,0:T(8,128)(2,1)S(1)} %get-tuple-element.22), channel_id=1, source_target_pairs={{0,2},{1,127},{2,4},{3,1},{4,6},{5,3},{6,8},{7,5},{8,10},{9,7},{10... | collective-permute-start | bytes 393224 | tf_op jit(solution)/shard_map/ppermute | solution.py:37
  5.3 11.7 %collective-permute-start.1 = (bf16[64,1024]{1,0:T(8,128)(2,1)S(1)}, bf16[64,1024]{1,0:T(8,128)(2,1)S(1)}, u32[]{:S(2)}, u32[]{:S(2)}) collective-permute-start(bf16[64,1024]{1,0:T(8,128)(2,1)S(1)} %get-tuple-element.29), channel_id=1, source_target_pairs={{1,127},{3,1},{5,3},{7,5},{9,7},{11,9},{13,11},{15,13},{17,15},{19... | collective-permute-start | bytes 393224 | tf_op jit(solution)/shard_map/ppermute | solution.py:37
  6.0 14.3 %collective-permute-start.3 = (bf16[64,1024]{1,0:T(8,128)(2,1)S(1)}, bf16[64,1024]{1,0:T(8,128)(2,1)S(1)}, u32[]{:S(2)}, u32[]{:S(2)}) collective-permute-start(bf16[64,1024]{1,0:T(8,128)(2,1)S(1)} %get-tuple-element.21), channel_id=1, source_target_pairs={{0,125},{1,4},{2,127},{3,6},{4,1},{5,8},{6,3},{7,10},{8,5},{9,12},... | collective-permute-start | bytes 393224 | tf_op jit(solution)/shard_map/ppermute | solution.py:37
  17.0 8.6 %collective-permute-start.2 = (bf16[64,1024]{1,0:T(8,128)(2,1)S(1)}, bf16[64,1024]{1,0:T(8,128)(2,1)S(1)}, u32[]{:S(2)}, u32[]{:S(2)}) collective-permute-start(bf16[64,1024]{1,0:T(8,128)(2,1)S(1)} %get-tuple-element.21), channel_id=1, source_target_pairs={{0,127},{1,2},{2,1},{3,4},{4,3},{5,6},{6,5},{7,8},{8,7},{9,10},{10... | collective-permute-start | bytes 393224 | tf_op jit(solution)/shard_map/ppermute | solution.py:37
  30.4 7.8 %collective-permute-start.5 = (bf16[128,1024]{1,0:T(8,128)(2,1)S(1)}, bf16[128,1024]{1,0:T(8,128)(2,1)S(1)}, u32[]{:S(2)}, u32[]{:S(2)}) collective-permute-start(bf16[128,1024]{1,0:T(8,128)(2,1)S(1)} %get-tuple-element.25), channel_id=1, source_target_pairs={{0,126},{1,3},{2,0},{3,5},{4,2},{5,7},{6,4},{7,9},{8,6},{9,11},{10... | collective-permute-start | bytes 786440 | tf_op jit(solution)/shard_map/ppermute | solution.py:37
  30.5 11.1 %collective-permute-start.7 = (bf16[64,1024]{1,0:T(8,128)(2,1)S(1)}, bf16[64,1024]{1,0:T(8,128)(2,1)S(1)}, u32[]{:S(2)}, u32[]{:S(2)}) collective-permute-start(bf16[64,1024]{1,0:T(8,128)(2,1)S(1)} %get-tuple-element.26), channel_id=1, source_target_pairs={{0,125},{1,4},{2,127},{3,6},{4,1},{5,8},{6,3},{7,10},{8,5},{9,12},... | collective-permute-start | bytes 393224 | tf_op jit(solution)/shard_map/ppermute | solution.py:37
  34.4 8.7 %collective-permute-start.8 = (bf16[64,1024]{1,0:T(8,128)(2,1)S(1)}, bf16[64,1024]{1,0:T(8,128)(2,1)S(1)}, u32[]{:S(2)}, u32[]{:S(2)}) collective-permute-start(bf16[64,1024]{1,0:T(8,128)(2,1)S(1)} %get-tuple-element.27), channel_id=1, source_target_pairs={{0,127},{1,2},{2,1},{3,4},{4,3},{5,6},{6,5},{7,8},{8,7},{9,10},{10... | collective-permute-start | bytes 393224 | tf_op jit(solution)/shard_map/ppermute | solution.py:37
  37.9 5.3 %collective-permute-start.9 = (bf16[192,2048]{1,0:T(8,128)(2,1)S(1)}, bf16[192,2048]{1,0:T(8,128)(2,1)S(1)}, u32[]{:S(2)}, u32[]{:S(2)}) collective-permute-start(bf16[192,2048]{1,0:T(8,128)(2,1)S(1)} %get-tuple-element.28), channel_id=1, source_target_pairs={{0,1},{1,0},{2,3},{3,2},{4,5},{5,4},{6,7},{7,6},{8,9},{9,8},{10,11... | collective-permute-start | bytes 2359304 | tf_op jit(solution)/shard_map/ppermute | solution.py:37
  38.2 5.0 %collective-permute-start.6 = (bf16[64,1024]{1,0:T(8,128)(2,1)S(1)}, bf16[64,1024]{1,0:T(8,128)(2,1)S(1)}, u32[]{:S(2)}, u32[]{:S(2)}) collective-permute-start(bf16[64,1024]{1,0:T(8,128)(2,1)S(1)} %slice_select_fusion), channel_id=1, source_target_pairs={{1,0},{3,2},{5,4},{7,6},{9,8},{11,10},{13,12},{15,14},{17,16},{19,... | collective-permute-start | bytes 393224 | tf_op jit(solution)/shard_map/ppermute | solution.py:37
